TPU v7x, 32 devices: a whole 2x2x4 slice. The times are simulated.
32 devices in a mesh: groups: 2 (over y), fsdp: 4 (over x, core), tensor: 4 (over z).
Axes of the slice: x: 2, y: 2, z: 4, core: 2. Of those that a mesh axis runs over, the one named last changes fastest.
Arguments:
- tokens: bfloat16 [1024, 8192], P(('groups', 'fsdp'), 'tensor'), parts along dimension 0, may hold values from -6 to 6
- hidden_cotangent: bfloat16 [1024, 14336], P(('groups', 'fsdp'), 'tensor'), parts along dimension 0, may hold values from -6 to 6
- gate_weight: bfloat16 [4096, 14336], P('fsdp', 'tensor'), may hold values from -0.09375 to 0.09375
- up_weight: bfloat16 [4096, 14336], P('fsdp', 'tensor'), may hold values from -0.09375 to 0.09375
- gate_kept: int32 [32, 112], P(None, 'tensor'), may hold values from 0 to 63, as said below
- up_kept: int32 [32, 112], P(None, 'tensor'), may hold values from 0 to 63, as said below
- example_number: int32 [1024], P(('groups', 'fsdp')), parts along dimension 0, may hold values from 0 to 3, as said below
- clip_norm: float32 [1], replicated, may hold values from 1 to 2
Outputs:
- hidden: bfloat16 [1024, 14336], P(('groups', 'fsdp'), 'tensor'), parts along dimension 0
- gate_grad: bfloat16 [8192, 14336], P(('groups', 'fsdp'), 'tensor'), parts along dimension 0
- up_grad: bfloat16 [8192, 14336], P(('groups', 'fsdp'), 'tensor'), parts along dimension 0
- token_grad: bfloat16 [1024, 8192], P(('groups', 'fsdp'), 'tensor'), parts along dimension 0
There are 2 independent parts, one for each index of `groups`. A program takes and returns all parts, laid end to end along the dimension named above; an argument that names none is the same for every part. Nothing has to cross between parts.
Inputs may be any that keep to these rules, and one draw needn't show every extreme that they name: `gate_kept`: each column lists 32 different row blocks. `up_kept`: each column lists 32 different row blocks. `example_number`: on each group of 128 consecutive tokens the numbers never fall and take every value from 0 to 3.
All inputs are finite; a program needn't handle non-finite values.
Results may differ from a plain program's by a relative error of at most 0.0095.
Values may be sent and summed in bfloat16 or wider, within the bound.
No kernel may reach another device: no remote copies, remote signals or barrier semaphores. Data moves between devices by JAX's collectives and lax.ppermute only.
A program may use at most 384 MiB of HBM per device.

v0:
```python
import math

import jax
import jax.numpy as jnp
from jax import lax
from jax.sharding import PartitionSpec as P

D = 8192
FFW = 14336
BLK = 128
EX_DEV = 4


def mask_matrix(kept, row_blocks):
    levels = jnp.arange(row_blocks, dtype=jnp.int32)
    return jnp.sum((kept[:, None, :] == levels[None, :, None]).astype(jnp.float32), axis=0)


def one_hot_rows(kept_column, row_blocks, dtype):
    levels = jnp.arange(row_blocks, dtype=jnp.int32)
    return (kept_column[:, None] == levels[None, :]).astype(dtype)


def pick_features(feature_blocks, kept_column):
    selector = one_hot_rows(kept_column, feature_blocks.shape[0], jnp.bfloat16)
    picked = jnp.einsum("ki,ibt->kbt", selector, feature_blocks, preferred_element_type=jnp.float32)
    return picked.astype(jnp.bfloat16).reshape(kept_column.shape[0] * BLK, feature_blocks.shape[2])


def pair_term(kept, token_pairs, cotangent):
    kept_mask = mask_matrix(kept, token_pairs.shape[0])
    reached = jnp.einsum("ij,its->jts", kept_mask, token_pairs, precision=lax.Precision.HIGHEST)
    shaped = cotangent.reshape(cotangent.shape[0], kept.shape[1], BLK)
    own_pairs = jnp.einsum("tjc,sjc->jts", shaped, shaped, preferred_element_type=jnp.float32)
    return jnp.sum(reached * own_pairs, axis=0)


def example_norms(partial_value):
    return lax.psum(partial_value, "tensor")


def shards(
    tokens, hidden_cotangent, gate_weight, up_weight, gate_kept, up_kept, example_number, clip_norm
):
    gathered = lax.all_gather(tokens, "tensor", axis=1, tiled=True)
    token_rows = gathered.shape[0]
    blocks = gate_kept.shape[1]
    local_width = blocks * BLK
    row_blocks = gathered.shape[1] // BLK
    feature_blocks = gathered.T.reshape(row_blocks, BLK, token_rows)
    gate_full, up_full = (
        lax.all_gather(gate_weight, "fsdp", axis=0, tiled=True),
        lax.all_gather(up_weight, "fsdp", axis=0, tiled=True),
    )

    def forward_per_block(block_index):
        gate_feat = pick_features(
            feature_blocks, lax.dynamic_index_in_dim(gate_kept, block_index, 1, False)
        )
        up_feat = pick_features(
            feature_blocks, lax.dynamic_index_in_dim(up_kept, block_index, 1, False)
        )
        gate_slab = lax.dynamic_slice_in_dim(gate_full, block_index * BLK, BLK, 1)
        up_slab = lax.dynamic_slice_in_dim(up_full, block_index * BLK, BLK, 1)
        gate_part = jnp.einsum(
            "nt,nc->tc", gate_feat, gate_slab, preferred_element_type=jnp.float32
        )
        up_part = jnp.einsum("nt,nc->tc", up_feat, up_slab, preferred_element_type=jnp.float32)
        return (gate_part, up_part)

    gate_acc, up_acc = lax.map(forward_per_block, jnp.arange(blocks))
    gate_sum = gate_acc.transpose(1, 0, 2).reshape(token_rows, local_width)
    up_sum = up_acc.transpose(1, 0, 2).reshape(token_rows, local_width)
    sigmoid_gate = jax.nn.sigmoid(gate_sum)
    silu_gate = gate_sum * sigmoid_gate
    hidden = (silu_gate * up_sum).astype(jnp.bfloat16)
    incoming = hidden_cotangent.astype(jnp.float32)
    gate_cot = (incoming * up_sum * sigmoid_gate * (1.0 + gate_sum * (1.0 - sigmoid_gate))).astype(
        jnp.bfloat16
    )
    up_cot = (incoming * silu_gate).astype(jnp.bfloat16)
    token_blocks = gathered.reshape(token_rows, row_blocks, BLK)
    token_pairs = jnp.einsum(
        "tib,sib->its", token_blocks, token_blocks, preferred_element_type=jnp.float32
    )
    pair_sum = pair_term(gate_kept, token_pairs, gate_cot) + pair_term(up_kept, token_pairs, up_cot)
    member = (example_number[:, None] == jnp.arange(EX_DEV, dtype=jnp.int32)[None, :]).astype(
        jnp.float32
    )
    same_example = (example_number[:, None] == example_number[None, :]).astype(jnp.float32)
    partial_value = jnp.dot(
        member.T, jnp.sum(pair_sum * same_example, axis=1), precision=lax.Precision.HIGHEST
    )
    squares = example_norms(partial_value)

    def step_block(accumulated, block_index):
        gate_slab = lax.dynamic_slice_in_dim(gate_full, block_index * BLK, BLK, 1)
        up_slab = lax.dynamic_slice_in_dim(up_full, block_index * BLK, BLK, 1)
        gate_cot_slab = lax.dynamic_slice_in_dim(gate_cot, block_index * BLK, BLK, 1)
        up_cot_slab = lax.dynamic_slice_in_dim(up_cot, block_index * BLK, BLK, 1)
        gate_back = jnp.einsum(
            "tc,gc->gt", gate_cot_slab, gate_slab, preferred_element_type=jnp.float32
        )
        up_back = jnp.einsum("tc,gc->gt", up_cot_slab, up_slab, preferred_element_type=jnp.float32)
        gate_place = one_hot_rows(
            lax.dynamic_index_in_dim(gate_kept, block_index, 1, False), row_blocks, jnp.float32
        )
        up_place = one_hot_rows(
            lax.dynamic_index_in_dim(up_kept, block_index, 1, False), row_blocks, jnp.float32
        )
        accumulated = accumulated + jnp.einsum(
            "ki,kbt->ibt",
            gate_place,
            gate_back.reshape(gate_kept.shape[0], BLK, token_rows),
            precision=lax.Precision.HIGHEST,
        )
        accumulated = accumulated + jnp.einsum(
            "ki,kbt->ibt",
            up_place,
            up_back.reshape(up_kept.shape[0], BLK, token_rows),
            precision=lax.Precision.HIGHEST,
        )
        return (accumulated, None)

    start_blocks = jnp.zeros((row_blocks, BLK, token_rows), jnp.float32)
    accumulated, unused = lax.scan(step_block, start_blocks, jnp.arange(blocks))
    accumulated = accumulated.reshape(row_blocks * BLK, token_rows)
    shares = lax.psum_scatter(
        accumulated.astype(jnp.bfloat16), "tensor", scatter_dimension=0, tiled=True
    ).astype(jnp.float32)
    token_grad = shares.T.astype(jnp.bfloat16)
    threshold = clip_norm[0] * math.sqrt(D * FFW)
    factor = threshold / jnp.maximum(jnp.sqrt(squares), threshold)
    token_factor = jnp.dot(member, factor, precision=lax.Precision.HIGHEST)
    gate_scaled = (token_factor[:, None] * gate_cot.astype(jnp.float32)).astype(jnp.bfloat16)
    up_scaled = (token_factor[:, None] * up_cot.astype(jnp.float32)).astype(jnp.bfloat16)
    gate_shaped = gate_scaled.reshape(token_rows, blocks, BLK)
    up_shaped = up_scaled.reshape(token_rows, blocks, BLK)

    def block_term(block_index):
        gate_feat = pick_features(
            feature_blocks, lax.dynamic_index_in_dim(gate_kept, block_index, 1, False)
        )
        up_feat = pick_features(
            feature_blocks, lax.dynamic_index_in_dim(up_kept, block_index, 1, False)
        )
        gate_term = jnp.dot(
            gate_feat,
            lax.dynamic_index_in_dim(gate_shaped, block_index, 1, False),
            preferred_element_type=jnp.float32,
        )
        up_term = jnp.dot(
            up_feat,
            lax.dynamic_index_in_dim(up_shaped, block_index, 1, False),
            preferred_element_type=jnp.float32,
        )
        return jnp.concatenate((gate_term, up_term), axis=1)

    row_count = gate_weight.shape[0] * lax.axis_size("fsdp")

    def grad_per_block(block_index):
        return block_term(block_index)

    terms = lax.map(grad_per_block, jnp.arange(blocks))
    summed = lax.psum_scatter(
        jnp.concatenate(
            (
                terms[:, :, :BLK].transpose(1, 0, 2).reshape(row_count, local_width),
                terms[:, :, BLK:].transpose(1, 0, 2).reshape(row_count, local_width),
            ),
            axis=1,
        ).astype(jnp.bfloat16),
        "fsdp",
        scatter_dimension=0,
        tiled=True,
    ).astype(jnp.float32)
    gate_grad = summed[:, :local_width].astype(jnp.bfloat16)
    up_grad = summed[:, local_width:].astype(jnp.bfloat16)
    return (hidden, gate_grad, up_grad, token_grad)


def solution(mesh):
    placed = (
        P(("groups", "fsdp"), "tensor"),
        P(("groups", "fsdp"), "tensor"),
        P("fsdp", "tensor"),
        P("fsdp", "tensor"),
        P(None, "tensor"),
        P(None, "tensor"),
        P(("groups", "fsdp")),
        P(),
    )
    return jax.shard_map(
        shards,
        mesh=mesh,
        in_specs=placed,
        out_specs=(
            P(("groups", "fsdp"), "tensor"),
            P(("groups", "fsdp"), "tensor"),
            P(("groups", "fsdp"), "tensor"),
            P(("groups", "fsdp"), "tensor"),
        ),
        check_vma=False,
    )
```

profile of v0, /device:TPU:0, one launch (start us, length us, event | category | flops | bytes accessed | tf_op | source)
XLA Modules:
  0.0 1576.3 jit_solution(7775061204502212676)
XLA Ops:
  13.4 45.4 %all-gather.4.cloned.1.call-done = bf16[128,8192]{0,1:T(8,128)(2,1)} async-done(((bf16[128,2048]{0,1:T(8,128)(2,1)}), bf16[128,8192]{0,1:T(8,128)(2,1)}) %all-gather.4.cloned.1.call-update) | async-done | bytes 2097168 | tf_op jit(solution)/shard_map/all_gather | solution.py:45
  62.8 6.1 fusion.51
  68.9 5.8 fusion.53
  74.7 162.4 %all-gather.6.cloned.1.call-done = bf16[4096,3584]{1,0:T(8,128)(2,1)} async-done(((bf16[1024,3584]{1,0:T(8,128)(2,1)}), bf16[4096,3584]{1,0:T(8,128)(2,1)}) %all-gather.6.cloned.1.call-update) | async-done | bytes 29360144 | tf_op jit(solution)/shard_map/all_gather | solution.py:52
  237.1 179.6 %all-gather.8.cloned.1.call-done = bf16[4096,3584]{1,0:T(8,128)(2,1)} async-done(((bf16[1024,3584]{1,0:T(8,128)(2,1)}), bf16[4096,3584]{1,0:T(8,128)(2,1)}) %all-gather.8.cloned.1.call-update) | async-done | bytes 29360144 | tf_op jit(solution)/shard_map/all_gather | solution.py:53
  416.8 271.5 %while.33 = (s32[]{:T(128)}, f32[28,128,128]{1,2,0:T(8,128)}, f32[28,128,128]{1,2,0:T(8,128)}, s32[28]{0:T(128)S(1)}, s32[32,28]{0,1:T(8,128)S(1)}, /*index=5*/b...) while((s32[]{:T(128)}, f32[28,128,128]{1,2,0:T(8,128)}, ...), condition=%wide.region_1.2_spmd, body=%wide.region_0.1_spmd.sunk | while | flops 403705856 | bytes 14812157 | solution.py:71
  688.3 4.5 fusion.57
  696.3 11.7 psum.7
  711.0 233.2 %while.34 = (s32[]{:T(128)}, bf16[28,4096,256]{1,2,0:T(8,128)(2,1)}, s32[28]{0:T(128)S(1)}, s32[32,28]{0,1:T(8,128)S(1)}, bf16[64,128,128]{2,0,1:T(8,128)(2,1)S(...) while((s32[]{:T(128)}, ...), condition=%wide.region_9.10_spmd, body=%wide.region_8.9_spmd.sunk | while | flops 407900160 | bytes 18940852 | solution.py:164
  944.2 39.0 %fusion.76 = (bf16[28,4096,128]{1,2,0:T(8,128)(2,1)}, bf16[28,4096,128]{1,2,0:T(8,128)(2,1)}) fusion(bf16[28,4096,256]{1,2,0:T(8,128)(2,1)} %get-tuple-element.143), kind=kLoop, calls=%fused_computation.111 | loop fusion | bytes 117440512 | tf_op jit(solution)/shard_map/slice | solution.py:168
  983.2 40.3 %pad_maximum_fusion = bf16[4096,7168]{0,1:T(8,128)(2,1)} fusion(bf16[4096,3584]{0,1:T(8,128)(2,1)} %bitcast.209, bf16[4096,3584]{0,1:T(8,128)(2,1)} %bitcast.208), kind=kLoop, calls=%fused_computation.65 | loop fusion | flops 117440512 | bytes 117440512 | tf_op jit(solution)/shard_map/concatenate | solution.py:166
  1023.5 493.0 %while.35 = (s32[]{:T(128)}, f32[64,128,128]{2,0,1:T(8,128)}, s32[28]{0:T(128)S(1)}, s32[32,28]{0,1:T(8,128)S(1)}, bf16[4096,3584]{1,0:T(8,128)(2,1)}, /*index=5...) while((s32[]{:T(128)}, f32[64,128,128]{2,0,1:T(8,128)}, ...), condition=%wide.region_12.13_spmd.clone, body=%wide.region_11.12_spmd.clone.sunk | while | flops 1076891648 | bytes 60886060 | solution.py:126
  1043.1 5.3 fusion.164
  1061.4 5.3 fusion.164
  1076.4 3.2 fusion.162
  1079.7 5.4 fusion.164
  1097.5 5.4 fusion.164
  1111.3 3.2 fusion.162
  1114.6 5.3 fusion.164
  1131.7 5.4 fusion.164
  1149.0 5.4 fusion.164
  1162.9 3.2 fusion.162
  1166.2 5.3 fusion.164
  1183.3 5.4 fusion.164
  1197.2 3.2 fusion.162
  1200.5 5.3 fusion.164
  1217.7 5.4 fusion.164
  1231.6 3.2 fusion.162
  1234.8 5.3 fusion.164
  1248.7 3.2 fusion.162
  1252.0 5.3 fusion.164
  1269.1 5.4 fusion.164
  1283.0 3.2 fusion.162
  1286.3 5.3 fusion.164
  1300.2 3.2 fusion.162
  1303.4 5.3 fusion.164
  1320.6 5.4 fusion.164
  1334.5 3.2 fusion.162
  1337.7 5.3 fusion.164
  1351.6 3.2 fusion.162
  1354.9 5.3 fusion.164
  1368.8 3.2 fusion.162
  1372.0 5.3 fusion.164
  1389.2 5.4 fusion.164
  1403.1 3.2 fusion.162
  1406.3 5.3 fusion.164
  1420.2 3.2 fusion.162
  1423.5 5.3 fusion.164
  1437.3 3.2 fusion.162
  1440.6 5.3 fusion.164
  1454.5 3.2 fusion.162
  1457.7 5.3 fusion.164
  1471.6 3.2 fusion.162
  1474.9 5.3 fusion.164
  1488.7 3.2 fusion.162
  1492.0 5.3 fusion.164
  1505.9 3.2 fusion.162
  1509.1 5.3 fusion.164
  1519.2 3.3 copy.127
  1522.5 4.7 copy.166
  1529.7 10.8 fusion.77
  1540.5 10.0 copy.130
  1550.5 10.0 copy.129
  1560.4 9.1 reduce-scatter.5.cloned.1.call-done
  (762 shorter events, 597.1 us)
Async XLA Ops:
  7.2 51.6 %all-gather.4.cloned.1.call-start = ((), (), s32[]{:S(2)}) async-start(), calls=%async_computation.2 | async-start | bytes 2621440 | tf_op jit(solution)/shard_map/all_gather | solution.py:45
  9.3 227.9 %all-gather.6.cloned.1.call-start = ((), (), s32[]{:S(2)}) async-start(), calls=%async_computation.3 | async-start | bytes 36700160 | tf_op jit(solution)/shard_map/all_gather | solution.py:52
  10.1 406.7 %all-gather.8.cloned.1.call-start = ((), (), s32[]{:S(2)}) async-start(), calls=%async_computation.4 | async-start | bytes 36700160 | tf_op jit(solution)/shard_map/all_gather | solution.py:53
  10.8 1518.9 %reduce-scatter.3.cloned.1.call-start = ((), (), s32[]{:S(2)}) async-start(), calls=%async_computation.5 | async-start | bytes 73400320 | tf_op jit(solution)/shard_map/reduce_scatter | solution.py:165
  58.8 3.1 copy-start.2
  688.3 4.5 copy-start.5
  692.8 3.2 copy-start.3
  1023.5 546.1 %reduce-scatter.5.cloned.1.call-start = ((), (), s32[]{:S(2)}) async-start(), calls=%async_computation.6 | async-start | bytes 2621440 | tf_op jit(solution)/shard_map/reduce_scatter | solution.py:128
  1039.8 3.3 copy-start
  1048.5 2.5 copy-start.1
  1058.1 3.3 copy-start
  1066.7 2.5 copy-start.1
  1076.4 3.3 copy-start
  1085.1 2.5 copy-start.1
  1094.2 3.3 copy-start
  1102.8 2.0 copy-start.1
  1111.3 3.3 copy-start
  1119.9 2.0 copy-start.1
  1128.5 3.3 copy-start
  1137.1 2.0 copy-start.1
  1145.8 3.3 copy-start
  1154.4 2.0 copy-start.1
  1162.9 3.3 copy-start
  1171.5 2.0 copy-start.1
  1180.0 3.3 copy-start
  1188.7 2.0 copy-start.1
  1197.2 3.3 copy-start
  1205.8 2.0 copy-start.1
  1214.4 3.3 copy-start
  1223.1 2.0 copy-start.1
  1231.6 3.3 copy-start
  1240.2 2.0 copy-start.1
  1248.7 3.3 copy-start
  1257.3 2.0 copy-start.1
  1265.9 3.3 copy-start
  1274.5 2.0 copy-start.1
  1283.0 3.3 copy-start
  1291.6 2.0 copy-start.1
  1300.2 3.3 copy-start
  1308.8 2.0 copy-start.1
  1317.3 3.3 copy-start
  1325.9 2.0 copy-start.1
  1334.5 3.3 copy-start
  1343.1 2.0 copy-start.1
  1351.6 3.3 copy-start
  1360.3 2.0 copy-start.1
  1368.8 3.3 copy-start
  1377.4 2.0 copy-start.1
  1385.9 3.3 copy-start
  1394.5 2.0 copy-start.1
  1403.0 3.3 copy-start
  1411.7 2.0 copy-start.1
  1420.2 3.3 copy-start
  1428.8 2.0 copy-start.1
  1437.3 3.3 copy-start
  1445.9 2.0 copy-start.1
  1454.5 3.3 copy-start
  1463.1 2.0 copy-start.1
  1471.6 3.3 copy-start
  1480.2 2.0 copy-start.1
  1488.7 3.3 copy-start
  1497.4 2.0 copy-start.1
  1505.9 3.3 copy-start
  1514.5 2.0 copy-start.1
  (6 other events, 9.8 us)
Sparse Core Ops, SparseCore 0:
  10.1 48.6 all-gather.3
  60.4 176.7 all-gather.5
  238.7 177.9 all-gather.7
  1023.6 394.9 reduce-scatter.2
  1527.4 42.1 reduce-scatter.4
where the time goes:
time: 1590 us; the launch traced here: 1580 us
  matrix products  603 us (38%)
  waiting for transfers between devices  398 us (25%)
  local copies, waits for them, and re-layouts  241 us (15%)
  loops' own time  214 us (13%)
  other arithmetic  94.4 us (6%)
    all_gather x1, waiting for transfers between devices, shards(): lax.all_gather(up_weight, 'fsdp', axis=0, tiled=True)  180 us
    all_gather x1, waiting for transfers between devices, shards(): lax.all_gather(gate_weight, 'fsdp', axis=0, tiled=True)  162 us
    dot_general x28, matrix products, step_block(): jnp.einsum('ki,kbt->ibt', up_place, up_back.reshape(up_kept.shape[0], BLK...  150 us
    dot_general x28, matrix products, step_block(): jnp.einsum('ki,kbt->ibt', gate_place, gate_back.reshape(gate_kept.shape[0...  90.7 us
    another operation x1, loops' own time, shards(): accumulated, unused = lax.scan(step_block, start_blocks, jnp.arange(blocks))  83.6 us
    another operation x1, loops' own time, shards(): gate_acc, up_acc = lax.map(forward_per_block, jnp.arange(blocks))  74 us
    dot_general x28, matrix products, forward_per_block(): jnp.einsum('nt,nc->tc', gate_feat, gate_slab, preferred_element_type=jnp....  65.5 us
    dot_general x28, matrix products, forward_per_block(): jnp.einsum('nt,nc->tc', up_feat, up_slab, preferred_element_type=jnp.floa...  65.4 us
  transfers between devices with their start and end apart: 5, of which 4 were waited for; matrix products, arithmetic and copies ran while one was open for 26% of the time, Pallas kernels for 0%

commit v1 on v0

v1 whole, which is shorter than its diff:
```python
import functools
import math

import jax
import jax.numpy as jnp
from jax import lax
from jax.experimental import pallas as pl
from jax.experimental.pallas import tpu as pltpu
from jax.sharding import PartitionSpec as P

D = 8192
FFW = 14336
BLK = 128
LANES = 128
CORES = 2
CHUNKS = 2
VMEM = 56 * 1024 * 1024
BF16 = jnp.bfloat16
F32 = jnp.float32


def column_group(blocks):
    return max(n for n in (1, 2, 3, 4) if blocks % n == 0)


def params():
    return pltpu.CompilerParams(vmem_limit_bytes=VMEM, dimension_semantics=("arbitrary",))


def block_at(index):
    return pl.ds(pl.multiple_of(index * BLK, BLK), BLK)


def copies_of(pieces, refs, target, sems):
    out = []
    for (array, parts, column), ref in zip(pieces, refs, strict=True):
        for source_row, rows, target_row in parts:
            out.append(
                pltpu.make_async_copy(
                    ref.at[pl.ds(source_row, rows), :],
                    target.at[pl.ds(target_row, rows), pl.ds(column, array.shape[1])],
                    sems.at[len(out)],
                )
            )
    return out


def copy_count(pieces):
    return sum(len(parts) for _, parts, _ in pieces)


def load_pieces(pieces, refs, target, sems):
    @pl.when(pl.program_id(0) == 0)
    def _():
        copies = copies_of(pieces, refs, target, sems)
        for copy in copies:
            copy.start()
        for copy in copies:
            copy.wait()


def forward(pieces, rows, width, gate_own, up_own, gate_weight, up_weight):
    slots, blocks = gate_own.shape
    group = column_group(blocks)
    half = rows // CORES
    depth = slots * BLK
    count = len(pieces)

    def kernel(gk, uk, *refs):
        token_refs = refs[:count]
        wg, wu, keep, send, held, sems = refs[count:]
        load_pieces(pieces, token_refs, held, sems)
        step = pl.program_id(0)
        for j in range(group):
            cols = slice(j * BLK, (j + 1) * BLK)
            for proj, (kept, weight) in enumerate(((gk, wg), (uk, wu))):
                feats = [held[:, block_at(kept[k * blocks + step * group + j])] for k in range(slots)]
                total = jnp.dot(
                    jnp.concatenate(feats, axis=1), weight[:, cols], preferred_element_type=F32
                )
                keep[proj, :, cols] = total[:half].astype(BF16)
                send[proj, :, cols] = total[half:].astype(BF16)

    weight_spec = pl.BlockSpec((depth, group * BLK), lambda i, *_: (0, i))
    out_spec = pl.BlockSpec((2, half, group * BLK), lambda i, *_: (0, 0, i))
    out = jax.ShapeDtypeStruct((2, half, blocks * BLK), BF16)
    return pl.pallas_call(
        kernel,
        out_shape=(out, out),
        grid_spec=pltpu.PrefetchScalarGridSpec(
            num_scalar_prefetch=2,
            grid=(blocks // group,),
            in_specs=[pl.BlockSpec(memory_space=pl.ANY)] * count + [weight_spec] * 2,
            out_specs=(out_spec, out_spec),
            scratch_shapes=[
                pltpu.VMEM((rows, width), BF16),
                pltpu.SemaphoreType.DMA((copy_count(pieces),)),
            ],
        ),
        compiler_params=params(),
        cost_estimate=pl.CostEstimate(
            flops=8 * rows * depth * blocks * BLK,
            bytes_accessed=4 * depth * blocks * BLK + 2 * rows * width,
            transcendentals=0,
        ),
        name="forward",
    )(
        gate_own.reshape(-1),
        up_own.reshape(-1),
        *[piece[0] for piece in pieces],
        gate_weight,
        up_weight,
    )


def transposed(pieces, rows, width):
    step_cols = 1024
    count = len(pieces)

    def kernel(*refs):
        token_refs = refs[:count]
        out, held, sems = refs[count:]
        load_pieces(pieces, token_refs, held, sems)
        step = pl.program_id(0)
        for j in range(step_cols // BLK):
            out[j * BLK : (j + 1) * BLK, :] = held[:, block_at(step * (step_cols // BLK) + j)].T

    return pl.pallas_call(
        kernel,
        out_shape=jax.ShapeDtypeStruct((width, rows), BF16),
        grid=(width // step_cols,),
        in_specs=[pl.BlockSpec(memory_space=pl.ANY)] * count,
        out_specs=pl.BlockSpec((step_cols, rows), lambda i: (i, 0)),
        scratch_shapes=[
            pltpu.VMEM((rows, width), BF16),
            pltpu.SemaphoreType.DMA((copy_count(pieces),)),
        ],
        compiler_params=params(),
        cost_estimate=pl.CostEstimate(
            flops=0, bytes_accessed=12 * rows * width, transcendentals=0
        ),
        name="transposed",
    )(*[piece[0] for piece in pieces])


def reached_pairs(pieces, rows, width, gate_kept, up_kept, same_example):
    keep, blocks = gate_kept.shape
    row_blocks = width // BLK
    count = len(pieces)

    def kernel(gk, uk, *refs):
        token_refs = refs[:count]
        same, out, held, pairs, sems = refs[count:]
        load_pieces(pieces, token_refs, held, sems)
        step = pl.program_id(0)

        @pl.when(step == 0)
        def _():
            def one(i, carry):
                feats = held[:, block_at(i)]
                pairs[i] = lax.dot_general(
                    feats, feats, (((1,), (1,)), ((), ())), preferred_element_type=F32
                )
                return carry

            lax.fori_loop(0, row_blocks, one, 0)

        for proj, kept in enumerate((gk, uk)):
            total = pairs[kept[step]]
            for k in range(1, keep):
                total = total + pairs[kept[k * blocks + step]]
            out[proj, 0] = total * same[...]

    return pl.pallas_call(
        kernel,
        out_shape=jax.ShapeDtypeStruct((2, blocks, rows, rows), F32),
        grid_spec=pltpu.PrefetchScalarGridSpec(
            num_scalar_prefetch=2,
            grid=(blocks,),
            in_specs=[pl.BlockSpec(memory_space=pl.ANY)] * count
            + [pl.BlockSpec((rows, rows), lambda i, *_: (0, 0))],
            out_specs=pl.BlockSpec((2, 1, rows, rows), lambda i, *_: (0, i, 0, 0)),
            scratch_shapes=[
                pltpu.VMEM((rows, width), BF16),
                pltpu.VMEM((row_blocks, rows, rows), F32),
                pltpu.SemaphoreType.DMA((copy_count(pieces),)),
            ],
        ),
        compiler_params=params(),
        cost_estimate=pl.CostEstimate(
            flops=2 * keep * blocks * rows * rows,
            bytes_accessed=40 * blocks * rows * rows,
            transcendentals=0,
        ),
        name="reached_pairs",
    )(gate_kept.reshape(-1), up_kept.reshape(-1), *[piece[0] for piece in pieces], same_example)


def example_squares(reached, cots, member):
    blocks, rows = reached.shape[1:3]
    group = column_group(blocks)
    count = len(cots)

    def kernel(*refs):
        cot_refs = refs[:count]
        reach, members, out, total = refs[count:]
        step = pl.program_id(0)

        @pl.when(step == 0)
        def _():
            total[...] = jnp.zeros_like(total)

        added = total[...]
        for j in range(group):
            cols = slice(j * BLK, (j + 1) * BLK)
            for proj in range(2):
                shaped = jnp.concatenate([ref[proj, :, cols] for ref in cot_refs], axis=0)
                own = lax.dot_general(
                    shaped, shaped, (((1,), (1,)), ((), ())), preferred_element_type=F32
                )
                added = added + own * reach[proj, j]
        total[...] = added

        @pl.when(step == pl.num_programs(0) - 1)
        def _():
            per_token = jnp.sum(total[...], axis=1, keepdims=True)
            per_example = jnp.sum(per_token * members[...], axis=0, keepdims=True)
            out[...] = jnp.broadcast_to(per_example, out.shape)

    cot_rows = cots[0].shape[1]
    return pl.pallas_call(
        kernel,
        out_shape=jax.ShapeDtypeStruct((8, LANES), F32),
        grid=(blocks // group,),
        in_specs=[pl.BlockSpec((2, cot_rows, group * BLK), lambda i: (0, 0, i))] * count
        + [
            pl.BlockSpec((2, group, rows, rows), lambda i: (0, i, 0, 0)),
            pl.BlockSpec((rows, LANES), lambda i: (0, 0)),
        ],
        out_specs=pl.BlockSpec((8, LANES), lambda i: (0, 0)),
        scratch_shapes=[pltpu.VMEM((rows, rows), F32)],
        compiler_params=params(),
        cost_estimate=pl.CostEstimate(
            flops=8 * blocks * rows * rows * BLK,
            bytes_accessed=8 * blocks * rows * rows,
            transcendentals=0,
        ),
        name="example_squares",
    )(*cots, reached, member)


def token_backward(cots, width, gate_own, up_own, gate_weight, up_weight):
    slots, blocks = gate_own.shape
    group = column_group(blocks)
    depth = slots * BLK
    count = len(cots)
    piece_rows = cots[0].shape[1]
    rows = piece_rows * count
    half = rows // CORES

    def kernel(gk, uk, *refs):
        cot_refs = refs[:count]
        wg, wu, keep, send, total = refs[count:]
        step = pl.program_id(0)

        @pl.when(step == 0)
        def _():
            total[...] = jnp.zeros_like(total)

        for j in range(group):
            cols = slice(j * BLK, (j + 1) * BLK)
            for proj, (kept, weight) in enumerate(((gk, wg), (uk, wu))):
                cot = jnp.concatenate([ref[proj, :, cols] for ref in cot_refs], axis=0)
                back = lax.dot_general(
                    cot, weight[:, cols], (((1,), (1,)), ((), ())), preferred_element_type=F32
                )
                for k in range(slots):
                    place = block_at(kept[k * blocks + step * group + j])
                    total[:, place] = total[:, place] + back[:, k * BLK : (k + 1) * BLK]

        @pl.when(step == pl.num_programs(0) - 1)
        def _():
            keep[...] = total[:half].astype(BF16)
            send[...] = total[half:].astype(BF16)

    weight_spec = pl.BlockSpec((depth, group * BLK), lambda i, *_: (0, i))
    out = jax.ShapeDtypeStruct((half, width), BF16)
    out_spec = pl.BlockSpec((half, width), lambda i, *_: (0, 0))
    return pl.pallas_call(
        kernel,
        out_shape=(out, out),
        grid_spec=pltpu.PrefetchScalarGridSpec(
            num_scalar_prefetch=2,
            grid=(blocks // group,),
            in_specs=[
                pl.BlockSpec((2, piece_rows, group * BLK), lambda i, *_: (0, 0, i))
            ]
            * count
            + [weight_spec] * 2,
            out_specs=(out_spec, out_spec),
            scratch_shapes=[pltpu.VMEM((rows, width), F32)],
        ),
        compiler_params=params(),
        cost_estimate=pl.CostEstimate(
            flops=8 * rows * depth * blocks * BLK,
            bytes_accessed=4 * depth * blocks * BLK + 2 * rows * width,
            transcendentals=0,
        ),
        name="token_backward",
    )(gate_own.reshape(-1), up_own.reshape(-1), *cots, gate_weight, up_weight)


def weight_gradients(turned, cots, factors, gate_own, up_own):
    slots, blocks = gate_own.shape
    group = column_group(blocks)
    depth = slots * BLK
    chunks = len(turned)
    per_chunk = len(cots) // chunks
    piece_rows = cots[0].shape[1]
    rows = piece_rows * per_chunk
    width = turned[0].shape[0]

    def kernel(gk, uk, *refs):
        token_refs = refs[:chunks]
        cot_refs = refs[chunks : chunks + len(cots)]
        factor, gate_out, up_out = refs[chunks + len(cots) :]
        step = pl.program_id(0)
        for j in range(group):
            cols = slice(j * BLK, (j + 1) * BLK)
            for proj, (kept, out) in enumerate(((gk, gate_out), (uk, up_out))):
                total = None
                for chunk in range(chunks):
                    cot = jnp.concatenate(
                        [
                            ref[proj, :, cols]
                            for ref in cot_refs[chunk * per_chunk : (chunk + 1) * per_chunk]
                        ],
                        axis=0,
                    )
                    scaled = (
                        factor[chunk * rows : (chunk + 1) * rows, :] * cot.astype(F32)
                    ).astype(BF16)
                    feats = [
                        token_refs[chunk][block_at(kept[k * blocks + step * group + j]), :]
                        for k in range(slots)
                    ]
                    term = jnp.dot(
                        jnp.concatenate(feats, axis=0), scaled, preferred_element_type=F32
                    )
                    total = term if total is None else total + term
                out[:, cols] = total.astype(BF16)

    out = jax.ShapeDtypeStruct((depth, blocks * BLK), BF16)
    out_spec = pl.BlockSpec((depth, group * BLK), lambda i, *_: (0, i))
    return pl.pallas_call(
        kernel,
        out_shape=(out, out),
        grid_spec=pltpu.PrefetchScalarGridSpec(
            num_scalar_prefetch=2,
            grid=(blocks // group,),
            in_specs=[
                pl.BlockSpec((width, rows), lambda i, *_: (0, 0), pipeline_mode=pl.Buffered(1))
            ]
            * chunks
            + [pl.BlockSpec((2, piece_rows, group * BLK), lambda i, *_: (0, 0, i))] * len(cots)
            + [pl.BlockSpec((rows * chunks, LANES), lambda i, *_: (0, 0))],
            out_specs=(out_spec, out_spec),
        ),
        compiler_params=params(),
        cost_estimate=pl.CostEstimate(
            flops=8 * rows * chunks * depth * blocks * BLK,
            bytes_accessed=4 * depth * blocks * BLK + 2 * rows * chunks * width,
            transcendentals=0,
        ),
        name="weight_gradients",
    )(gate_own.reshape(-1), up_own.reshape(-1), *turned, *cots, factors)


def shards(
    tokens,
    hidden_cotangent,
    gate_weight,
    up_weight,
    gate_kept,
    up_kept,
    example_number,
    clip_norm,
    fsdp,
    tensor,
):
    chips = fsdp // CORES
    own_rows, own_features = tokens.shape
    blocks = gate_kept.shape[1]
    width = own_features * tensor
    blocks_each = own_features // BLK
    chunk_rows = own_rows // CHUNKS
    half = chips * chunk_rows
    rows = CORES * half
    z = lax.axis_index("tensor")
    f = lax.axis_index("fsdp")

    def from_chip(value, back):
        pairs = [
            (i, ((i // CORES + back) % chips) * CORES + i % CORES) for i in range(fsdp)
        ]
        return lax.ppermute(value, "fsdp", pairs)

    def from_core(value):
        return lax.ppermute(value, "fsdp", [(i, i ^ 1) for i in range(fsdp)])

    def from_tensor(value, back):
        return lax.ppermute(value, "tensor", [(i, (i + back) % tensor) for i in range(tensor)])

    def renumber(kept):
        return jnp.mod(z - kept // blocks_each, tensor) * blocks_each + kept % blocks_each

    gate_all, up_all = renumber(gate_kept), renumber(up_kept)
    slots = gate_weight.shape[0] // BLK
    gate_own = lax.dynamic_slice_in_dim(gate_all, f * slots, slots, 0)
    up_own = lax.dynamic_slice_in_dim(up_all, f * slots, slots, 0)

    def gather_tokens(chunk):
        own = tokens[chunk * chunk_rows : (chunk + 1) * chunk_rows]
        held = jnp.concatenate([own] + [from_chip(own, s) for s in range(1, chips)], axis=0)
        near = [held]
        for _ in range(1, tensor):
            held = from_tensor(held, 1)
            near.append(held)
        far = [from_core(part) for part in near]
        pieces = []
        for core, parts in enumerate((near, far)):
            for p, part in enumerate(parts):
                pieces.append((part, [(0, half, core * half)], p * own_features))
        mine = [
            (part, [(0, chunk_rows, chunk * chunk_rows)], p * own_features)
            for p, part in enumerate(near)
        ]
        return pieces, mine

    gathered = [gather_tokens(chunk) for chunk in range(CHUNKS)]

    lanes = jnp.arange(LANES, dtype=jnp.int32)
    member = (example_number[:, None] == lanes[None, :]).astype(F32)
    same_example = (example_number[:, None] == example_number[None, :]).astype(F32)

    hidden_parts, own_cots, all_cots, turned = [], [], [], []
    for chunk in range(CHUNKS):
        pieces, _ = gathered[chunk]
        keep, send = forward(pieces, rows, width, gate_own, up_own, gate_weight, up_weight)
        received = from_core(send)

        def pair(s):
            span = slice(s * chunk_rows, (s + 1) * chunk_rows)
            return keep[:, span].astype(F32) + received[:, span].astype(F32)

        sums = pair(0)
        for s in range(1, chips):
            sums = sums + from_chip(pair(s).astype(BF16), -s).astype(F32)
        gate_sum, up_sum = sums[0], sums[1]
        sigmoid_gate = jax.nn.sigmoid(gate_sum)
        silu_gate = gate_sum * sigmoid_gate
        hidden_parts.append((silu_gate * up_sum).astype(BF16))
        incoming = hidden_cotangent[chunk * chunk_rows : (chunk + 1) * chunk_rows].astype(F32)
        gate_cot = incoming * up_sum * sigmoid_gate * (1.0 + gate_sum * (1.0 - sigmoid_gate))
        up_cot = incoming * silu_gate
        cots = jnp.stack([gate_cot.astype(BF16), up_cot.astype(BF16)])
        own_cots.append(cots)
        near = [cots] + [from_chip(cots, s) for s in range(1, chips)]
        all_cots.append(near + [from_core(part) for part in near])

    mine = [piece for _, pieces in gathered for piece in pieces]
    reached = reached_pairs(mine, own_rows, width, gate_all, up_all, same_example)
    turned = [transposed(pieces, rows, width) for pieces, _ in gathered]

    partial = example_squares(reached, own_cots, member)[0]
    squares = partial
    for p in range(1, tensor):
        squares = squares + from_tensor(partial, p)
    threshold = clip_norm[0] * math.sqrt(D * FFW)
    factor = threshold / jnp.maximum(jnp.sqrt(squares), threshold)
    own_factor = jnp.sum(member * factor[None, :], axis=1)
    near = [own_factor] + [from_chip(own_factor, s) for s in range(1, chips)]
    every = near + [from_core(part) for part in near]
    factors = jnp.concatenate(
        [
            part[chunk * chunk_rows : (chunk + 1) * chunk_rows]
            for chunk in range(CHUNKS)
            for part in every
        ]
    )
    factors = jnp.broadcast_to(factors[:, None], (rows * CHUNKS, LANES))

    token_parts = []
    for chunk in range(CHUNKS):
        keep, send = token_backward(
            all_cots[chunk], width, gate_own, up_own, gate_weight, up_weight
        )
        received = from_core(send)

        def share(p):
            span = slice(p * own_features, (p + 1) * own_features)
            return keep[:, span].astype(F32) + received[:, span].astype(F32)

        held = share(tensor - 1)
        for p in range(tensor - 2, -1, -1):
            held = share(p) + from_tensor(held.astype(BF16), -1).astype(F32)
        total = held[:chunk_rows]
        for s in range(1, chips):
            part = held[s * chunk_rows : (s + 1) * chunk_rows].astype(BF16)
            total = total + from_chip(part, -s).astype(F32)
        token_parts.append(total.astype(BF16))

    gate_grad, up_grad = weight_gradients(
        turned, [part for cots in all_cots for part in cots], factors, gate_own, up_own
    )
    hidden = jnp.concatenate(hidden_parts, axis=0)
    token_grad = jnp.concatenate(token_parts, axis=0)
    return (hidden, gate_grad, up_grad, token_grad)


def solution(mesh):
    rows_by_columns = P(("groups", "fsdp"), "tensor")
    return jax.shard_map(
        functools.partial(shards, fsdp=mesh.shape["fsdp"], tensor=mesh.shape["tensor"]),
        mesh=mesh,
        in_specs=(
            rows_by_columns,
            rows_by_columns,
            P("fsdp", "tensor"),
            P("fsdp", "tensor"),
            P(None, "tensor"),
            P(None, "tensor"),
            P(("groups", "fsdp")),
            P(),
        ),
        out_specs=(rows_by_columns,) * 4,
        check_vma=False,
    )
```

time: 1590 us -> 410 us (0.26)
  matrix products: 603 us -> 0 us
  local copies, waits for them, and re-layouts: 241 us -> 11 us
  loops' own time: 214 us -> 0 us
  waiting for transfers between devices: 398 us -> 194 us
  Pallas kernels: 0 us -> 149 us
  other arithmetic: 94.4 us -> 17 us
  starting transfers between devices: 0.2 us -> 36.7 us
    dot_general x343 -> x0, matrix products: 603 us -> none  [the longest x28 150 us: step_block(): jnp.einsum('ki,kbt->ibt', up_place, up_back.reshape(up_kept.shape[0], BLK...]
    all_gather x3 -> x0, waiting for transfers between devices: 387 us -> none  [the longest x1 180 us: shards(): lax.all_gather(up_weight, 'fsdp', axis=0, tiled=True)]
    another operation x3 -> x0, loops' own time: 214 us -> none  [the longest x1 83.6 us: shards(): accumulated, unused = lax.scan(step_block, start_blocks, jnp.arange(blocks))]
    ppermute x0 -> x42, waiting for transfers between devices: none -> 194 us  [the longest x9 98.5 us: from_chip(): return lax.ppermute(value, 'fsdp', pairs)]
    pallas_call x0 -> x9, Pallas kernels: none -> 149 us  [the longest x2 48.5 us: token_backward(): pl.pallas_call(kernel, out_shape=(out, out), grid_spec=pltpu.PrefetchScal...]
    while x115 -> x0, local copies, waits for them, and re-layouts: 61.2 us -> none
    convert_element_type x113 -> x0, local copies, waits for them, and re-layouts: 49 us -> none  [the longest x112 45.7 us: pick_features(): picked.astype(jnp.bfloat16)]
    dynamic_slice x84 -> x2, local copies, waits for them, and re-layouts: 48.9 us -> 0.01 us  [the longest x1 0.01 us: shards(): gate_own = lax.dynamic_slice_in_dim(gate_all, f * slots, slots, 0)]
  transfers between devices with their start and end apart: 5 -> 42, of which waited for: 4 -> 22; matrix products, arithmetic and copies ran while one was open for 26% -> 5% of each run, Pallas kernels for 0% -> 36%
where the time goes in v1:
time: 410 us; the launch traced here: 409 us
  waiting for transfers between devices  194 us (47%)
  Pallas kernels  149 us (36%)
  starting transfers between devices  36.7 us (9%)
  other arithmetic  17 us (4%)
  local copies, waits for them, and re-layouts  11 us (3%)
    ppermute x9, waiting for transfers between devices, from_chip(): return lax.ppermute(value, 'fsdp', pairs)  98.5 us
    ppermute x15, waiting for transfers between devices, from_tensor(): lax.ppermute(value, 'tensor', [(i, (i + back) % tensor) for i in range(te...  92.8 us
    pallas_call x2, Pallas kernels, token_backward(): pl.pallas_call(kernel, out_shape=(out, out), grid_spec=pltpu.PrefetchScal...  48.5 us
    pallas_call x2, Pallas kernels, forward(): pl.pallas_call(kernel, out_shape=(out, out), grid_spec=pltpu.PrefetchScal...  32.1 us
    pallas_call x1, Pallas kernels, reached_pairs(): pl.pallas_call(kernel, out_shape=jax.ShapeDtypeStruct((2, blocks, rows, r...  25.8 us
    pallas_call x1, Pallas kernels, weight_gradients(): pl.pallas_call(kernel, out_shape=(out, out), grid_spec=pltpu.PrefetchScal...  22.8 us
    ppermute x15, starting transfers between devices, from_tensor(): lax.ppermute(value, 'tensor', [(i, (i + back) % tensor) for i in range(te...  19.8 us
    ppermute x9, starting transfers between devices, from_chip(): return lax.ppermute(value, 'fsdp', pairs)  13.6 us
  transfers between devices with their start and end apart: 42, of which 22 were waited for; matrix products, arithmetic and copies ran while one was open for 5% of the time, Pallas kernels for 36%

profile of v1, /device:TPU:0, one launch (start us, length us, event | category | flops | bytes accessed | tf_op | source)
XLA Modules:
  0.0 408.8 jit_solution(16518087903613886942)
XLA Ops:
  0.7 1.1 fusion.27
  1.7 3.0 collective-permute-start.10
  4.7 6.3 %collective-permute-done.10 = bf16[64,2048]{1,0:T(8,128)(2,1)S(1)} collective-permute-done((bf16[64,2048]{1,0:T(8,128)(2,1)S(1)}, bf16[64,2048]{1,0:T(8,128)(2,1)S(1)}, u32[]{:S(2)}, u32[]{:S(2)}) %collective-permute-start.10) | collective-permute-done | bytes 262176 | tf_op jit(solution)/shard_map/ppermute | solution.py:406
  11.1 1.9 collective-permute-start.11
  13.0 1.5 collective-permute-start
  14.5 5.4 %collective-permute-done = bf16[64,2048]{1,0:T(8,128)(2,1)S(1)} collective-permute-done((bf16[64,2048]{1,0:T(8,128)(2,1)S(1)}, bf16[64,2048]{1,0:T(8,128)(2,1)S(1)}, u32[]{:S(2)}, u32[]{:S(2)}) %collective-permute-start) | collective-permute-done | bytes 262176 | tf_op jit(solution)/shard_map/ppermute | solution.py:406
  19.9 1.6 collective-permute-start.1
  21.6 6.3 %collective-permute-done.11.refs_1_.refs_5_ = bf16[128,2048]{1,0:T(8,128)(2,1)S(1)} collective-permute-done((bf16[128,2048]{1,0:T(8,128)(2,1)S(1)}, bf16[128,2048]{1,0:T(8,128)(2,1)S(1)}, u32[]{:S(2)}, u32[]{:S(2)}) %collective-permute-start.11) | collective-permute-done | bytes 524320 | tf_op jit(solution)/shard_map/ppermute | solution.py:412
  27.8 11.2 %collective-permute-done.1.refs_1_ = bf16[128,2048]{1,0:T(8,128)(2,1)S(1)} collective-permute-done((bf16[128,2048]{1,0:T(8,128)(2,1)S(1)}, bf16[128,2048]{1,0:T(8,128)(2,1)S(1)}, u32[]{:S(2)}, u32[]{:S(2)}) %collective-permute-start.1) | collective-permute-done | bytes 524320 | tf_op jit(solution)/shard_map/ppermute | solution.py:412
  39.1 11.2 %collective-permute-done.12.refs_2_.refs_6_ = bf16[128,2048]{1,0:T(8,128)(2,1)S(1)} collective-permute-done((bf16[128,2048]{1,0:T(8,128)(2,1)S(1)}, bf16[128,2048]{1,0:T(8,128)(2,1)S(1)}, u32[]{:S(2)}, u32[]{:S(2)}) %collective-permute-start.12) | collective-permute-done | bytes 524320 | tf_op jit(solution)/shard_map/ppermute | solution.py:412
  50.9 10.8 %collective-permute-done.2.refs_2_ = bf16[128,2048]{1,0:T(8,128)(2,1)} collective-permute-done((bf16[128,2048]{1,0:T(8,128)(2,1)S(1)}, bf16[128,2048]{1,0:T(8,128)(2,1)}, u32[]{:S(2)}, u32[]{:S(2)}) %collective-permute-start.2) | collective-permute-done | bytes 524320 | tf_op jit(solution)/shard_map/ppermute | solution.py:412
  61.7 11.1 %collective-permute-done.13.refs_3_.refs_7_ = bf16[128,2048]{1,0:T(8,128)(2,1)S(1)} collective-permute-done((bf16[128,2048]{1,0:T(8,128)(2,1)S(1)}, bf16[128,2048]{1,0:T(8,128)(2,1)S(1)}, u32[]{:S(2)}, u32[]{:S(2)}) %collective-permute-start.13) | collective-permute-done | bytes 524320 | tf_op jit(solution)/shard_map/ppermute | solution.py:412
  75.2 7.1 %collective-permute-done.3.refs_3_ = bf16[128,2048]{1,0:T(8,128)(2,1)} collective-permute-done((bf16[128,2048]{1,0:T(8,128)(2,1)}, bf16[128,2048]{1,0:T(8,128)(2,1)}, u32[]{:S(2)}, u32[]{:S(2)}) %collective-permute-start.3) | collective-permute-done | bytes 524320 | tf_op jit(solution)/shard_map/ppermute | solution.py:412
  82.4 16.0 %forward.3 = (bf16[2,128,3584]{2,1,0:T(8,128)(2,1)}, bf16[2,128,3584]{2,1,0:T(8,128)(2,1)}) custom-call(s32[224]{0:T(256)} %reshape.34.gk, s32[224]{0:T(256)} %reshape.35.uk, bf16[128,2048]{1,0:T(8,128)(2,1)} %copy-done, bf16[128,2048]{1,0:T(8,128)(2,1)} %copy-done.4, bf16[128,2048]{1,0:T(8,128)(2,1)} %copy-done.5, bf16[128,2048]{1,0:T(8,128)(2,1)} %copy-done.7, ...), custom_call_target="tpu_custom_call" | custom-call | flops 7516192768 | bytes 18874368 | tf_op jit(solution)/shard_map/forward/pallas_call | solution.py:87
  101.1 16.0 %forward.2 = (bf16[2,128,3584]{2,1,0:T(8,128)(2,1)}, bf16[2,128,3584]{2,1,0:T(8,128)(2,1)}) custom-call(s32[224]{0:T(256)} %reshape.34.gk, s32[224]{0:T(256)} %reshape.35.uk, bf16[128,2048]{1,0:T(8,128)(2,1)} %copy-done.1, bf16[128,2048]{1,0:T(8,128)(2,1)} %copy-done.6, bf16[128,2048]{1,0:T(8,128)(2,1)} %collective-permute-done.2.refs_2_, ...), custom_call_target="tpu_custom_call" | custom-call | flops 7516192768 | bytes 18874368 | tf_op jit(solution)/shard_map/forward/pallas_call | solution.py:87
  117.5 1.5 collective-permute-start.19
  119.0 2.2 collective-permute-done.8
  121.5 1.5 collective-permute-start.9
  123.0 17.8 %collective-permute-done.19 = bf16[2,64,3584]{2,1,0:T(8,128)(2,1)S(1)} collective-permute-done((bf16[2,64,3584]{2,1,0:T(8,128)(2,1)S(1)}, bf16[2,64,3584]{2,1,0:T(8,128)(2,1)S(1)}, u32[]{:S(2)}, u32[]{:S(2)}) %collective-permute-start.19) | collective-permute-done | bytes 917536 | tf_op jit(solution)/shard_map/ppermute | solution.py:406
  141.1 18.9 %collective-permute-done.9 = bf16[2,64,3584]{2,1,0:T(8,128)(2,1)S(1)} collective-permute-done((bf16[2,64,3584]{2,1,0:T(8,128)(2,1)S(1)}, bf16[2,64,3584]{2,1,0:T(8,128)(2,1)S(1)}, u32[]{:S(2)}, u32[]{:S(2)}) %collective-permute-start.9) | collective-permute-done | bytes 917536 | tf_op jit(solution)/shard_map/ppermute | solution.py:406
  160.3 1.3 fusion.14
  161.6 1.5 collective-permute-start.23
  163.9 21.1 %collective-permute-done.23.refs_7_.refs_1_ = bf16[2,64,3584]{2,1,0:T(8,128)(2,1)S(1)} collective-permute-done((bf16[2,64,3584]{2,1,0:T(8,128)(2,1)S(1)}, bf16[2,64,3584]{2,1,0:T(8,128)(2,1)S(1)}, u32[]{:S(2)}, u32[]{:S(2)}) %collective-permute-start.23) | collective-permute-done | bytes 917536 | tf_op jit(solution)/shard_map/ppermute | solution.py:406
  185.5 17.8 %collective-permute-done.20.refs_3_.refs_1_ = bf16[2,64,3584]{2,1,0:T(8,128)(2,1)S(1)} collective-permute-done((bf16[2,64,3584]{2,1,0:T(8,128)(2,1)S(1)}, bf16[2,64,3584]{2,1,0:T(8,128)(2,1)S(1)}, u32[]{:S(2)}, u32[]{:S(2)}) %collective-permute-start.20) | collective-permute-done | bytes 917536 | tf_op jit(solution)/shard_map/ppermute | solution.py:406
  203.3 1.0 copy-done.23
  204.4 1.0 copy-done.24
  205.4 24.2 %token_backward.3 = (bf16[128,8192]{1,0:T(8,128)(2,1)}, bf16[128,8192]{1,0:T(8,128)(2,1)}) custom-call(s32[224]{0:T(256)} %reshape.34.gk, s32[224]{0:T(256)} %reshape.35.uk, bf16[2,64,3584]{2,1,0:T(8,128)(2,1)} %copy-done.2, bf16[2,64,3584]{2,1,0:T(8,128)(2,1)} %copy-done.21, bf16[2,64,3584]{2,1,0:T(8,128)(2,1)} %copy-done.23, ...), custom_call_target="tpu_custom_call" | custom-call | flops 7516192768 | bytes 18874368 | tf_op jit(solution)/shard_map/token_backward/pallas_call | solution.py:289
  230.1 0.9 copy-done.25
  231.0 24.3 %token_backward.2 = (bf16[128,8192]{1,0:T(8,128)(2,1)}, bf16[128,8192]{1,0:T(8,128)(2,1)}) custom-call(s32[224]{0:T(256)} %reshape.34.gk, s32[224]{0:T(256)} %reshape.35.uk, bf16[2,64,3584]{2,1,0:T(8,128)(2,1)} %copy-done.3, bf16[2,64,3584]{2,1,0:T(8,128)(2,1)} %copy-done.22, bf16[2,64,3584]{2,1,0:T(8,128)(2,1)} %copy-done.25, ...), custom_call_target="tpu_custom_call" | custom-call | flops 7516192768 | bytes 18874368 | tf_op jit(solution)/shard_map/token_backward/pallas_call | solution.py:289
  258.1 25.8 %reached_pairs.1.refs_2_ = f32[2,28,128,128]{3,2,1,0:T(8,128)} custom-call(s32[896]{0:T(1024)} %reshape.36.gk, s32[896]{0:T(1024)} %reshape.37.uk, bf16[128,2048]{1,0:T(8,128)(2,1)} %copy-done.1, bf16[128,2048]{1,0:T(8,128)(2,1)} %copy-done.6, bf16[128,2048]{1,0:T(8,128)(2,1)} %collective-permute-done.2.refs_2_, ...), custom_call_target="tpu_custom_call" | custom-call | flops 29360128 | bytes 18350080 | tf_op jit(solution)/shard_map/reached_pairs/pallas_call | solution.py:174
  284.0 6.4 %transposed.2.refs_0_ = bf16[8192,256]{1,0:T(8,128)(2,1)} custom-call(bf16[128,2048]{1,0:T(8,128)(2,1)} %copy-done.1, bf16[128,2048]{1,0:T(8,128)(2,1)} %copy-done.6, bf16[128,2048]{1,0:T(8,128)(2,1)} %collective-permute-done.2.refs_2_, bf16[128,2048]{1,0:T(8,128)(2,1)} %collective-permute-done.3.refs_3_, bf16[128,2048]{1,0:T(8,128)(2,1)} %copy-done.14, ...), custom_call_target="tpu_custom_call" | custom-call | bytes 25165824 | tf_op jit(solution)/shard_map/transposed/pallas_call | solution.py:128
  290.4 6.5 %transposed.3.refs_1_ = bf16[8192,256]{1,0:T(8,128)(2,1)} custom-call(bf16[128,2048]{1,0:T(8,128)(2,1)} %copy-done, bf16[128,2048]{1,0:T(8,128)(2,1)} %copy-done.4, bf16[128,2048]{1,0:T(8,128)(2,1)} %copy-done.5, bf16[128,2048]{1,0:T(8,128)(2,1)} %copy-done.7, bf16[128,2048]{1,0:T(8,128)(2,1)} %collective-permute-done.14.refs_4_, ...), custom_call_target="tpu_custom_call" | custom-call | bytes 25165824 | tf_op jit(solution)/shard_map/transposed/pallas_call | solution.py:128
  296.9 6.7 %example_squares.1 = f32[8,128]{1,0:T(8,128)} custom-call(bf16[2,64,3584]{2,1,0:T(8,128)(2,1)} %copy-done.3, bf16[2,64,3584]{2,1,0:T(8,128)(2,1)} %copy-done.2, f32[2,28,128,128]{3,2,1,0:T(8,128)} %reached_pairs.1.refs_2_, f32[128,128]{1,0:T(8,128)} %get-tuple-element.43.refs_3_), custom_call_target="tpu_custom_call" | custom-call | flops 469762048 | bytes 3670016 | tf_op jit(solution)/shard_map/example_squares/pallas_call | solution.py:231
  303.6 0.8 slice_bitcast_fusion.4
  304.5 1.7 collective-permute-start.28
  306.2 1.1 collective-permute-start.26
  307.3 1.0 pad_maximum_fusion
  308.3 2.4 collective-permute-done.27
  310.7 0.9 collective-permute-done.26
  312.4 1.7 collective-permute-start.29
  314.2 1.8 collective-permute-done.29
  316.1 1.2 add_convert_fusion.4
  317.3 0.9 collective-permute-start.38
  318.2 1.2 add_convert_fusion.7
  319.4 1.8 collective-permute-start.33
  321.2 10.8 %collective-permute-done.38 = bf16[128,2048]{1,0:T(8,128)(2,1)S(1)} collective-permute-done((bf16[128,2048]{1,0:T(8,128)(2,1)S(1)}, bf16[128,2048]{1,0:T(8,128)(2,1)S(1)}, u32[]{:S(2)}, u32[]{:S(2)}) %collective-permute-start.38) | collective-permute-done | bytes 524320 | tf_op jit(solution)/shard_map/ppermute | solution.py:412
  332.1 1.3 add_convert_fusion.3
  333.4 2.7 collective-permute-start.39
  336.1 7.3 %collective-permute-done.33 = bf16[128,2048]{1,0:T(8,128)(2,1)S(1)} collective-permute-done((bf16[128,2048]{1,0:T(8,128)(2,1)S(1)}, bf16[128,2048]{1,0:T(8,128)(2,1)S(1)}, u32[]{:S(2)}, u32[]{:S(2)}) %collective-permute-start.33) | collective-permute-done | bytes 524320 | tf_op jit(solution)/shard_map/ppermute | solution.py:412
  343.3 2.1 add_convert_fusion.6
  345.4 2.6 collective-permute-start.34
  348.2 6.4 %collective-permute-done.39 = bf16[128,2048]{1,0:T(8,128)(2,1)S(1)} collective-permute-done((bf16[128,2048]{1,0:T(8,128)(2,1)S(1)}, bf16[128,2048]{1,0:T(8,128)(2,1)S(1)}, u32[]{:S(2)}, u32[]{:S(2)}) %collective-permute-start.39) | collective-permute-done | bytes 524320 | tf_op jit(solution)/shard_map/ppermute | solution.py:412
  354.5 1.3 add_convert_fusion.2
  355.8 2.7 collective-permute-start.40
  358.5 7.4 %collective-permute-done.34 = bf16[128,2048]{1,0:T(8,128)(2,1)} collective-permute-done((bf16[128,2048]{1,0:T(8,128)(2,1)}, bf16[128,2048]{1,0:T(8,128)(2,1)}, u32[]{:S(2)}, u32[]{:S(2)}) %collective-permute-start.34) | collective-permute-done | bytes 524320 | tf_op jit(solution)/shard_map/ppermute | solution.py:412
  365.9 1.4 add_convert_fusion.5
  367.3 2.7 collective-permute-start.35
  370.9 22.8 %weight_gradients.1 = (bf16[1024,3584]{1,0:T(8,128)(2,1)}, bf16[1024,3584]{1,0:T(8,128)(2,1)}) custom-call(s32[224]{0:T(256)} %reshape.34.gk, s32[224]{0:T(256)} %reshape.35.uk, bf16[8192,256]{1,0:T(8,128)(2,1)} %transposed.2.refs_0_, bf16[8192,256]{1,0:T(8,128)(2,1)} %transposed.3.refs_1_, bf16[2,64,3584]{2,1,0:T(8,128)(2,1)} %copy-done.3, ...), custom_call_target="tpu_custom_call" | custom-call | flops 15032385536 | bytes 23068672 | tf_op jit(solution)/shard_map/weight_gradients/pallas_call | solution.py:355
  393.7 1.3 convert_add_fusion.2
  395.0 1.7 collective-permute-start.41
  396.7 1.3 convert_add_fusion.3
  398.4 5.8 %collective-permute-done.41 = bf16[64,2048]{1,0:T(8,128)(2,1)S(1)} collective-permute-done((bf16[64,2048]{1,0:T(8,128)(2,1)S(1)}, bf16[64,2048]{1,0:T(8,128)(2,1)S(1)}, u32[]{:S(2)}, u32[]{:S(2)}) %collective-permute-start.41) | collective-permute-done | bytes 262176 | tf_op jit(solution)/shard_map/ppermute | solution.py:406
  404.3 3.6 collective-permute-done.36
  408.0 0.8 pad_maximum_fusion.5
  (122 shorter events, 13.7 us)
Async XLA Ops:
  0.6 72.2 %copy-start.18 = (s32[32,28]{1,0:T(8,128)S(1)}, s32[32,28]{1,0:T(8,128)}, u32[]{:S(2)}) copy-start(s32[32,28]{1,0:T(8,128)} %param.12) | copy-start | bytes 10756
  0.6 72.2 %copy-start.19 = (s32[32,28]{1,0:T(8,128)S(1)}, s32[32,28]{1,0:T(8,128)}, u32[]{:S(2)}) copy-start(s32[32,28]{1,0:T(8,128)} %param.13) | copy-start | bytes 10756
  1.7 9.3 %collective-permute-start.10 = (bf16[64,2048]{1,0:T(8,128)(2,1)S(1)}, bf16[64,2048]{1,0:T(8,128)(2,1)S(1)}, u32[]{:S(2)}, u32[]{:S(2)}) collective-permute-start(bf16[64,2048]{1,0:T(8,128)(2,1)S(1)} %get-tuple-element.34), channel_id=1, source_target_pairs={{0,8},{4,12},{8,0},{12,4},{1,9},{5,13},{9,1},{13,5},{2,10},{6,14},... | collective-permute-start | bytes 786440 | tf_op jit(solution)/shard_map/ppermute | solution.py:406
  11.1 71.3 %copy-start = (bf16[128,2048]{1,0:T(8,128)(2,1)}, bf16[128,2048]{1,0:T(8,128)(2,1)S(1)}, u32[]{:S(2)}) copy-start(bf16[128,2048]{1,0:T(8,128)(2,1)S(1)} %pad_maximum_fusion.4.refs_0_.refs_4_) | copy-start | bytes 1572868
  11.1 16.7 %collective-permute-start.11 = (bf16[128,2048]{1,0:T(8,128)(2,1)S(1)}, bf16[128,2048]{1,0:T(8,128)(2,1)S(1)}, u32[]{:S(2)}, u32[]{:S(2)}) collective-permute-start(bf16[128,2048]{1,0:T(8,128)(2,1)S(1)} %pad_maximum_fusion.4.refs_0_.refs_4_), channel_id=1, source_target_pairs={{0,1},{1,2},{2,3},{3,0},{4,5},{5,6},{6,7},{7,4},{8,9},{9,10},{10,1... | collective-permute-start | bytes 1572872 | tf_op jit(solution)/shard_map/ppermute | solution.py:412
  13.0 6.9 %collective-permute-start = (bf16[64,2048]{1,0:T(8,128)(2,1)S(1)}, bf16[64,2048]{1,0:T(8,128)(2,1)S(1)}, u32[]{:S(2)}, u32[]{:S(2)}) collective-permute-start(bf16[64,2048]{1,0:T(8,128)(2,1)S(1)} %get-tuple-element.33), channel_id=1, source_target_pairs={{0,8},{4,12},{8,0},{12,4},{1,9},{5,13},{9,1},{13,5},{2,10},{6,14},... | collective-permute-start | bytes 786440 | tf_op jit(solution)/shard_map/ppermute | solution.py:406
  19.9 78.5 %copy-start.1 = (bf16[128,2048]{1,0:T(8,128)(2,1)}, bf16[128,2048]{1,0:T(8,128)(2,1)S(1)}, u32[]{:S(2)}) copy-start(bf16[128,2048]{1,0:T(8,128)(2,1)S(1)} %pad_maximum_fusion.3.refs_0_) | copy-start | bytes 1572868
  19.9 19.1 %collective-permute-start.1 = (bf16[128,2048]{1,0:T(8,128)(2,1)S(1)}, bf16[128,2048]{1,0:T(8,128)(2,1)S(1)}, u32[]{:S(2)}, u32[]{:S(2)}) collective-permute-start(bf16[128,2048]{1,0:T(8,128)(2,1)S(1)} %pad_maximum_fusion.3.refs_0_), channel_id=1, source_target_pairs={{0,1},{1,2},{2,3},{3,0},{4,5},{5,6},{6,7},{7,4},{8,9},{9,10},{10,1... | collective-permute-start | bytes 1572872 | tf_op jit(solution)/shard_map/ppermute | solution.py:412
  27.8 54.5 %copy-start.4 = (bf16[128,2048]{1,0:T(8,128)(2,1)}, bf16[128,2048]{1,0:T(8,128)(2,1)S(1)}, u32[]{:S(2)}) copy-start(bf16[128,2048]{1,0:T(8,128)(2,1)S(1)} %collective-permute-done.11.refs_1_.refs_5_) | copy-start | bytes 1572868
  27.8 22.5 %collective-permute-start.12 = (bf16[128,2048]{1,0:T(8,128)(2,1)S(1)}, bf16[128,2048]{1,0:T(8,128)(2,1)S(1)}, u32[]{:S(2)}, u32[]{:S(2)}) collective-permute-start(bf16[128,2048]{1,0:T(8,128)(2,1)S(1)} %collective-permute-done.11.refs_1_.refs_5_), channel_id=1, source_target_pairs={{0,1},{1,2},{2,3},{3,0},{4,5},{5,6},{6,7},{7,4},{8,9},{9,10},{10,1... | collective-permute-start | bytes 1572872 | tf_op jit(solution)/shard_map/ppermute | solution.py:412
  39.1 59.4 %copy-start.6 = (bf16[128,2048]{1,0:T(8,128)(2,1)}, bf16[128,2048]{1,0:T(8,128)(2,1)S(1)}, u32[]{:S(2)}) copy-start(bf16[128,2048]{1,0:T(8,128)(2,1)S(1)} %collective-permute-done.1.refs_1_) | copy-start | bytes 1572868
  39.1 22.6 %collective-permute-start.2 = (bf16[128,2048]{1,0:T(8,128)(2,1)S(1)}, bf16[128,2048]{1,0:T(8,128)(2,1)}, u32[]{:S(2)}, u32[]{:S(2)}) collective-permute-start(bf16[128,2048]{1,0:T(8,128)(2,1)S(1)} %collective-permute-done.1.refs_1_), channel_id=1, source_target_pairs={{0,1},{1,2},{2,3},{3,0},{4,5},{5,6},{6,7},{7,4},{8,9},{9,10},{10,1... | collective-permute-start | bytes 1572872 | tf_op jit(solution)/shard_map/ppermute | solution.py:412
  50.3 32.1 %copy-start.5 = (bf16[128,2048]{1,0:T(8,128)(2,1)}, bf16[128,2048]{1,0:T(8,128)(2,1)S(1)}, u32[]{:S(2)}) copy-start(bf16[128,2048]{1,0:T(8,128)(2,1)S(1)} %collective-permute-done.12.refs_2_.refs_6_) | copy-start | bytes 1572868
  50.3 22.5 %collective-permute-start.13 = (bf16[128,2048]{1,0:T(8,128)(2,1)S(1)}, bf16[128,2048]{1,0:T(8,128)(2,1)S(1)}, u32[]{:S(2)}, u32[]{:S(2)}) collective-permute-start(bf16[128,2048]{1,0:T(8,128)(2,1)S(1)} %collective-permute-done.12.refs_2_.refs_6_), channel_id=1, source_target_pairs={{0,1},{1,2},{2,3},{3,0},{4,5},{5,6},{6,7},{7,4},{8,9},{9,10},{10,1... | collective-permute-start | bytes 1572872 | tf_op jit(solution)/shard_map/ppermute | solution.py:412
  50.3 23.9 %collective-permute-start.14 = (bf16[128,2048]{1,0:T(8,128)(2,1)S(1)}, bf16[128,2048]{1,0:T(8,128)(2,1)}, u32[]{:S(2)}, u32[]{:S(2)}) collective-permute-start(bf16[128,2048]{1,0:T(8,128)(2,1)S(1)} %pad_maximum_fusion.4.refs_0_.refs_4_), channel_id=1, source_target_pairs={{0,4},{4,0},{8,12},{12,8},{1,5},{5,1},{9,13},{13,9},{2,6},{6,2},{1... | collective-permute-start | bytes 1572872 | tf_op jit(solution)/shard_map/ppermute | solution.py:409
  50.3 24.4 %collective-permute-start.15 = (bf16[128,2048]{1,0:T(8,128)(2,1)S(1)}, bf16[128,2048]{1,0:T(8,128)(2,1)}, u32[]{:S(2)}, u32[]{:S(2)}) collective-permute-start(bf16[128,2048]{1,0:T(8,128)(2,1)S(1)} %collective-permute-done.11.refs_1_.refs_5_), channel_id=1, source_target_pairs={{0,4},{4,0},{8,12},{12,8},{1,5},{5,1},{9,13},{13,9},{2,6},{6,2},{1... | collective-permute-start | bytes 1572872 | tf_op jit(solution)/shard_map/ppermute | solution.py:409
  50.8 23.9 %collective-permute-start.16 = (bf16[128,2048]{1,0:T(8,128)(2,1)S(1)}, bf16[128,2048]{1,0:T(8,128)(2,1)}, u32[]{:S(2)}, u32[]{:S(2)}) collective-permute-start(bf16[128,2048]{1,0:T(8,128)(2,1)S(1)} %collective-permute-done.12.refs_2_.refs_6_), channel_id=1, source_target_pairs={{0,4},{4,0},{8,12},{12,8},{1,5},{5,1},{9,13},{13,9},{2,6},{6,2},{1... | collective-permute-start | bytes 1572872 | tf_op jit(solution)/shard_map/ppermute | solution.py:409
  61.7 20.7 %collective-permute-start.3 = (bf16[128,2048]{1,0:T(8,128)(2,1)}, bf16[128,2048]{1,0:T(8,128)(2,1)}, u32[]{:S(2)}, u32[]{:S(2)}) collective-permute-start(bf16[128,2048]{1,0:T(8,128)(2,1)} %collective-permute-done.2.refs_2_), channel_id=1, source_target_pairs={{0,1},{1,2},{2,3},{3,0},{4,5},{5,6},{6,7},{7,4},{8,9},{9,10},{10,1... | collective-permute-start | bytes 1572872 | tf_op jit(solution)/shard_map/ppermute | solution.py:412
  72.8 9.6 %copy-start.7 = (bf16[128,2048]{1,0:T(8,128)(2,1)}, bf16[128,2048]{1,0:T(8,128)(2,1)S(1)}, u32[]{:S(2)}) copy-start(bf16[128,2048]{1,0:T(8,128)(2,1)S(1)} %collective-permute-done.13.refs_3_.refs_7_) | copy-start | bytes 1572868
  72.8 9.6 %collective-permute-start.17 = (bf16[128,2048]{1,0:T(8,128)(2,1)S(1)}, bf16[128,2048]{1,0:T(8,128)(2,1)}, u32[]{:S(2)}, u32[]{:S(2)}) collective-permute-start(bf16[128,2048]{1,0:T(8,128)(2,1)S(1)} %collective-permute-done.13.refs_3_.refs_7_), channel_id=1, source_target_pairs={{0,4},{4,0},{8,12},{12,8},{1,5},{5,1},{9,13},{13,9},{2,6},{6,2},{1... | collective-permute-start | bytes 1572872 | tf_op jit(solution)/shard_map/ppermute | solution.py:409
  74.2 24.8 %collective-permute-start.4 = (bf16[128,2048]{1,0:T(8,128)(2,1)S(1)}, bf16[128,2048]{1,0:T(8,128)(2,1)S(1)}, u32[]{:S(2)}, u32[]{:S(2)}) collective-permute-start(bf16[128,2048]{1,0:T(8,128)(2,1)S(1)} %pad_maximum_fusion.3.refs_0_), channel_id=1, source_target_pairs={{0,4},{4,0},{8,12},{12,8},{1,5},{5,1},{9,13},{13,9},{2,6},{6,2},{1... | collective-permute-start | bytes 1572872 | tf_op jit(solution)/shard_map/ppermute | solution.py:409
  74.7 24.4 %collective-permute-start.5 = (bf16[128,2048]{1,0:T(8,128)(2,1)S(1)}, bf16[128,2048]{1,0:T(8,128)(2,1)S(1)}, u32[]{:S(2)}, u32[]{:S(2)}) collective-permute-start(bf16[128,2048]{1,0:T(8,128)(2,1)S(1)} %collective-permute-done.1.refs_1_), channel_id=1, source_target_pairs={{0,4},{4,0},{8,12},{12,8},{1,5},{5,1},{9,13},{13,9},{2,6},{6,2},{1... | collective-permute-start | bytes 1572872 | tf_op jit(solution)/shard_map/ppermute | solution.py:409
  74.8 24.3 %collective-permute-start.6 = (bf16[128,2048]{1,0:T(8,128)(2,1)}, bf16[128,2048]{1,0:T(8,128)(2,1)S(1)}, u32[]{:S(2)}, u32[]{:S(2)}) collective-permute-start(bf16[128,2048]{1,0:T(8,128)(2,1)} %collective-permute-done.2.refs_2_), channel_id=1, source_target_pairs={{0,4},{4,0},{8,12},{12,8},{1,5},{5,1},{9,13},{13,9},{2,6},{6,2},{1... | collective-permute-start | bytes 1572872 | tf_op jit(solution)/shard_map/ppermute | solution.py:409
  82.3 16.8 %collective-permute-start.7 = (bf16[128,2048]{1,0:T(8,128)(2,1)}, bf16[128,2048]{1,0:T(8,128)(2,1)S(1)}, u32[]{:S(2)}, u32[]{:S(2)}) collective-permute-start(bf16[128,2048]{1,0:T(8,128)(2,1)} %collective-permute-done.3.refs_3_), channel_id=1, source_target_pairs={{0,4},{4,0},{8,12},{12,8},{1,5},{5,1},{9,13},{13,9},{2,6},{6,2},{1... | collective-permute-start | bytes 1572872 | tf_op jit(solution)/shard_map/ppermute | solution.py:409
  98.4 18.9 %copy-start.11 = (bf16[2,128,3584]{2,1,0:T(8,128)(2,1)S(1)}, bf16[2,128,3584]{2,1,0:T(8,128)(2,1)}, u32[]{:S(2)}) copy-start(bf16[2,128,3584]{2,1,0:T(8,128)(2,1)} %get-tuple-element.16) | copy-start | bytes 5505028
  98.5 18.9 %collective-permute-start.18 = (bf16[2,128,3584]{2,1,0:T(8,128)(2,1)}, bf16[2,128,3584]{2,1,0:T(8,128)(2,1)S(1)}, u32[]{:S(2)}, u32[]{:S(2)}) collective-permute-start(bf16[2,128,3584]{2,1,0:T(8,128)(2,1)} %get-tuple-element.17), channel_id=1, source_target_pairs={{0,4},{4,0},{8,12},{12,8},{1,5},{5,1},{9,13},{13,9},{2,6},{6,2},{1... | collective-permute-start | bytes 5505032 | tf_op jit(solution)/shard_map/ppermute | solution.py:409
  99.1 1.2 copy-start.16
  117.2 4.1 copy-start.12
  117.2 4.1 collective-permute-start.8
  117.5 23.2 %collective-permute-start.19 = (bf16[2,64,3584]{2,1,0:T(8,128)(2,1)S(1)}, bf16[2,64,3584]{2,1,0:T(8,128)(2,1)S(1)}, u32[]{:S(2)}, u32[]{:S(2)}) collective-permute-start(bf16[2,64,3584]{2,1,0:T(8,128)(2,1)S(1)} %add_convert_fusion), channel_id=1, source_target_pairs={{0,8},{4,12},{8,0},{12,4},{1,9},{5,13},{9,1},{13,5},{2,10},{6,14},... | collective-permute-start | bytes 2752520 | tf_op jit(solution)/shard_map/ppermute | solution.py:406
  121.5 38.5 %collective-permute-start.9 = (bf16[2,64,3584]{2,1,0:T(8,128)(2,1)S(1)}, bf16[2,64,3584]{2,1,0:T(8,128)(2,1)S(1)}, u32[]{:S(2)}, u32[]{:S(2)}) collective-permute-start(bf16[2,64,3584]{2,1,0:T(8,128)(2,1)S(1)} %add_convert_fusion.1), channel_id=1, source_target_pairs={{0,8},{4,12},{8,0},{12,4},{1,9},{5,13},{9,1},{13,5},{2,10},{6,14},... | collective-permute-start | bytes 2752520 | tf_op jit(solution)/shard_map/ppermute | solution.py:406
  141.0 19.2 %copy-start.13 = (bf16[128,3584]{1,0:T(8,128)(2,1)S(1)}, bf16[128,3584]{1,0:T(8,128)(2,1)}, u32[]{:S(2)}) copy-start(bf16[128,3584]{1,0:T(8,128)(2,1)} %param.9) | copy-start | bytes 2752516
  161.6 41.7 %copy-start.2 = (bf16[2,64,3584]{2,1,0:T(8,128)(2,1)}, bf16[2,64,3584]{2,1,0:T(8,128)(2,1)S(1)}, u32[]{:S(2)}) copy-start(bf16[2,64,3584]{2,1,0:T(8,128)(2,1)S(1)} %pad_maximum_fusion.2.refs_1_.refs_6_.refs_0_) | copy-start | bytes 2752516
  161.6 23.3 %collective-permute-start.23 = (bf16[2,64,3584]{2,1,0:T(8,128)(2,1)S(1)}, bf16[2,64,3584]{2,1,0:T(8,128)(2,1)S(1)}, u32[]{:S(2)}, u32[]{:S(2)}) collective-permute-start(bf16[2,64,3584]{2,1,0:T(8,128)(2,1)S(1)} %pad_maximum_fusion.2.refs_1_.refs_6_.refs_0_), channel_id=1, source_target_pairs={{0,8},{4,12},{8,0},{12,4},{1,9},{5,13},{9,1},{13,5},{2,10},{6,14},... | collective-permute-start | bytes 2752520 | tf_op jit(solution)/shard_map/ppermute | solution.py:406
  163.3 66.3 %copy-start.3 = (bf16[2,64,3584]{2,1,0:T(8,128)(2,1)}, bf16[2,64,3584]{2,1,0:T(8,128)(2,1)S(1)}, u32[]{:S(2)}) copy-start(bf16[2,64,3584]{2,1,0:T(8,128)(2,1)S(1)} %pad_maximum_fusion.1.refs_0_.refs_2_) | copy-start | bytes 2752516
  163.3 40.0 %collective-permute-start.20 = (bf16[2,64,3584]{2,1,0:T(8,128)(2,1)S(1)}, bf16[2,64,3584]{2,1,0:T(8,128)(2,1)S(1)}, u32[]{:S(2)}, u32[]{:S(2)}) collective-permute-start(bf16[2,64,3584]{2,1,0:T(8,128)(2,1)S(1)} %pad_maximum_fusion.1.refs_0_.refs_2_), channel_id=1, source_target_pairs={{0,8},{4,12},{8,0},{12,4},{1,9},{5,13},{9,1},{13,5},{2,10},{6,14},... | collective-permute-start | bytes 2752520 | tf_op jit(solution)/shard_map/ppermute | solution.py:406
  163.9 39.4 %collective-permute-start.24 = (bf16[2,64,3584]{2,1,0:T(8,128)(2,1)S(1)}, bf16[2,64,3584]{2,1,0:T(8,128)(2,1)S(1)}, u32[]{:S(2)}, u32[]{:S(2)}) collective-permute-start(bf16[2,64,3584]{2,1,0:T(8,128)(2,1)S(1)} %pad_maximum_fusion.2.refs_1_.refs_6_.refs_0_), channel_id=1, source_target_pairs={{0,4},{4,0},{8,12},{12,8},{1,5},{5,1},{9,13},{13,9},{2,6},{6,2},{1... | collective-permute-start | bytes 2752520 | tf_op jit(solution)/shard_map/ppermute | solution.py:409
  185.0 18.4 %copy-start.21 = (bf16[2,64,3584]{2,1,0:T(8,128)(2,1)}, bf16[2,64,3584]{2,1,0:T(8,128)(2,1)S(1)}, u32[]{:S(2)}) copy-start(bf16[2,64,3584]{2,1,0:T(8,128)(2,1)S(1)} %collective-permute-done.23.refs_7_.refs_1_) | copy-start | bytes 2752516
  185.0 18.4 %collective-permute-start.25 = (bf16[2,64,3584]{2,1,0:T(8,128)(2,1)S(1)}, bf16[2,64,3584]{2,1,0:T(8,128)(2,1)S(1)}, u32[]{:S(2)}, u32[]{:S(2)}) collective-permute-start(bf16[2,64,3584]{2,1,0:T(8,128)(2,1)S(1)} %collective-permute-done.23.refs_7_.refs_1_), channel_id=1, source_target_pairs={{0,4},{4,0},{8,12},{12,8},{1,5},{5,1},{9,13},{13,9},{2,6},{6,2},{1... | collective-permute-start | bytes 2752520 | tf_op jit(solution)/shard_map/ppermute | solution.py:409
  185.0 45.1 %collective-permute-start.21 = (bf16[2,64,3584]{2,1,0:T(8,128)(2,1)S(1)}, bf16[2,64,3584]{2,1,0:T(8,128)(2,1)S(1)}, u32[]{:S(2)}, u32[]{:S(2)}) collective-permute-start(bf16[2,64,3584]{2,1,0:T(8,128)(2,1)S(1)} %pad_maximum_fusion.1.refs_0_.refs_2_), channel_id=1, source_target_pairs={{0,4},{4,0},{8,12},{12,8},{1,5},{5,1},{9,13},{13,9},{2,6},{6,2},{1... | collective-permute-start | bytes 2752520 | tf_op jit(solution)/shard_map/ppermute | solution.py:409
  203.3 26.3 %copy-start.22 = (bf16[2,64,3584]{2,1,0:T(8,128)(2,1)}, bf16[2,64,3584]{2,1,0:T(8,128)(2,1)S(1)}, u32[]{:S(2)}) copy-start(bf16[2,64,3584]{2,1,0:T(8,128)(2,1)S(1)} %collective-permute-done.20.refs_3_.refs_1_) | copy-start | bytes 2752516
  203.3 26.8 %collective-permute-start.22 = (bf16[2,64,3584]{2,1,0:T(8,128)(2,1)S(1)}, bf16[2,64,3584]{2,1,0:T(8,128)(2,1)}, u32[]{:S(2)}, u32[]{:S(2)}) collective-permute-start(bf16[2,64,3584]{2,1,0:T(8,128)(2,1)S(1)} %collective-permute-done.20.refs_3_.refs_1_), channel_id=1, source_target_pairs={{0,4},{4,0},{8,12},{12,8},{1,5},{5,1},{9,13},{13,9},{2,6},{6,2},{1... | collective-permute-start | bytes 2752520 | tf_op jit(solution)/shard_map/ppermute | solution.py:409
  203.3 1.1 copy-start.23
  204.4 1.0 copy-start.24
  229.6 25.8 %copy-start.20 = (s32[128]{0:T(128)S(1)}, s32[128]{0:T(128)}, u32[]{:S(2)}) copy-start(s32[128]{0:T(128)} %param.14) | copy-start | bytes 1540
  229.6 86.5 %collective-permute-start.37 = (bf16[128,8192]{1,0:T(8,128)(2,1)}, bf16[128,8192]{1,0:T(8,128)(2,1)}, u32[]{:S(2)}, u32[]{:S(2)}) collective-permute-start(bf16[128,8192]{1,0:T(8,128)(2,1)} %get-tuple-element.23), channel_id=1, source_target_pairs={{0,4},{4,0},{8,12},{12,8},{1,5},{5,1},{9,13},{13,9},{2,6},{6,2},{1... | collective-permute-start | bytes 6291464 | tf_op jit(solution)/shard_map/ppermute | solution.py:409
  255.3 62.9 %collective-permute-start.32 = (bf16[128,8192]{1,0:T(8,128)(2,1)}, bf16[128,8192]{1,0:T(8,128)(2,1)}, u32[]{:S(2)}, u32[]{:S(2)}) collective-permute-start(bf16[128,8192]{1,0:T(8,128)(2,1)} %get-tuple-element.21), channel_id=1, source_target_pairs={{0,4},{4,0},{8,12},{12,8},{1,5},{5,1},{9,13},{13,9},{2,6},{6,2},{1... | collective-permute-start | bytes 6291464 | tf_op jit(solution)/shard_map/ppermute | solution.py:409
  296.9 19.2 %copy-start.8 = (bf16[128,8192]{1,0:T(8,128)(2,1)S(1)}, bf16[128,8192]{1,0:T(8,128)(2,1)}, u32[]{:S(2)}) copy-start(bf16[128,8192]{1,0:T(8,128)(2,1)} %get-tuple-element.22) | copy-start | bytes 6291460
  303.6 14.6 %copy-start.9 = (bf16[128,8192]{1,0:T(8,128)(2,1)S(1)}, bf16[128,8192]{1,0:T(8,128)(2,1)}, u32[]{:S(2)}) copy-start(bf16[128,8192]{1,0:T(8,128)(2,1)} %get-tuple-element.20) | copy-start | bytes 6291460
  304.5 3.8 collective-permute-start.28
  306.2 4.4 %collective-permute-start.27 = (f32[128]{0:T(128)S(1)}, f32[128]{0:T(128)S(1)}, u32[]{:S(2)}, u32[]{:S(2)}) collective-permute-start(f32[128]{0:T(128)S(1)} %slice_bitcast_fusion.4), channel_id=1, source_target_pairs={{0,2},{1,3},{2,0},{3,1},{4,6},{5,7},{6,4},{7,5},{8,10},{9,11},{10,... | collective-permute-start | bytes 1544 | tf_op jit(solution)/shard_map/ppermute | solution.py:412
  306.2 5.3 %collective-permute-start.26 = (f32[128]{0:T(128)S(1)}, f32[128]{0:T(128)S(1)}, u32[]{:S(2)}, u32[]{:S(2)}) collective-permute-start(f32[128]{0:T(128)S(1)} %slice_bitcast_fusion.4), channel_id=1, source_target_pairs={{0,1},{1,2},{2,3},{3,0},{4,5},{5,6},{6,7},{7,4},{8,9},{9,10},{10,1... | collective-permute-start | bytes 1544 | tf_op jit(solution)/shard_map/ppermute | solution.py:412
  312.4 3.6 collective-permute-start.29
  314.2 6.9 %collective-permute-start.30 = (f32[128]{0:T(128)S(1)}, f32[128]{0:T(128)S(1)}, u32[]{:S(2)}, u32[]{:S(2)}) collective-permute-start(f32[128]{0:T(128)S(1)} %select_reduce_fusion), channel_id=1, source_target_pairs={{0,4},{4,0},{8,12},{12,8},{1,5},{5,1},{9,13},{13,9},{2,6},{6,2},{1... | collective-permute-start | bytes 1544 | tf_op jit(solution)/shard_map/ppermute | solution.py:409
  316.0 32.0 %collective-permute-start.31 = (f32[128]{0:T(128)S(1)}, f32[128]{0:T(128)S(1)}, u32[]{:S(2)}, u32[]{:S(2)}) collective-permute-start(f32[128]{0:T(128)S(1)} %collective-permute-done.29), channel_id=1, source_target_pairs={{0,4},{4,0},{8,12},{12,8},{1,5},{5,1},{9,13},{13,9},{2,6},{6,2},{1... | collective-permute-start | bytes 1544 | tf_op jit(solution)/shard_map/ppermute | solution.py:409
  317.3 14.8 %collective-permute-start.38 = (bf16[128,2048]{1,0:T(8,128)(2,1)S(1)}, bf16[128,2048]{1,0:T(8,128)(2,1)S(1)}, u32[]{:S(2)}, u32[]{:S(2)}) collective-permute-start(bf16[128,2048]{1,0:T(8,128)(2,1)S(1)} %add_convert_fusion.4), channel_id=1, source_target_pairs={{0,3},{1,0},{2,1},{3,2},{4,7},{5,4},{6,5},{7,6},{8,11},{9,8},{10,9... | collective-permute-start | bytes 1572872 | tf_op jit(solution)/shard_map/ppermute | solution.py:412
  319.4 23.9 %collective-permute-start.33 = (bf16[128,2048]{1,0:T(8,128)(2,1)S(1)}, bf16[128,2048]{1,0:T(8,128)(2,1)S(1)}, u32[]{:S(2)}, u32[]{:S(2)}) collective-permute-start(bf16[128,2048]{1,0:T(8,128)(2,1)S(1)} %add_convert_fusion.7), channel_id=1, source_target_pairs={{0,3},{1,0},{2,1},{3,2},{4,7},{5,4},{6,5},{7,6},{8,11},{9,8},{10,9... | collective-permute-start | bytes 1572872 | tf_op jit(solution)/shard_map/ppermute | solution.py:412
  333.4 21.2 %collective-permute-start.39 = (bf16[128,2048]{1,0:T(8,128)(2,1)S(1)}, bf16[128,2048]{1,0:T(8,128)(2,1)S(1)}, u32[]{:S(2)}, u32[]{:S(2)}) collective-permute-start(bf16[128,2048]{1,0:T(8,128)(2,1)S(1)} %add_convert_fusion.3), channel_id=1, source_target_pairs={{0,3},{1,0},{2,1},{3,2},{4,7},{5,4},{6,5},{7,6},{8,11},{9,8},{10,9... | collective-permute-start | bytes 1572872 | tf_op jit(solution)/shard_map/ppermute | solution.py:412
  345.4 20.5 %collective-permute-start.34 = (bf16[128,2048]{1,0:T(8,128)(2,1)}, bf16[128,2048]{1,0:T(8,128)(2,1)}, u32[]{:S(2)}, u32[]{:S(2)}) collective-permute-start(bf16[128,2048]{1,0:T(8,128)(2,1)} %add_convert_fusion.6), channel_id=1, source_target_pairs={{0,3},{1,0},{2,1},{3,2},{4,7},{5,4},{6,5},{7,6},{8,11},{9,8},{10,9... | collective-permute-start | bytes 1572872 | tf_op jit(solution)/shard_map/ppermute | solution.py:412
  348.2 17.7 %copy-start.10 = (bf16[128,8192]{1,0:T(8,128)(2,1)S(1)}, bf16[128,8192]{1,0:T(8,128)(2,1)}, u32[]{:S(2)}) copy-start(bf16[128,8192]{1,0:T(8,128)(2,1)} %get-tuple-element.20) | copy-start | bytes 6291460
  355.8 37.9 %collective-permute-start.40 = (bf16[128,2048]{1,0:T(8,128)(2,1)S(1)}, bf16[128,2048]{1,0:T(8,128)(2,1)S(1)}, u32[]{:S(2)}, u32[]{:S(2)}) collective-permute-start(bf16[128,2048]{1,0:T(8,128)(2,1)S(1)} %add_convert_fusion.2), channel_id=1, source_target_pairs={{0,3},{1,0},{2,1},{3,2},{4,7},{5,4},{6,5},{7,6},{8,11},{9,8},{10,9... | collective-permute-start | bytes 1572872 | tf_op jit(solution)/shard_map/ppermute | solution.py:412
  367.3 29.3 %collective-permute-start.35 = (bf16[128,2048]{1,0:T(8,128)(2,1)S(1)}, bf16[128,2048]{1,0:T(8,128)(2,1)S(1)}, u32[]{:S(2)}, u32[]{:S(2)}) collective-permute-start(bf16[128,2048]{1,0:T(8,128)(2,1)S(1)} %add_convert_fusion.5), channel_id=1, source_target_pairs={{0,3},{1,0},{2,1},{3,2},{4,7},{5,4},{6,5},{7,6},{8,11},{9,8},{10,9... | collective-permute-start | bytes 1572872 | tf_op jit(solution)/shard_map/ppermute | solution.py:412
  395.0 9.3 %collective-permute-start.41 = (bf16[64,2048]{1,0:T(8,128)(2,1)S(1)}, bf16[64,2048]{1,0:T(8,128)(2,1)S(1)}, u32[]{:S(2)}, u32[]{:S(2)}) collective-permute-start(bf16[64,2048]{1,0:T(8,128)(2,1)S(1)} %slice.277), channel_id=1, source_target_pairs={{0,8},{4,12},{8,0},{12,4},{1,9},{5,13},{9,1},{13,5},{2,10},{6,14},... | collective-permute-start | bytes 786440 | tf_op jit(solution)/shard_map/ppermute | solution.py:406
  398.0 10.0 %collective-permute-start.36 = (bf16[64,2048]{1,0:T(8,128)(2,1)S(1)}, bf16[64,2048]{1,0:T(8,128)(2,1)S(1)}, u32[]{:S(2)}, u32[]{:S(2)}) collective-permute-start(bf16[64,2048]{1,0:T(8,128)(2,1)S(1)} %slice.278), channel_id=1, source_target_pairs={{0,8},{4,12},{8,0},{12,4},{1,9},{5,13},{9,1},{13,5},{2,10},{6,14},... | collective-permute-start | bytes 786440 | tf_op jit(solution)/shard_map/ppermute | solution.py:406
  (4 other events, 3.6 us)

commit v2 on v1

--- a/solution.py
+++ b/solution.py
@@ -59,7 +59,11 @@
             copy.wait()
 
 
-def forward(pieces, rows, width, gate_own, up_own, gate_weight, up_weight):
+def waits(deps):
+    return [pl.BlockSpec(memory_space=pl.ANY)] * len(deps)
+
+
+def forward(pieces, rows, width, gate_own, up_own, gate_weight, up_weight, deps):
     slots, blocks = gate_own.shape
     group = column_group(blocks)
     half = rows // CORES
@@ -68,7 +72,8 @@
 
     def kernel(gk, uk, *refs):
         token_refs = refs[:count]
-        wg, wu, keep, send, held, sems = refs[count:]
+        wg, wu = refs[count : count + 2]
+        keep, send, held, sems = refs[count + 2 + len(deps) :]
         load_pieces(pieces, token_refs, held, sems)
         step = pl.program_id(0)
         for j in range(group):
@@ -90,7 +95,7 @@
         grid_spec=pltpu.PrefetchScalarGridSpec(
             num_scalar_prefetch=2,
             grid=(blocks // group,),
-            in_specs=[pl.BlockSpec(memory_space=pl.ANY)] * count + [weight_spec] * 2,
+            in_specs=[pl.BlockSpec(memory_space=pl.ANY)] * count + [weight_spec] * 2 + waits(deps),
             out_specs=(out_spec, out_spec),
             scratch_shapes=[
                 pltpu.VMEM((rows, width), BF16),
@@ -110,16 +115,78 @@
         *[piece[0] for piece in pieces],
         gate_weight,
         up_weight,
-    )
-
-
-def transposed(pieces, rows, width):
+        *deps,
+    )
+
+
+def after(arrays, deps):
+    arrays = list(arrays)
+
+    def kernel(*refs):
+        pass
+
+    return pl.pallas_call(
+        kernel,
+        out_shape=[jax.ShapeDtypeStruct(array.shape, array.dtype) for array in arrays],
+        in_specs=waits(arrays) + waits(deps),
+        out_specs=waits(arrays),
+        input_output_aliases={n: n for n in range(len(arrays))},
+        cost_estimate=pl.CostEstimate(flops=0, bytes_accessed=0, transcendentals=0),
+        name="after",
+    )(*arrays, *deps)
+
+
+def rows_of(array, spans, deps):
+    width = array.shape[1]
+
+    def kernel(*refs):
+        for (first, count), out in zip(spans, refs[1 + len(deps) :], strict=True):
+            out[...] = refs[0][first : first + count, :]
+
+    return pl.pallas_call(
+        kernel,
+        out_shape=[jax.ShapeDtypeStruct((count, width), array.dtype) for _, count in spans],
+        in_specs=[pl.BlockSpec(memory_space=pltpu.VMEM)] + waits(deps),
+        out_specs=[pl.BlockSpec(memory_space=pltpu.VMEM)] * len(spans),
+        compiler_params=pltpu.CompilerParams(vmem_limit_bytes=VMEM),
+        cost_estimate=pl.CostEstimate(
+            flops=0, bytes_accessed=4 * array.shape[0] * width, transcendentals=0
+        ),
+        name="rows_of",
+    )(array, *deps)
+
+
+def turned_weight(weight, deps):
+    depth, width = weight.shape
+    group = column_group(width // BLK)
+
+    def kernel(source, *refs):
+        out = refs[len(deps)]
+        for j in range(group):
+            cols = slice(j * BLK, (j + 1) * BLK)
+            out[cols, :] = source[:, cols].T
+
+    return pl.pallas_call(
+        kernel,
+        out_shape=jax.ShapeDtypeStruct((width, depth), BF16),
+        grid=(width // BLK // group,),
+        in_specs=[pl.BlockSpec((depth, group * BLK), lambda i: (0, i))] + waits(deps),
+        out_specs=pl.BlockSpec((group * BLK, depth), lambda i: (i, 0)),
+        compiler_params=params(),
+        cost_estimate=pl.CostEstimate(
+            flops=0, bytes_accessed=4 * depth * width, transcendentals=0
+        ),
+        name="turned_weight",
+    )(weight, *deps)
+
+
+def transposed(pieces, rows, width, deps):
     step_cols = 1024
     count = len(pieces)
 
     def kernel(*refs):
         token_refs = refs[:count]
-        out, held, sems = refs[count:]
+        out, held, sems = refs[count + len(deps) :]
         load_pieces(pieces, token_refs, held, sems)
         step = pl.program_id(0)
         for j in range(step_cols // BLK):
@@ -129,7 +196,7 @@
         kernel,
         out_shape=jax.ShapeDtypeStruct((width, rows), BF16),
         grid=(width // step_cols,),
-        in_specs=[pl.BlockSpec(memory_space=pl.ANY)] * count,
+        in_specs=[pl.BlockSpec(memory_space=pl.ANY)] * count + waits(deps),
         out_specs=pl.BlockSpec((step_cols, rows), lambda i: (i, 0)),
         scratch_shapes=[
             pltpu.VMEM((rows, width), BF16),
@@ -137,33 +204,103 @@
         ],
         compiler_params=params(),
         cost_estimate=pl.CostEstimate(
-            flops=0, bytes_accessed=12 * rows * width, transcendentals=0
+            flops=0, bytes_accessed=4 * rows * width, transcendentals=0
         ),
         name="transposed",
-    )(*[piece[0] for piece in pieces])
-
-
-def reached_pairs(pieces, rows, width, gate_kept, up_kept, same_example):
+    )(*[piece[0] for piece in pieces], *deps)
+
+
+def chip_share(keep, received, s, chunk_rows, deps):
+    width = keep.shape[2]
+
+    def kernel(a, b, *refs):
+        refs[len(deps)][...] = (a[...].astype(F32) + b[...].astype(F32)).astype(BF16)
+
+    spec = pl.BlockSpec((1, chunk_rows, width), lambda i: (i, s, 0))
+    return pl.pallas_call(
+        kernel,
+        out_shape=jax.ShapeDtypeStruct((2, chunk_rows, width), BF16),
+        grid=(2,),
+        in_specs=[spec, spec] + waits(deps),
+        out_specs=pl.BlockSpec((1, chunk_rows, width), lambda i: (i, 0, 0)),
+        compiler_params=params(),
+        cost_estimate=pl.CostEstimate(
+            flops=2 * chunk_rows * width, bytes_accessed=12 * chunk_rows * width, transcendentals=0
+        ),
+        name="chip_share",
+    )(keep, received, *deps)
+
+
+def cotangents(keep, received, arrived, incoming, chunk, chunk_rows, before, deps):
+    width = keep.shape[2]
+    cols = max(n for n in range(1, 8) if width // BLK % n == 0) * BLK
+    unread = list(before) + list(deps)
+
+    def kernel(a, b, *refs):
+        others = refs[: len(arrived)]
+        cot_in = refs[len(arrived)]
+        hidden, cots = refs[len(arrived) + 1 + len(unread) :]
+        sums = []
+        for proj in range(2):
+            total = a[proj].astype(F32) + b[proj].astype(F32)
+            for other in others:
+                total = total + other[proj].astype(F32)
+            sums.append(total)
+        gate_sum, up_sum = sums
+        sigmoid_gate = jax.nn.sigmoid(gate_sum)
+        silu_gate = gate_sum * sigmoid_gate
+        hidden[...] = (silu_gate * up_sum).astype(BF16)
+        value = cot_in[...].astype(F32)
+        slope = sigmoid_gate * (1.0 + gate_sum * (1.0 - sigmoid_gate))
+        cots[0] = (value * up_sum * slope).astype(BF16)
+        cots[1] = (value * silu_gate).astype(BF16)
+
+    both = pl.BlockSpec((2, chunk_rows, cols), lambda i: (0, 0, i))
+    return pl.pallas_call(
+        kernel,
+        out_shape=(
+            jax.ShapeDtypeStruct(incoming.shape, BF16),
+            jax.ShapeDtypeStruct((2, chunk_rows, width), BF16),
+        ),
+        grid=(width // cols,),
+        in_specs=[both] * (2 + len(arrived))
+        + [pl.BlockSpec((chunk_rows, cols), lambda i: (chunk, i))]
+        + waits(unread),
+        out_specs=(pl.BlockSpec((chunk_rows, cols), lambda i: (chunk, i)), both),
+        input_output_aliases={3 + len(arrived) + n: n for n in range(len(before))},
+        compiler_params=params(),
+        cost_estimate=pl.CostEstimate(
+            flops=20 * chunk_rows * width,
+            bytes_accessed=20 * chunk_rows * width,
+            transcendentals=chunk_rows * width,
+        ),
+        name="cotangents",
+    )(keep, received, *arrived, incoming, *unread)
+
+
+def reached_pairs(pieces, rows, width, gate_kept, up_kept, same_example, deps):
     keep, blocks = gate_kept.shape
     row_blocks = width // BLK
     count = len(pieces)
 
     def kernel(gk, uk, *refs):
         token_refs = refs[:count]
-        same, out, held, pairs, sems = refs[count:]
+        same = refs[count]
+        out, held, pairs, sems = refs[count + 1 + len(deps) :]
         load_pieces(pieces, token_refs, held, sems)
         step = pl.program_id(0)
 
         @pl.when(step == 0)
         def _():
-            def one(i, carry):
-                feats = held[:, block_at(i)]
-                pairs[i] = lax.dot_general(
-                    feats, feats, (((1,), (1,)), ((), ())), preferred_element_type=F32
-                )
+            def some(i, carry):
+                for n in range(8):
+                    feats = held[:, block_at(i * 8 + n)]
+                    pairs[i * 8 + n] = lax.dot_general(
+                        feats, feats, (((1,), (1,)), ((), ())), preferred_element_type=F32
+                    )
                 return carry
 
-            lax.fori_loop(0, row_blocks, one, 0)
+            lax.fori_loop(0, row_blocks // 8, some, 0)
 
         for proj, kept in enumerate((gk, uk)):
             total = pairs[kept[step]]
@@ -178,7 +315,8 @@
             num_scalar_prefetch=2,
             grid=(blocks,),
             in_specs=[pl.BlockSpec(memory_space=pl.ANY)] * count
-            + [pl.BlockSpec((rows, rows), lambda i, *_: (0, 0))],
+            + [pl.BlockSpec((rows, rows), lambda i, *_: (0, 0))]
+            + waits(deps),
             out_specs=pl.BlockSpec((2, 1, rows, rows), lambda i, *_: (0, i, 0, 0)),
             scratch_shapes=[
                 pltpu.VMEM((rows, width), BF16),
@@ -193,17 +331,24 @@
             transcendentals=0,
         ),
         name="reached_pairs",
-    )(gate_kept.reshape(-1), up_kept.reshape(-1), *[piece[0] for piece in pieces], same_example)
-
-
-def example_squares(reached, cots, member):
+    )(
+        gate_kept.reshape(-1),
+        up_kept.reshape(-1),
+        *[piece[0] for piece in pieces],
+        same_example,
+        *deps,
+    )
+
+
+def example_squares(reached, cots, member, deps):
     blocks, rows = reached.shape[1:3]
     group = column_group(blocks)
     count = len(cots)
 
     def kernel(*refs):
         cot_refs = refs[:count]
-        reach, members, out, total = refs[count:]
+        reach, members = refs[count : count + 2]
+        out, total = refs[count + 2 + len(deps) :]
         step = pl.program_id(0)
 
         @pl.when(step == 0)
@@ -236,7 +381,8 @@
         + [
             pl.BlockSpec((2, group, rows, rows), lambda i: (0, i, 0, 0)),
             pl.BlockSpec((rows, LANES), lambda i: (0, 0)),
-        ],
+        ]
+        + waits(deps),
         out_specs=pl.BlockSpec((8, LANES), lambda i: (0, 0)),
         scratch_shapes=[pltpu.VMEM((rows, rows), F32)],
         compiler_params=params(),
@@ -246,10 +392,10 @@
             transcendentals=0,
         ),
         name="example_squares",
-    )(*cots, reached, member)
-
-
-def token_backward(cots, width, gate_own, up_own, gate_weight, up_weight):
+    )(*cots, reached, member, *deps)
+
+
+def token_backward(cots, width, gate_own, up_own, gate_turned, up_turned, deps):
     slots, blocks = gate_own.shape
     group = column_group(blocks)
     depth = slots * BLK
@@ -260,7 +406,8 @@
 
     def kernel(gk, uk, *refs):
         cot_refs = refs[:count]
-        wg, wu, keep, send, total = refs[count:]
+        wg, wu = refs[count : count + 2]
+        keep, send, total = refs[count + 2 + len(deps) :]
         step = pl.program_id(0)
 
         @pl.when(step == 0)
@@ -271,19 +418,19 @@
             cols = slice(j * BLK, (j + 1) * BLK)
             for proj, (kept, weight) in enumerate(((gk, wg), (uk, wu))):
                 cot = jnp.concatenate([ref[proj, :, cols] for ref in cot_refs], axis=0)
-                back = lax.dot_general(
-                    cot, weight[:, cols], (((1,), (1,)), ((), ())), preferred_element_type=F32
-                )
+                back = jnp.dot(cot, weight[cols, :], preferred_element_type=F32)
                 for k in range(slots):
-                    place = block_at(kept[k * blocks + step * group + j])
-                    total[:, place] = total[:, place] + back[:, k * BLK : (k + 1) * BLK]
+                    place = kept[k * blocks + step * group + j]
+                    total[place] = total[place] + back[:, k * BLK : (k + 1) * BLK]
 
         @pl.when(step == pl.num_programs(0) - 1)
         def _():
-            keep[...] = total[:half].astype(BF16)
-            send[...] = total[half:].astype(BF16)
-
-    weight_spec = pl.BlockSpec((depth, group * BLK), lambda i, *_: (0, i))
+            for i in range(width // BLK):
+                cols = slice(i * BLK, (i + 1) * BLK)
+                keep[:, cols] = total[i, :half].astype(BF16)
+                send[:, cols] = total[i, half:].astype(BF16)
+
+    weight_spec = pl.BlockSpec((group * BLK, depth), lambda i, *_: (i, 0))
     out = jax.ShapeDtypeStruct((half, width), BF16)
     out_spec = pl.BlockSpec((half, width), lambda i, *_: (0, 0))
     return pl.pallas_call(
@@ -296,9 +443,10 @@
                 pl.BlockSpec((2, piece_rows, group * BLK), lambda i, *_: (0, 0, i))
             ]
             * count
-            + [weight_spec] * 2,
+            + [weight_spec] * 2
+            + waits(deps),
             out_specs=(out_spec, out_spec),
-            scratch_shapes=[pltpu.VMEM((rows, width), F32)],
+            scratch_shapes=[pltpu.VMEM((width // BLK, rows, BLK), F32)],
         ),
         compiler_params=params(),
         cost_estimate=pl.CostEstimate(
@@ -307,10 +455,39 @@
             transcendentals=0,
         ),
         name="token_backward",
-    )(gate_own.reshape(-1), up_own.reshape(-1), *cots, gate_weight, up_weight)
-
-
-def weight_gradients(turned, cots, factors, gate_own, up_own):
+    )(gate_own.reshape(-1), up_own.reshape(-1), *cots, gate_turned, up_turned, *deps)
+
+
+def added_cuts(arrays, outputs, deps):
+    count = len(arrays)
+
+    def kernel(*refs):
+        for cuts, out in zip(outputs, refs[count + len(deps) :], strict=True):
+            target = 0
+            for which, row, rows, col, cols in cuts:
+                at = (slice(row, row + rows), slice(col, col + cols))
+                total = refs[which[0]][at].astype(F32)
+                for n in which[1:]:
+                    total = total + refs[n][at].astype(F32)
+                out[target : target + rows, :] = total.astype(BF16)
+                target += rows
+
+    size = sum(array.shape[0] * array.shape[1] for array in arrays)
+    return pl.pallas_call(
+        kernel,
+        out_shape=[
+            jax.ShapeDtypeStruct((sum(cut[2] for cut in cuts), cuts[0][4]), BF16)
+            for cuts in outputs
+        ],
+        in_specs=[pl.BlockSpec(memory_space=pltpu.VMEM)] * count + waits(deps),
+        out_specs=[pl.BlockSpec(memory_space=pltpu.VMEM)] * len(outputs),
+        compiler_params=pltpu.CompilerParams(vmem_limit_bytes=VMEM),
+        cost_estimate=pl.CostEstimate(flops=size, bytes_accessed=4 * size, transcendentals=0),
+        name="added_cuts",
+    )(*arrays, *deps)
+
+
+def weight_gradients(turned, cots, factors, gate_own, up_own, deps):
     slots, blocks = gate_own.shape
     group = column_group(blocks)
     depth = slots * BLK
@@ -319,11 +496,13 @@
     piece_rows = cots[0].shape[1]
     rows = piece_rows * per_chunk
     width = turned[0].shape[0]
+    steps = blocks // group
 
     def kernel(gk, uk, *refs):
         token_refs = refs[:chunks]
         cot_refs = refs[chunks : chunks + len(cots)]
-        factor, gate_out, up_out = refs[chunks + len(cots) :]
+        factor = refs[chunks + len(cots)]
+        gate_out, up_out = refs[chunks + len(cots) + 1 + len(deps) :]
         step = pl.program_id(0)
         for j in range(group):
             cols = slice(j * BLK, (j + 1) * BLK)
@@ -352,28 +531,31 @@
 
     out = jax.ShapeDtypeStruct((depth, blocks * BLK), BF16)
     out_spec = pl.BlockSpec((depth, group * BLK), lambda i, *_: (0, i))
+    operands = [gate_own.reshape(-1), up_own.reshape(-1), *turned, *cots, factors]
     return pl.pallas_call(
         kernel,
         out_shape=(out, out),
         grid_spec=pltpu.PrefetchScalarGridSpec(
             num_scalar_prefetch=2,
-            grid=(blocks // group,),
+            grid=(steps,),
             in_specs=[
                 pl.BlockSpec((width, rows), lambda i, *_: (0, 0), pipeline_mode=pl.Buffered(1))
             ]
             * chunks
-            + [pl.BlockSpec((2, piece_rows, group * BLK), lambda i, *_: (0, 0, i))] * len(cots)
-            + [pl.BlockSpec((rows * chunks, LANES), lambda i, *_: (0, 0))],
+            + [pl.BlockSpec((2, piece_rows, group * BLK), lambda i, *_: (0, 0, i))]
+            * len(cots)
+            + [pl.BlockSpec((rows * chunks, LANES), lambda i, *_: (0, 0))]
+            + waits(deps),
             out_specs=(out_spec, out_spec),
         ),
         compiler_params=params(),
         cost_estimate=pl.CostEstimate(
-            flops=8 * rows * chunks * depth * blocks * BLK,
-            bytes_accessed=4 * depth * blocks * BLK + 2 * rows * chunks * width,
+            flops=8 * rows * chunks * depth * steps * group * BLK,
+            bytes_accessed=4 * depth * steps * group * BLK + 2 * rows * chunks * width,
             transcendentals=0,
         ),
         name="weight_gradients",
-    )(gate_own.reshape(-1), up_own.reshape(-1), *turned, *cots, factors)
+    )(*operands, *deps)
 
 
 def shards(
@@ -394,6 +576,7 @@
     width = own_features * tensor
     blocks_each = own_features // BLK
     chunk_rows = own_rows // CHUNKS
+    first_rows = chunk_rows // 2
     half = chips * chunk_rows
     rows = CORES * half
     z = lax.axis_index("tensor")
@@ -408,6 +591,13 @@
     def from_core(value):
         return lax.ppermute(value, "fsdp", [(i, i ^ 1) for i in range(fsdp)])
 
+    def from_rank(value, core, back):
+        pairs = [
+            (i, ((i // CORES + back) % chips) * CORES + (i % CORES + core) % CORES)
+            for i in range(fsdp)
+        ]
+        return lax.ppermute(value, "fsdp", pairs)
+
     def from_tensor(value, back):
         return lax.ppermute(value, "tensor", [(i, (i + back) % tensor) for i in range(tensor)])
 
@@ -419,102 +609,154 @@
     gate_own = lax.dynamic_slice_in_dim(gate_all, f * slots, slots, 0)
     up_own = lax.dynamic_slice_in_dim(up_all, f * slots, slots, 0)
 
-    def gather_tokens(chunk):
-        own = tokens[chunk * chunk_rows : (chunk + 1) * chunk_rows]
-        held = jnp.concatenate([own] + [from_chip(own, s) for s in range(1, chips)], axis=0)
-        near = [held]
-        for _ in range(1, tensor):
-            held = from_tensor(held, 1)
-            near.append(held)
-        far = [from_core(part) for part in near]
-        pieces = []
-        for core, parts in enumerate((near, far)):
-            for p, part in enumerate(parts):
-                pieces.append((part, [(0, half, core * half)], p * own_features))
-        mine = [
-            (part, [(0, chunk_rows, chunk * chunk_rows)], p * own_features)
-            for p, part in enumerate(near)
-        ]
-        return pieces, mine
-
-    gathered = [gather_tokens(chunk) for chunk in range(CHUNKS)]
-
     lanes = jnp.arange(LANES, dtype=jnp.int32)
     member = (example_number[:, None] == lanes[None, :]).astype(F32)
     same_example = (example_number[:, None] == example_number[None, :]).astype(F32)
 
-    hidden_parts, own_cots, all_cots, turned = [], [], [], []
-    for chunk in range(CHUNKS):
-        pieces, _ = gathered[chunk]
-        keep, send = forward(pieces, rows, width, gate_own, up_own, gate_weight, up_weight)
-        received = from_core(send)
-
-        def pair(s):
-            span = slice(s * chunk_rows, (s + 1) * chunk_rows)
-            return keep[:, span].astype(F32) + received[:, span].astype(F32)
-
-        sums = pair(0)
-        for s in range(1, chips):
-            sums = sums + from_chip(pair(s).astype(BF16), -s).astype(F32)
-        gate_sum, up_sum = sums[0], sums[1]
-        sigmoid_gate = jax.nn.sigmoid(gate_sum)
-        silu_gate = gate_sum * sigmoid_gate
-        hidden_parts.append((silu_gate * up_sum).astype(BF16))
-        incoming = hidden_cotangent[chunk * chunk_rows : (chunk + 1) * chunk_rows].astype(F32)
-        gate_cot = incoming * up_sum * sigmoid_gate * (1.0 + gate_sum * (1.0 - sigmoid_gate))
-        up_cot = incoming * silu_gate
-        cots = jnp.stack([gate_cot.astype(BF16), up_cot.astype(BF16)])
-        own_cots.append(cots)
-        near = [cots] + [from_chip(cots, s) for s in range(1, chips)]
-        all_cots.append(near + [from_core(part) for part in near])
-
-    mine = [piece for _, pieces in gathered for piece in pieces]
-    reached = reached_pairs(mine, own_rows, width, gate_all, up_all, same_example)
-    turned = [transposed(pieces, rows, width) for pieces, _ in gathered]
-
-    partial = example_squares(reached, own_cots, member)[0]
-    squares = partial
-    for p in range(1, tensor):
-        squares = squares + from_tensor(partial, p)
+    def piece(array, core, s, p):
+        target = core * half + s * chunk_rows
+        return (array, [(0, array.shape[0], target)], p * own_features)
+
+    part_0, part_1 = rows_of(tokens, [(0, chunk_rows), (chunk_rows, chunk_rows)], ())
+    along = [part_0] + [from_tensor(part_0, p) for p in range(1, tensor)]
+    stack = jnp.concatenate([part_1] + [from_chip(part_1, s) for s in range(1, chips)], axis=0)
+    (stack,) = after([stack], along[1:])
+    pieces_0, mine = [], []
+    for p in range(tensor):
+        mine.append((along[p], [(0, chunk_rows, 0)], p * own_features))
+        for s in range(chips):
+            array = along[p] if s == 0 else from_chip(along[p], s)
+            pieces_0 += [piece(array, 0, s, p), piece(from_core(array), 1, s, p)]
+    middle = tensor // 2
+    others = [p for p in range(1, tensor) if p != middle]
+    first, second = others[: len(others) // 2], others[len(others) // 2 :]
+    direct = {0: stack} | {p: from_tensor(stack, p) for p in range(1, tensor)}
+    keep_0, send_0 = forward(
+        pieces_0, rows, width, gate_own, up_own, gate_weight, up_weight, [stack]
+    )
+    send_0, *done = after([send_0] + [direct[p] for p in first], ())
+    direct.update(zip(first, done, strict=True))
+    received_0 = from_core(send_0)
+    gate_turned = turned_weight(gate_weight, [send_0])
+    received_0, *done = after([received_0] + [direct[p] for p in second], [gate_turned])
+    direct.update(zip(second, done, strict=True))
+    leaving_0 = [chip_share(keep_0, received_0, s, chunk_rows, ()) for s in range(1, chips)]
+    up_turned = turned_weight(up_weight, leaving_0)
+    tokens_0 = transposed(pieces_0, rows, width, [up_turned])
+    (direct[middle],) = after([direct[middle]], [tokens_0])
+    direct = [direct[p] for p in range(tensor)]
+    arrived_0 = [from_chip(part, -s - 1) for s, part in enumerate(leaving_0)]
+    pieces_1 = []
+    for p, array in enumerate(direct):
+        mine.append((array, [(0, chunk_rows, chunk_rows)], p * own_features))
+        pieces_1 += [piece(array, 0, 0, p), piece(from_core(array), 1, 0, p)]
+
+    hidden_0, cots_0 = cotangents(
+        keep_0, received_0, arrived_0, hidden_cotangent, 0, chunk_rows, (), [direct[middle]]
+    )
+    far_0 = [from_chip(cots_0, s) for s in range(1, chips)]
+    keep_1, send_1 = forward(
+        pieces_1, rows, width, gate_own, up_own, gate_weight, up_weight, [cots_0]
+    )
+    *far_0, send_1 = after(far_0 + [send_1], [keep_1])
+    received_1 = from_core(send_1)
+    tokens_1 = transposed(pieces_1, rows, width, [send_1])
+    (received_1,) = after([received_1], [tokens_1])
+    leaving_1 = [chip_share(keep_1, received_1, s, chunk_rows, ()) for s in range(1, chips)]
+    arrived_1 = [from_chip(part, -s - 1) for s, part in enumerate(leaving_1)]
+    every_0 = [cots_0] + far_0 + [from_core(part) for part in [cots_0] + far_0]
+    back_0 = token_backward(
+        every_0, width, gate_own, up_own, gate_turned, up_turned, leaving_1
+    )
+    *arrived_1, sent = after(arrived_1 + [back_0[1]], ())
+    received = from_core(sent)
+    hidden, cots_1 = cotangents(
+        keep_1, received_1, arrived_1, hidden_cotangent, 1, chunk_rows, [hidden_0], back_0[:1]
+    )
+    far_1 = [from_chip(cots_1, s) for s in range(1, chips)]
+
+    def leave(keep, received, count, deps):
+        rest = chunk_rows - count
+        outputs = [
+            [
+                ((0, 1), s * chunk_rows, count, p * own_features, own_features)
+                for s in range(chips)
+            ]
+            for p in range(tensor)
+        ]
+        if rest:
+            outputs += [[((0, 1), s * chunk_rows + count, rest, 0, width)] for s in range(chips)]
+        outs = added_cuts([keep, received], outputs, deps)
+        return outs[:tensor], outs[tensor:]
+
+    def over_tensor_first(stacks):
+        return [stacks[0]] + [from_tensor(stacks[p], -p) for p in range(1, tensor)]
+
+    def then_chips(stacks, count, deps):
+        every = tuple(range(len(stacks)))
+        outputs = [[(every, s * count, count, 0, own_features)] for s in range(chips)]
+        outs = added_cuts(stacks, outputs, deps)
+        return [outs[0]] + [from_chip(outs[s], -s) for s in range(1, chips)]
+
+    parts_0, _ = leave(back_0[0], received, chunk_rows, [cots_1])
+    crossing_0 = over_tensor_first(parts_0)
+    reached = reached_pairs(
+        mine, own_rows, width, gate_all, up_all, same_example, parts_0[:1]
+    )
+    partial = example_squares(reached, [cots_0, cots_1], member, ())
+    early = [p for p in range(1, tensor) if p != middle]
+    ordered = after(far_1 + [crossing_0[p] for p in early], [partial])
+    far_1 = list(ordered[: len(far_1)])
+    for p, array in zip(early, ordered[len(far_1) :], strict=True):
+        crossing_0[p] = array
+    every_1 = [cots_1] + far_1 + [from_core(part) for part in [cots_1] + far_1]
+    apart = [from_tensor(partial, p) for p in range(1, tensor)]
+    back_1 = token_backward(
+        every_1, width, gate_own, up_own, gate_turned, up_turned, apart
+    )
+    crossing_0[middle], sent, *apart = after([crossing_0[middle], back_1[1]] + apart, ())
+    squares = partial[0]
+    for array in apart:
+        squares = squares + array[0]
     threshold = clip_norm[0] * math.sqrt(D * FFW)
     factor = threshold / jnp.maximum(jnp.sqrt(squares), threshold)
     own_factor = jnp.sum(member * factor[None, :], axis=1)
-    near = [own_factor] + [from_chip(own_factor, s) for s in range(1, chips)]
-    every = near + [from_core(part) for part in near]
+    factors_near = [own_factor] + [
+        from_rank(own_factor, core, s) for core in range(CORES) for s in range(chips) if core or s
+    ]
+    received = from_core(sent)
+    final_0 = then_chips(crossing_0, chunk_rows, [sent])
     factors = jnp.concatenate(
         [
             part[chunk * chunk_rows : (chunk + 1) * chunk_rows]
             for chunk in range(CHUNKS)
-            for part in every
+            for part in factors_near
         ]
     )
     factors = jnp.broadcast_to(factors[:, None], (rows * CHUNKS, LANES))
 
-    token_parts = []
-    for chunk in range(CHUNKS):
-        keep, send = token_backward(
-            all_cots[chunk], width, gate_own, up_own, gate_weight, up_weight
-        )
-        received = from_core(send)
-
-        def share(p):
-            span = slice(p * own_features, (p + 1) * own_features)
-            return keep[:, span].astype(F32) + received[:, span].astype(F32)
-
-        held = share(tensor - 1)
-        for p in range(tensor - 2, -1, -1):
-            held = share(p) + from_tensor(held.astype(BF16), -1).astype(F32)
-        total = held[:chunk_rows]
-        for s in range(1, chips):
-            part = held[s * chunk_rows : (s + 1) * chunk_rows].astype(BF16)
-            total = total + from_chip(part, -s).astype(F32)
-        token_parts.append(total.astype(BF16))
+    parts_1, rest_1 = leave(back_1[0], received, first_rows, [final_0[0], factors])
+    crossing_1 = over_tensor_first(parts_1)
+    over_chips = [rest_1[0]] + [from_chip(rest_1[s], -s) for s in range(1, chips)]
+    rest = chunk_rows - first_rows
 
     gate_grad, up_grad = weight_gradients(
-        turned, [part for cots in all_cots for part in cots], factors, gate_own, up_own
-    )
-    hidden = jnp.concatenate(hidden_parts, axis=0)
-    token_grad = jnp.concatenate(token_parts, axis=0)
+        [tokens_0, tokens_1], every_0 + every_1, factors, gate_own, up_own, [parts_1[0]]
+    )
+    every = tuple(range(chips))
+    shares = added_cuts(
+        over_chips,
+        [[(every, 0, rest, p * own_features, own_features)] for p in range(tensor)],
+        [gate_grad],
+    )
+    late = [shares[0]] + [from_tensor(shares[p], -p) for p in range(1, tensor)]
+    final_1 = then_chips(crossing_1, first_rows, [gate_grad])
+    parts, cuts = [], []
+    for arrays, count in ((final_0, chunk_rows), (final_1, first_rows), (late, rest)):
+        places = tuple(range(len(parts), len(parts) + len(arrays)))
+        parts += arrays
+        cuts.append((places, 0, count, 0, own_features))
+    (token_grad,) = added_cuts(parts, [cuts], [gate_grad])
     return (hidden, gate_grad, up_grad, token_grad)
 
 

time: 410 us -> 320 us (0.78)
  waiting for transfers between devices: 194 us -> 60.8 us
  Pallas kernels: 149 us -> 178 us
  starting transfers between devices: 36.7 us -> 49.8 us
  other arithmetic: 17 us -> 4.19 us
  local copies, waits for them, and re-layouts: 11 us -> 23.5 us
    ppermute x9 -> x12, waiting for transfers between devices: 98.5 us -> 22.9 us  [from_chip(): return lax.ppermute(value, 'fsdp', pairs)]
    ppermute x15 -> x18, waiting for transfers between devices: 92.8 us -> 37.8 us  [from_tensor(): lax.ppermute(value, 'tensor', [(i, (i + back) % tensor) for i in range(te...]
    pallas_call x0 -> x22, Pallas kernels: none -> 50 us  [the longest x2 18.9 us: turned_weight(): pl.pallas_call(kernel, out_shape=jax.ShapeDtypeStruct((width, depth), BF1...]
    unnamed x52 -> x98, local copies, waits for them, and re-layouts: 5.07 us -> 19.5 us
    pallas_call x2, Pallas kernels: 48.5 us -> 35.1 us  [token_backward(): pl.pallas_call(kernel, out_shape=(out, out), grid_spec=pltpu.PrefetchScal...]
    ppermute x15 -> x18, starting transfers between devices: 19.8 us -> 31.6 us  [from_tensor(): lax.ppermute(value, 'tensor', [(i, (i + back) % tensor) for i in range(te...]
    convert_element_type x10 -> x0, other arithmetic: 8.92 us -> none  [the longest x6 8.41 us: shards(): held = share(p) + from_tensor(held.astype(BF16), -1).astype(F32)]
    pallas_call x1, Pallas kernels: 25.8 us -> 18.4 us  [reached_pairs(): pl.pallas_call(kernel, out_shape=jax.ShapeDtypeStruct((2, blocks, rows, r...]
  transfers between devices with their start and end apart: 42 -> 53, of which waited for: 22 -> 12; matrix products, arithmetic and copies ran while one was open for 5% -> 3% of each run, Pallas kernels for 36% -> 54%
where the time goes in v2:
time: 320 us; the launch traced here: 318 us
  Pallas kernels  178 us (56%)
  waiting for transfers between devices  60.8 us (19%)
  starting transfers between devices  49.8 us (16%)
  local copies, waits for them, and re-layouts  23.5 us (7%)
  other arithmetic  4.19 us (1%)
    ppermute x18, waiting for transfers between devices, from_tensor(): lax.ppermute(value, 'tensor', [(i, (i + back) % tensor) for i in range(te...  37.8 us
    pallas_call x2, Pallas kernels, token_backward(): pl.pallas_call(kernel, out_shape=(out, out), grid_spec=pltpu.PrefetchScal...  35.1 us
    pallas_call x2, Pallas kernels, forward(): pl.pallas_call(kernel, out_shape=(out, out), grid_spec=pltpu.PrefetchScal...  32.3 us
    ppermute x18, starting transfers between devices, from_tensor(): lax.ppermute(value, 'tensor', [(i, (i + back) % tensor) for i in range(te...  31.6 us
    ppermute x12, waiting for transfers between devices, from_chip(): return lax.ppermute(value, 'fsdp', pairs)  22.9 us
    pallas_call x1, Pallas kernels, weight_gradients(): pl.pallas_call(kernel, out_shape=(out, out), grid_spec=pltpu.PrefetchScal...  22.8 us
    unnamed x98, local copies, waits for them, and re-layouts  19.5 us
    pallas_call x2, Pallas kernels, turned_weight(): pl.pallas_call(kernel, out_shape=jax.ShapeDtypeStruct((width, depth), BF1...  18.9 us
  transfers between devices with their start and end apart: 53, of which 12 were waited for; matrix products, arithmetic and copies ran while one was open for 3% of the time, Pallas kernels for 54%

profile of v2, /device:TPU:0, one launch (start us, length us, event | category | flops | bytes accessed | tf_op | source)
XLA Modules:
  0.0 318.3 jit_solution(14730507427091547481)
XLA Ops:
  0.6 1.8 rows_of.1
  2.5 3.0 collective-permute-start.1
  5.5 2.6 collective-permute-start.2
  8.1 1.3 collective-permute-start.3
  9.4 1.5 collective-permute-start
  11.5 3.5 %collective-permute-done.1.refs_1_.refs_4_ = bf16[64,2048]{1,0:T(8,128)(2,1)S(1)} collective-permute-done((bf16[64,2048]{1,0:T(8,128)(2,1)}, bf16[64,2048]{1,0:T(8,128)(2,1)S(1)}, u32[]{:S(2)}, u32[]{:S(2)}) %collective-permute-start.1) | collective-permute-done | bytes 262176 | tf_op jit(solution)/shard_map/ppermute | solution.py:602
  15.0 10.4 %collective-permute-done.2.refs_2_.refs_8_ = bf16[64,2048]{1,0:T(8,128)(2,1)S(1)} collective-permute-done((bf16[64,2048]{1,0:T(8,128)(2,1)}, bf16[64,2048]{1,0:T(8,128)(2,1)S(1)}, u32[]{:S(2)}, u32[]{:S(2)}) %collective-permute-start.2) | collective-permute-done | bytes 262176 | tf_op jit(solution)/shard_map/ppermute | solution.py:602
  25.4 1.5 collective-permute-start.12
  27.7 1.5 collective-permute-start.9
  30.0 14.8 %collective-permute-done.9.refs_6_ = bf16[64,2048]{1,0:T(8,128)(2,1)S(1)} collective-permute-done((bf16[64,2048]{1,0:T(8,128)(2,1)S(1)}, bf16[64,2048]{1,0:T(8,128)(2,1)S(1)}, u32[]{:S(2)}, u32[]{:S(2)}) %collective-permute-start.9) | collective-permute-done | bytes 262176 | tf_op jit(solution)/shard_map/ppermute | solution.py:589
  47.2 1.8 pad_maximum_fusion.refs_0_
  49.0 3.5 %collective-permute-start.17 = (bf16[128,2048]{1,0:T(8,128)(2,1)}, bf16[128,2048]{1,0:T(8,128)(2,1)S(1)}, u32[]{:S(2)}, u32[]{:S(2)}) collective-permute-start(bf16[128,2048]{1,0:T(8,128)(2,1)} %after.9.refs_18_.refs_0_.refs_4_), channel_id=1, source_target_pairs={{0,1},{1,2},{2,3},{3,0},{4,5},{5,6},{6,7},{7,4},{8,9},{9,10},{10,1... | collective-permute-start | bytes 1572872 | tf_op jit(solution)/shard_map/ppermute | solution.py:602
  52.6 16.2 %forward.2 = (bf16[2,128,3584]{2,1,0:T(8,128)(2,1)}, bf16[2,128,3584]{2,1,0:T(8,128)(2,1)}) custom-call(s32[224]{0:T(256)} %reshape.33.gk, s32[224]{0:T(256)} %reshape.34.uk, bf16[64,2048]{1,0:T(8,128)(2,1)} %get-tuple-element.55.refs_0_, bf16[64,2048]{1,0:T(8,128)(2,1)} %copy-done.27, bf16[64,2048]{1,0:T(8,128)(2,1)} %copy-done.26, ...), custom_call_target="tpu_custom_call" | custom-call | flops 7516192768 | bytes 18874368 | tf_op jit(solution)/shard_map/forward/pallas_call | solution.py:92
  70.0 3.2 %collective-permute-start.21 = (bf16[128,2048]{1,0:T(8,128)(2,1)S(1)}, bf16[128,2048]{1,0:T(8,128)(2,1)S(1)}, u32[]{:S(2)}, u32[]{:S(2)}) collective-permute-start(bf16[128,2048]{1,0:T(8,128)(2,1)S(1)} %copy-done.3), channel_id=1, source_target_pairs={{0,3},{1,0},{2,1},{3,2},{4,7},{5,4},{6,5},{7,6},{8,11},{9,8},{10,9... | collective-permute-start | bytes 1572872 | tf_op jit(solution)/shard_map/ppermute | solution.py:602
  73.2 9.5 %turned_weight.2.refs_2_.refs_4_ = bf16[3584,1024]{1,0:T(8,128)(2,1)} custom-call(bf16[1024,3584]{1,0:T(8,128)(2,1)} %refs_8_.1, bf16[2,128,3584]{2,1,0:T(8,128)(2,1)} %get-tuple-element.59.refs_0_), custom_call_target="tpu_custom_call" | custom-call | bytes 14680064 | tf_op jit(solution)/shard_map/turned_weight/pallas_call | solution.py:169
  82.7 2.3 collective-permute-done.21.refs_1_
  85.8 1.3 copy-done
  87.1 2.4 chip_share.2.refs_0_
  89.5 1.5 collective-permute-start.24
  91.0 2.3 collective-permute-start.19
  93.7 9.5 %turned_weight.3.refs_16_.refs_5_ = bf16[3584,1024]{1,0:T(8,128)(2,1)} custom-call(bf16[1024,3584]{1,0:T(8,128)(2,1)} %refs_9_.1, bf16[2,64,3584]{2,1,0:T(8,128)(2,1)} %chip_share.2.refs_0_), custom_call_target="tpu_custom_call" | custom-call | bytes 14680064 | tf_op jit(solution)/shard_map/turned_weight/pallas_call | solution.py:169
  103.2 6.5 %transposed.2.refs_1_.refs_0_ = bf16[8192,256]{1,0:T(8,128)(2,1)} custom-call(bf16[64,2048]{1,0:T(8,128)(2,1)} %get-tuple-element.55.refs_0_, bf16[64,2048]{1,0:T(8,128)(2,1)} %copy-done.27, bf16[64,2048]{1,0:T(8,128)(2,1)} %copy-done.26, bf16[64,2048]{1,0:T(8,128)(2,1)} %collective-permute-done.7.refs_3_, bf16[64,2048]{1,0:T(8,128)(2,1)} %copy-done.10, ...), custom_call_target="tpu_custom_call" | custom-call | bytes 8388608 | tf_op jit(solution)/shard_map/transposed/pallas_call | solution.py:195
  109.8 6.5 %collective-permute-done.19.refs_0_ = bf16[128,2048]{1,0:T(8,128)(2,1)S(1)} collective-permute-done((bf16[128,2048]{1,0:T(8,128)(2,1)S(1)}, bf16[128,2048]{1,0:T(8,128)(2,1)S(1)}, u32[]{:S(2)}, u32[]{:S(2)}) %collective-permute-start.19) | collective-permute-done | bytes 524320 | tf_op jit(solution)/shard_map/ppermute | solution.py:602
  116.2 0.8 copy-done.2
  117.6 0.9 copy-done.20
  118.5 4.2 %cotangents.2 = (bf16[128,3584]{1,0:T(8,128)(2,1)}, bf16[2,64,3584]{2,1,0:T(8,128)(2,1)}) custom-call(bf16[2,128,3584]{2,1,0:T(8,128)(2,1)} %get-tuple-element.58.a, bf16[2,128,3584]{2,1,0:T(8,128)(2,1)} %get-tuple-element.60.b, bf16[2,64,3584]{2,1,0:T(8,128)(2,1)} %copy-done.20, bf16[128,3584]{1,0:T(8,128)(2,1)} %refs_1_.3, ...), custom_call_target="tpu_custom_call" | custom-call | flops 4587520 | bytes 4587520 | tf_op jit(solution)/shard_map/cotangents/pallas_call | solution.py:259
  125.2 16.1 %forward.3 = (bf16[2,128,3584]{2,1,0:T(8,128)(2,1)}, bf16[2,128,3584]{2,1,0:T(8,128)(2,1)}) custom-call(s32[224]{0:T(256)} %reshape.33.gk, s32[224]{0:T(256)} %reshape.34.uk, bf16[128,2048]{1,0:T(8,128)(2,1)} %after.9.refs_18_.refs_0_.refs_4_, bf16[128,2048]{1,0:T(8,128)(2,1)} %copy-done.22, bf16[128,2048]{1,0:T(8,128)(2,1)} %get-tuple-element.57.refs_2_.refs_5_, ...), custom_call_target="tpu_custom_call" | custom-call | flops 7516192768 | bytes 18874368 | tf_op jit(solution)/shard_map/forward/pallas_call | solution.py:92
  141.3 3.9 %collective-permute-done.25.refs_0_ = bf16[2,64,3584]{2,1,0:T(8,128)(2,1)S(1)} collective-permute-done((bf16[2,64,3584]{2,1,0:T(8,128)(2,1)}, bf16[2,64,3584]{2,1,0:T(8,128)(2,1)S(1)}, u32[]{:S(2)}, u32[]{:S(2)}) %collective-permute-start.25) | collective-permute-done | bytes 917536 | tf_op jit(solution)/shard_map/ppermute | solution.py:589
  145.2 1.0 copy-done.21
  146.2 1.2 copy-done.18
  147.9 6.5 %transposed.3.refs_1_ = bf16[8192,256]{1,0:T(8,128)(2,1)} custom-call(bf16[128,2048]{1,0:T(8,128)(2,1)} %after.9.refs_18_.refs_0_.refs_4_, bf16[128,2048]{1,0:T(8,128)(2,1)} %copy-done.22, bf16[128,2048]{1,0:T(8,128)(2,1)} %get-tuple-element.57.refs_2_.refs_5_, bf16[128,2048]{1,0:T(8,128)(2,1)} %collective-permute-done.18.refs_3_, ...), custom_call_target="tpu_custom_call" | custom-call | bytes 8388608 | tf_op jit(solution)/shard_map/transposed/pallas_call | solution.py:195
  154.4 1.2 copy-done.1
  155.6 2.3 chip_share.3.refs_6_
  158.6 17.6 %token_backward.2 = (bf16[128,8192]{1,0:T(8,128)(2,1)}, bf16[128,8192]{1,0:T(8,128)(2,1)}) custom-call(s32[224]{0:T(256)} %reshape.33.gk, s32[224]{0:T(256)} %reshape.34.uk, bf16[2,64,3584]{2,1,0:T(8,128)(2,1)} %get-tuple-element.62.refs_10_.refs_0_.refs_2_, bf16[2,64,3584]{2,1,0:T(8,128)(2,1)} %get-tuple-element.66.refs_1_.refs_3_, ...), custom_call_target="tpu_custom_call" | custom-call | flops 7516192768 | bytes 18874368 | tf_op jit(solution)/shard_map/token_backward/pallas_call | solution.py:436
  176.2 4.2 %collective-permute-done.27.refs_0_ = bf16[2,64,3584]{2,1,0:T(8,128)(2,1)S(1)} collective-permute-done((bf16[2,64,3584]{2,1,0:T(8,128)(2,1)}, bf16[2,64,3584]{2,1,0:T(8,128)(2,1)S(1)}, u32[]{:S(2)}, u32[]{:S(2)}) %collective-permute-start.27) | collective-permute-done | bytes 917536 | tf_op jit(solution)/shard_map/ppermute | solution.py:589
  180.5 0.9 copy-done.8
  181.4 4.3 %cotangents.3 = (bf16[128,3584]{1,0:T(8,128)(2,1)}, bf16[2,64,3584]{2,1,0:T(8,128)(2,1)}) custom-call(bf16[2,128,3584]{2,1,0:T(8,128)(2,1)} %get-tuple-element.63.refs_2_.a, bf16[2,128,3584]{2,1,0:T(8,128)(2,1)} %after.14.b, bf16[2,64,3584]{2,1,0:T(8,128)(2,1)} %get-tuple-element.68.refs_0_, ...), custom_call_target="tpu_custom_call", output_to_operand_aliasing={{0}: (4, {})} | custom-call | flops 4587520 | bytes 4587520 | tf_op jit(solution)/shard_map/cotangents/pallas_call | solution.py:259
  186.4 1.4 copy-done.14
  187.8 3.7 %added_cuts.6 = (bf16[128,2048]{1,0:T(8,128)(2,1)}, bf16[128,2048]{1,0:T(8,128)(2,1)}, bf16[128,2048]{1,0:T(8,128)(2,1)}, bf16[128,2048]{1,0:T(8,128)(2,1)}) custom-call(bf16[128,8192]{1,0:T(8,128)(2,1)} %get-tuple-element.70.refs_3_.refs_0_, bf16[128,8192]{1,0:T(8,128)(2,1)} %copy-done.14, bf16[2,64,3584]{2,1,0:T(8,128)(2,1)} %get-tuple-element.72.refs_2_.refs_1_.refs_0_.refs_6_), custom_call_target="tpu_custom_call" | custom-call | flops 2097152 | bytes 8388608 | tf_op jit(solution)/shard_map/added_cuts/pallas_call | solution.py:476
  191.4 2.8 collective-permute-start.32
  196.4 18.4 %reached_pairs.1.refs_2_ = f32[2,28,128,128]{3,2,1,0:T(8,128)} custom-call(s32[896]{0:T(1024)} %reshape.35.gk, s32[896]{0:T(1024)} %reshape.36.uk, bf16[64,2048]{1,0:T(8,128)(2,1)} %get-tuple-element.55.refs_0_, bf16[64,2048]{1,0:T(8,128)(2,1)} %copy-done.10, bf16[64,2048]{1,0:T(8,128)(2,1)} %copy-done.11, bf16[64,2048]{1,0:T(8,128)(2,1)} %copy-done.12, ...), custom_call_target="tpu_custom_call" | custom-call | flops 29360128 | bytes 18350080 | tf_op jit(solution)/shard_map/reached_pairs/pallas_call | solution.py:311
  214.8 6.6 %example_squares.1.refs_3_ = f32[8,128]{1,0:T(8,128)} custom-call(bf16[2,64,3584]{2,1,0:T(8,128)(2,1)} %get-tuple-element.62.refs_10_.refs_0_.refs_2_, bf16[2,64,3584]{2,1,0:T(8,128)(2,1)} %get-tuple-element.72.refs_2_.refs_1_.refs_0_.refs_6_, f32[2,28,128,128]{3,2,1,0:T(8,128)} %reached_pairs.1.refs_2_, f32[128,128]{1,0:T(8,128)} %get-tuple-element.112.refs_3_), custom_call_target="tpu_custom_call" | custom-call | flops 469762048 | bytes 3670016 | tf_op jit(solution)/shard_map/example_squares/pallas_call | solution.py:376
  221.5 0.9 copy-done.19
  223.8 4.4 %collective-permute-start.38 = (f32[8,128]{1,0:T(8,128)}, f32[8,128]{1,0:T(8,128)S(1)}, u32[]{:S(2)}, u32[]{:S(2)}) collective-permute-start(f32[8,128]{1,0:T(8,128)} %example_squares.1.refs_3_), channel_id=1, source_target_pairs={{0,2},{1,3},{2,0},{3,1},{4,6},{5,7},{6,4},{7,5},{8,10},{9,11},{10,... | collective-permute-start | bytes 12296 | tf_op jit(solution)/shard_map/ppermute | solution.py:602
  228.2 1.5 collective-permute-start.36
  230.0 2.4 collective-permute-done.39.refs_8_.refs_4_
  233.0 1.0 copy-done.48
  234.0 17.6 %token_backward.3 = (bf16[128,8192]{1,0:T(8,128)(2,1)}, bf16[128,8192]{1,0:T(8,128)(2,1)}) custom-call(s32[224]{0:T(256)} %reshape.33.gk, s32[224]{0:T(256)} %reshape.34.uk, bf16[2,64,3584]{2,1,0:T(8,128)(2,1)} %get-tuple-element.72.refs_2_.refs_1_.refs_0_.refs_6_, bf16[2,64,3584]{2,1,0:T(8,128)(2,1)} %get-tuple-element.77.refs_1_.refs_7_, ...), custom_call_target="tpu_custom_call" | custom-call | flops 7516192768 | bytes 18874368 | tf_op jit(solution)/shard_map/token_backward/pallas_call | solution.py:436
  251.5 2.4 collective-permute-done.36.refs_0_
  256.2 1.6 collective-permute-start.42
  258.5 2.5 added_cuts.7
  261.0 1.5 collective-permute-start.44
  262.8 1.0 broadcast_in_dim.2.refs_3_.refs_10_
  264.2 3.6 %added_cuts.8 = (bf16[64,2048]{1,0:T(8,128)(2,1)}, bf16[64,2048]{1,0:T(8,128)(2,1)}, bf16[64,2048]{1,0:T(8,128)(2,1)}, bf16[64,2048]{1,0:T(8,128)(2,1)}, bf16[32...) custom-call(bf16[128,8192]{1,0:T(8,128)(2,1)} %get-tuple-element.83.refs_0_, bf16[128,8192]{1,0:T(8,128)(2,1)} %copy-done.13, ...), custom_call_target="tpu_custom_call" | custom-call | flops 2097152 | bytes 8388608 | tf_op jit(solution)/shard_map/added_cuts/pallas_call | solution.py:476
  268.3 1.5 collective-permute-start.45
  270.4 22.8 %weight_gradients.1 = (bf16[1024,3584]{1,0:T(8,128)(2,1)}, bf16[1024,3584]{1,0:T(8,128)(2,1)}) custom-call(s32[224]{0:T(256)} %reshape.33.gk, s32[224]{0:T(256)} %reshape.34.uk, bf16[8192,256]{1,0:T(8,128)(2,1)} %transposed.2.refs_1_.refs_0_, bf16[8192,256]{1,0:T(8,128)(2,1)} %transposed.3.refs_1_, ...), custom_call_target="tpu_custom_call" | custom-call | flops 15032385536 | bytes 23068672 | tf_op jit(solution)/shard_map/weight_gradients/pallas_call | solution.py:535
  294.2 2.0 added_cuts.9
  296.1 1.5 collective-permute-start.48
  298.4 2.0 added_cuts.10
  300.4 3.3 %collective-permute-start.50 = (bf16[32,2048]{1,0:T(8,128)(2,1)}, bf16[32,2048]{1,0:T(8,128)(2,1)S(1)}, u32[]{:S(2)}, u32[]{:S(2)}) collective-permute-start(bf16[32,2048]{1,0:T(8,128)(2,1)} %get-tuple-element.101), channel_id=1, source_target_pairs={{0,3},{1,0},{2,1},{3,2},{4,7},{5,4},{6,5},{7,6},{8,11},{9,8},{10,9... | collective-permute-start | bytes 393224 | tf_op jit(solution)/shard_map/ppermute | solution.py:602
  303.7 1.1 collective-permute-start.51
  305.3 2.6 collective-permute-done.50.refs_5_
  307.9 7.4 %collective-permute-done.51.refs_6_ = bf16[32,2048]{1,0:T(8,128)(2,1)S(1)} collective-permute-done((bf16[32,2048]{1,0:T(8,128)(2,1)}, bf16[32,2048]{1,0:T(8,128)(2,1)S(1)}, u32[]{:S(2)}, u32[]{:S(2)}) %collective-permute-start.51) | collective-permute-done | bytes 131104 | tf_op jit(solution)/shard_map/ppermute | solution.py:602
  316.1 2.3 added_cuts.11
  (188 shorter events, 23.4 us)
Async XLA Ops:
  2.5 12.5 %collective-permute-start.1 = (bf16[64,2048]{1,0:T(8,128)(2,1)}, bf16[64,2048]{1,0:T(8,128)(2,1)S(1)}, u32[]{:S(2)}, u32[]{:S(2)}) collective-permute-start(bf16[64,2048]{1,0:T(8,128)(2,1)} %get-tuple-element.55.refs_0_), channel_id=1, source_target_pairs={{0,1},{1,2},{2,3},{3,0},{4,5},{5,6},{6,7},{7,4},{8,9},{9,10},{10,1... | collective-permute-start | bytes 786440 | tf_op jit(solution)/shard_map/ppermute | solution.py:602
  5.5 19.9 %collective-permute-start.2 = (bf16[64,2048]{1,0:T(8,128)(2,1)}, bf16[64,2048]{1,0:T(8,128)(2,1)S(1)}, u32[]{:S(2)}, u32[]{:S(2)}) collective-permute-start(bf16[64,2048]{1,0:T(8,128)(2,1)} %get-tuple-element.55.refs_0_), channel_id=1, source_target_pairs={{0,2},{1,3},{2,0},{3,1},{4,6},{5,7},{6,4},{7,5},{8,10},{9,11},{10,... | collective-permute-start | bytes 786440 | tf_op jit(solution)/shard_map/ppermute | solution.py:602
  8.1 18.8 %collective-permute-start.3 = (bf16[64,2048]{1,0:T(8,128)(2,1)}, bf16[64,2048]{1,0:T(8,128)(2,1)S(1)}, u32[]{:S(2)}, u32[]{:S(2)}) collective-permute-start(bf16[64,2048]{1,0:T(8,128)(2,1)} %get-tuple-element.55.refs_0_), channel_id=1, source_target_pairs={{0,3},{1,0},{2,1},{3,2},{4,7},{5,4},{6,5},{7,6},{8,11},{9,8},{10,9... | collective-permute-start | bytes 786440 | tf_op jit(solution)/shard_map/ppermute | solution.py:602
  9.4 17.5 %collective-permute-start = (bf16[64,2048]{1,0:T(8,128)(2,1)}, bf16[64,2048]{1,0:T(8,128)(2,1)S(1)}, u32[]{:S(2)}, u32[]{:S(2)}) collective-permute-start(bf16[64,2048]{1,0:T(8,128)(2,1)} %get-tuple-element.54), channel_id=1, source_target_pairs={{0,8},{4,12},{8,0},{12,4},{1,9},{5,13},{9,1},{13,5},{2,10},{6,14},... | collective-permute-start | bytes 786440 | tf_op jit(solution)/shard_map/ppermute | solution.py:589
  10.9 16.6 %collective-permute-start.6 = (bf16[64,2048]{1,0:T(8,128)(2,1)}, bf16[64,2048]{1,0:T(8,128)(2,1)S(1)}, u32[]{:S(2)}, u32[]{:S(2)}) collective-permute-start(bf16[64,2048]{1,0:T(8,128)(2,1)} %get-tuple-element.55.refs_0_), channel_id=1, source_target_pairs={{0,8},{4,12},{8,0},{12,4},{1,9},{5,13},{9,1},{13,5},{2,10},{6,14},... | collective-permute-start | bytes 786440 | tf_op jit(solution)/shard_map/ppermute | solution.py:589
  15.0 33.9 %copy-start.10 = (bf16[64,2048]{1,0:T(8,128)(2,1)}, bf16[64,2048]{1,0:T(8,128)(2,1)S(1)}, u32[]{:S(2)}) copy-start(bf16[64,2048]{1,0:T(8,128)(2,1)S(1)} %collective-permute-done.1.refs_1_.refs_4_) | copy-start | bytes 786436
  15.0 12.7 %collective-permute-start.5 = (bf16[64,2048]{1,0:T(8,128)(2,1)}, bf16[64,2048]{1,0:T(8,128)(2,1)S(1)}, u32[]{:S(2)}, u32[]{:S(2)}) collective-permute-start(bf16[64,2048]{1,0:T(8,128)(2,1)} %get-tuple-element.55.refs_0_), channel_id=1, source_target_pairs={{0,4},{4,0},{8,12},{12,8},{1,5},{5,1},{9,13},{13,9},{2,6},{6,2},{1... | collective-permute-start | bytes 786440 | tf_op jit(solution)/shard_map/ppermute | solution.py:592
  25.4 23.5 %copy-start.11 = (bf16[64,2048]{1,0:T(8,128)(2,1)}, bf16[64,2048]{1,0:T(8,128)(2,1)S(1)}, u32[]{:S(2)}) copy-start(bf16[64,2048]{1,0:T(8,128)(2,1)S(1)} %collective-permute-done.2.refs_2_.refs_8_) | copy-start | bytes 786436
  25.4 19.4 %collective-permute-start.12 = (bf16[64,2048]{1,0:T(8,128)(2,1)S(1)}, bf16[64,2048]{1,0:T(8,128)(2,1)S(1)}, u32[]{:S(2)}, u32[]{:S(2)}) collective-permute-start(bf16[64,2048]{1,0:T(8,128)(2,1)S(1)} %collective-permute-done.2.refs_2_.refs_8_), channel_id=1, source_target_pairs={{0,8},{4,12},{8,0},{12,4},{1,9},{5,13},{9,1},{13,5},{2,10},{6,14},... | collective-permute-start | bytes 786440 | tf_op jit(solution)/shard_map/ppermute | solution.py:589
  26.9 22.0 %copy-start.12 = (bf16[64,2048]{1,0:T(8,128)(2,1)}, bf16[64,2048]{1,0:T(8,128)(2,1)S(1)}, u32[]{:S(2)}) copy-start(bf16[64,2048]{1,0:T(8,128)(2,1)S(1)} %collective-permute-done.3.refs_3_.refs_12_) | copy-start | bytes 786436
  26.9 18.5 %collective-permute-start.11 = (bf16[64,2048]{1,0:T(8,128)(2,1)S(1)}, bf16[64,2048]{1,0:T(8,128)(2,1)S(1)}, u32[]{:S(2)}, u32[]{:S(2)}) collective-permute-start(bf16[64,2048]{1,0:T(8,128)(2,1)S(1)} %collective-permute-done.2.refs_2_.refs_8_), channel_id=1, source_target_pairs={{0,4},{4,0},{8,12},{12,8},{1,5},{5,1},{9,13},{13,9},{2,6},{6,2},{1... | collective-permute-start | bytes 786440 | tf_op jit(solution)/shard_map/ppermute | solution.py:592
  26.9 18.4 %collective-permute-start.15 = (bf16[64,2048]{1,0:T(8,128)(2,1)S(1)}, bf16[64,2048]{1,0:T(8,128)(2,1)S(1)}, u32[]{:S(2)}, u32[]{:S(2)}) collective-permute-start(bf16[64,2048]{1,0:T(8,128)(2,1)S(1)} %collective-permute-done.3.refs_3_.refs_12_), channel_id=1, source_target_pairs={{0,8},{4,12},{8,0},{12,4},{1,9},{5,13},{9,1},{13,5},{2,10},{6,14},... | collective-permute-start | bytes 786440 | tf_op jit(solution)/shard_map/ppermute | solution.py:589
  27.5 25.0 %copy-start.26 = (bf16[64,2048]{1,0:T(8,128)(2,1)}, bf16[64,2048]{1,0:T(8,128)(2,1)S(1)}, u32[]{:S(2)}) copy-start(bf16[64,2048]{1,0:T(8,128)(2,1)S(1)} %collective-permute-done.6.refs_2_) | copy-start | bytes 786436
  27.5 18.3 %collective-permute-start.14 = (bf16[64,2048]{1,0:T(8,128)(2,1)S(1)}, bf16[64,2048]{1,0:T(8,128)(2,1)S(1)}, u32[]{:S(2)}, u32[]{:S(2)}) collective-permute-start(bf16[64,2048]{1,0:T(8,128)(2,1)S(1)} %collective-permute-done.3.refs_3_.refs_12_), channel_id=1, source_target_pairs={{0,4},{4,0},{8,12},{12,8},{1,5},{5,1},{9,13},{13,9},{2,6},{6,2},{1... | collective-permute-start | bytes 786440 | tf_op jit(solution)/shard_map/ppermute | solution.py:592
  27.7 24.8 %copy-start.27 = (bf16[64,2048]{1,0:T(8,128)(2,1)}, bf16[64,2048]{1,0:T(8,128)(2,1)S(1)}, u32[]{:S(2)}) copy-start(bf16[64,2048]{1,0:T(8,128)(2,1)S(1)} %collective-permute-done.5.refs_1_) | copy-start | bytes 786436
  27.7 17.1 %collective-permute-start.9 = (bf16[64,2048]{1,0:T(8,128)(2,1)S(1)}, bf16[64,2048]{1,0:T(8,128)(2,1)S(1)}, u32[]{:S(2)}, u32[]{:S(2)}) collective-permute-start(bf16[64,2048]{1,0:T(8,128)(2,1)S(1)} %collective-permute-done.1.refs_1_.refs_4_), channel_id=1, source_target_pairs={{0,8},{4,12},{8,0},{12,4},{1,9},{5,13},{9,1},{13,5},{2,10},{6,14},... | collective-permute-start | bytes 786440 | tf_op jit(solution)/shard_map/ppermute | solution.py:589
  30.0 38.8 %copy-start.42 = (s32[32,28]{1,0:T(8,128)}, s32[32,28]{1,0:T(8,128)S(1)}, u32[]{:S(2)}) copy-start(s32[32,28]{1,0:T(8,128)S(1)} %get-tuple-element.114) | copy-start | bytes 10756
  44.8 4.2 %collective-permute-start.8 = (bf16[64,2048]{1,0:T(8,128)(2,1)S(1)}, bf16[64,2048]{1,0:T(8,128)(2,1)S(1)}, u32[]{:S(2)}, u32[]{:S(2)}) collective-permute-start(bf16[64,2048]{1,0:T(8,128)(2,1)S(1)} %collective-permute-done.1.refs_1_.refs_4_), channel_id=1, source_target_pairs={{0,4},{4,0},{8,12},{12,8},{1,5},{5,1},{9,13},{13,9},{2,6},{6,2},{1... | collective-permute-start | bytes 786440 | tf_op jit(solution)/shard_map/ppermute | solution.py:592
  44.8 7.7 %collective-permute-start.7 = (bf16[64,2048]{1,0:T(8,128)(2,1)S(1)}, bf16[64,2048]{1,0:T(8,128)(2,1)}, u32[]{:S(2)}, u32[]{:S(2)}) collective-permute-start(bf16[64,2048]{1,0:T(8,128)(2,1)S(1)} %collective-permute-done.6.refs_2_), channel_id=1, source_target_pairs={{0,4},{4,0},{8,12},{12,8},{1,5},{5,1},{9,13},{13,9},{2,6},{6,2},{1... | collective-permute-start | bytes 786440 | tf_op jit(solution)/shard_map/ppermute | solution.py:592
  45.3 7.2 %collective-permute-start.10 = (bf16[64,2048]{1,0:T(8,128)(2,1)S(1)}, bf16[64,2048]{1,0:T(8,128)(2,1)}, u32[]{:S(2)}, u32[]{:S(2)}) collective-permute-start(bf16[64,2048]{1,0:T(8,128)(2,1)S(1)} %collective-permute-done.9.refs_6_), channel_id=1, source_target_pairs={{0,4},{4,0},{8,12},{12,8},{1,5},{5,1},{9,13},{13,9},{2,6},{6,2},{1... | collective-permute-start | bytes 786440 | tf_op jit(solution)/shard_map/ppermute | solution.py:592
  45.4 7.1 %collective-permute-start.13 = (bf16[64,2048]{1,0:T(8,128)(2,1)S(1)}, bf16[64,2048]{1,0:T(8,128)(2,1)}, u32[]{:S(2)}, u32[]{:S(2)}) collective-permute-start(bf16[64,2048]{1,0:T(8,128)(2,1)S(1)} %collective-permute-done.12.refs_10_), channel_id=1, source_target_pairs={{0,4},{4,0},{8,12},{12,8},{1,5},{5,1},{9,13},{13,9},{2,6},{6,2},{1... | collective-permute-start | bytes 786440 | tf_op jit(solution)/shard_map/ppermute | solution.py:592
  45.8 6.7 %collective-permute-start.16 = (bf16[64,2048]{1,0:T(8,128)(2,1)S(1)}, bf16[64,2048]{1,0:T(8,128)(2,1)}, u32[]{:S(2)}, u32[]{:S(2)}) collective-permute-start(bf16[64,2048]{1,0:T(8,128)(2,1)S(1)} %collective-permute-done.15.refs_14_), channel_id=1, source_target_pairs={{0,4},{4,0},{8,12},{12,8},{1,5},{5,1},{9,13},{13,9},{2,6},{6,2},{1... | collective-permute-start | bytes 786440 | tf_op jit(solution)/shard_map/ppermute | solution.py:592
  49.0 19.8 %collective-permute-start.17 = (bf16[128,2048]{1,0:T(8,128)(2,1)}, bf16[128,2048]{1,0:T(8,128)(2,1)S(1)}, u32[]{:S(2)}, u32[]{:S(2)}) collective-permute-start(bf16[128,2048]{1,0:T(8,128)(2,1)} %after.9.refs_18_.refs_0_.refs_4_), channel_id=1, source_target_pairs={{0,1},{1,2},{2,3},{3,0},{4,5},{5,6},{6,7},{7,4},{8,9},{9,10},{10,1... | collective-permute-start | bytes 1572872 | tf_op jit(solution)/shard_map/ppermute | solution.py:602
  69.6 15.4 %collective-permute-start.20 = (bf16[2,128,3584]{2,1,0:T(8,128)(2,1)}, bf16[2,128,3584]{2,1,0:T(8,128)(2,1)S(1)}, u32[]{:S(2)}, u32[]{:S(2)}) collective-permute-start(bf16[2,128,3584]{2,1,0:T(8,128)(2,1)} %get-tuple-element.59.refs_0_), channel_id=1, source_target_pairs={{0,4},{4,0},{8,12},{12,8},{1,5},{5,1},{9,13},{13,9},{2,6},{6,2},{1... | collective-permute-start | bytes 5505032 | tf_op jit(solution)/shard_map/ppermute | solution.py:592
  70.0 15.0 %collective-permute-start.21 = (bf16[128,2048]{1,0:T(8,128)(2,1)S(1)}, bf16[128,2048]{1,0:T(8,128)(2,1)S(1)}, u32[]{:S(2)}, u32[]{:S(2)}) collective-permute-start(bf16[128,2048]{1,0:T(8,128)(2,1)S(1)} %copy-done.3), channel_id=1, source_target_pairs={{0,3},{1,0},{2,1},{3,2},{4,7},{5,4},{6,5},{7,6},{8,11},{9,8},{10,9... | collective-permute-start | bytes 1572872 | tf_op jit(solution)/shard_map/ppermute | solution.py:602
  89.5 28.1 %collective-permute-start.24 = (bf16[2,64,3584]{2,1,0:T(8,128)(2,1)}, bf16[2,64,3584]{2,1,0:T(8,128)(2,1)S(1)}, u32[]{:S(2)}, u32[]{:S(2)}) collective-permute-start(bf16[2,64,3584]{2,1,0:T(8,128)(2,1)} %chip_share.2.refs_0_), channel_id=1, source_target_pairs={{0,8},{4,12},{8,0},{12,4},{1,9},{5,13},{9,1},{13,5},{2,10},{6,14},... | collective-permute-start | bytes 2752520 | tf_op jit(solution)/shard_map/ppermute | solution.py:589
  91.0 25.2 %collective-permute-start.19 = (bf16[128,2048]{1,0:T(8,128)(2,1)S(1)}, bf16[128,2048]{1,0:T(8,128)(2,1)S(1)}, u32[]{:S(2)}, u32[]{:S(2)}) collective-permute-start(bf16[128,2048]{1,0:T(8,128)(2,1)S(1)} %copy-done.3), channel_id=1, source_target_pairs={{0,2},{1,3},{2,0},{3,1},{4,6},{5,7},{6,4},{7,5},{8,10},{9,11},{10,... | collective-permute-start | bytes 1572872 | tf_op jit(solution)/shard_map/ppermute | solution.py:602
  93.2 30.2 %collective-permute-start.4 = (bf16[128,2048]{1,0:T(8,128)(2,1)S(1)}, bf16[128,2048]{1,0:T(8,128)(2,1)S(1)}, u32[]{:S(2)}, u32[]{:S(2)}) collective-permute-start(bf16[128,2048]{1,0:T(8,128)(2,1)S(1)} %copy-done.3), channel_id=1, source_target_pairs={{0,4},{4,0},{8,12},{12,8},{1,5},{5,1},{9,13},{13,9},{2,6},{6,2},{1... | collective-permute-start | bytes 1572872 | tf_op jit(solution)/shard_map/ppermute | solution.py:592
  93.2 30.2 %collective-permute-start.18 = (bf16[128,2048]{1,0:T(8,128)(2,1)S(1)}, bf16[128,2048]{1,0:T(8,128)(2,1)}, u32[]{:S(2)}, u32[]{:S(2)}) collective-permute-start(bf16[128,2048]{1,0:T(8,128)(2,1)S(1)} %copy-done.7), channel_id=1, source_target_pairs={{0,4},{4,0},{8,12},{12,8},{1,5},{5,1},{9,13},{13,9},{2,6},{6,2},{1... | collective-permute-start | bytes 1572872 | tf_op jit(solution)/shard_map/ppermute | solution.py:592
  117.1 6.4 %collective-permute-start.22 = (bf16[128,2048]{1,0:T(8,128)(2,1)}, bf16[128,2048]{1,0:T(8,128)(2,1)S(1)}, u32[]{:S(2)}, u32[]{:S(2)}) collective-permute-start(bf16[128,2048]{1,0:T(8,128)(2,1)} %after.12.refs_2_.refs_4_.refs_6_), channel_id=1, source_target_pairs={{0,4},{4,0},{8,12},{12,8},{1,5},{5,1},{9,13},{13,9},{2,6},{6,2},{1... | collective-permute-start | bytes 1572872 | tf_op jit(solution)/shard_map/ppermute | solution.py:592
  117.1 6.4 %collective-permute-start.23 = (bf16[128,2048]{1,0:T(8,128)(2,1)S(1)}, bf16[128,2048]{1,0:T(8,128)(2,1)S(1)}, u32[]{:S(2)}, u32[]{:S(2)}) collective-permute-start(bf16[128,2048]{1,0:T(8,128)(2,1)S(1)} %copy-done.5), channel_id=1, source_target_pairs={{0,4},{4,0},{8,12},{12,8},{1,5},{5,1},{9,13},{13,9},{2,6},{6,2},{1... | collective-permute-start | bytes 1572872 | tf_op jit(solution)/shard_map/ppermute | solution.py:592
  122.8 22.5 %collective-permute-start.25 = (bf16[2,64,3584]{2,1,0:T(8,128)(2,1)}, bf16[2,64,3584]{2,1,0:T(8,128)(2,1)S(1)}, u32[]{:S(2)}, u32[]{:S(2)}) collective-permute-start(bf16[2,64,3584]{2,1,0:T(8,128)(2,1)} %get-tuple-element.62.refs_10_.refs_0_.refs_2_), channel_id=1, source_target_pairs={{0,8},{4,12},{8,0},{12,4},{1,9},{5,13},{9,1},{13,5},{2,10},{6,14},... | collective-permute-start | bytes 2752520 | tf_op jit(solution)/shard_map/ppermute | solution.py:589
  146.2 8.2 %collective-permute-start.26 = (bf16[2,128,3584]{2,1,0:T(8,128)(2,1)}, bf16[2,128,3584]{2,1,0:T(8,128)(2,1)S(1)}, u32[]{:S(2)}, u32[]{:S(2)}) collective-permute-start(bf16[2,128,3584]{2,1,0:T(8,128)(2,1)} %get-tuple-element.65.refs_8_), channel_id=1, source_target_pairs={{0,4},{4,0},{8,12},{12,8},{1,5},{5,1},{9,13},{13,9},{2,6},{6,2},{1... | collective-permute-start | bytes 5505032 | tf_op jit(solution)/shard_map/ppermute | solution.py:592
  147.4 11.3 %collective-permute-start.28 = (bf16[2,64,3584]{2,1,0:T(8,128)(2,1)S(1)}, bf16[2,64,3584]{2,1,0:T(8,128)(2,1)}, u32[]{:S(2)}, u32[]{:S(2)}) collective-permute-start(bf16[2,64,3584]{2,1,0:T(8,128)(2,1)S(1)} %copy-done.18), channel_id=1, source_target_pairs={{0,4},{4,0},{8,12},{12,8},{1,5},{5,1},{9,13},{13,9},{2,6},{6,2},{1... | collective-permute-start | bytes 2752520 | tf_op jit(solution)/shard_map/ppermute | solution.py:592
  147.4 11.3 %collective-permute-start.29 = (bf16[2,64,3584]{2,1,0:T(8,128)(2,1)}, bf16[2,64,3584]{2,1,0:T(8,128)(2,1)}, u32[]{:S(2)}, u32[]{:S(2)}) collective-permute-start(bf16[2,64,3584]{2,1,0:T(8,128)(2,1)} %get-tuple-element.66.refs_1_.refs_3_), channel_id=1, source_target_pairs={{0,4},{4,0},{8,12},{12,8},{1,5},{5,1},{9,13},{13,9},{2,6},{6,2},{1... | collective-permute-start | bytes 2752520 | tf_op jit(solution)/shard_map/ppermute | solution.py:592
  158.0 22.5 %collective-permute-start.27 = (bf16[2,64,3584]{2,1,0:T(8,128)(2,1)}, bf16[2,64,3584]{2,1,0:T(8,128)(2,1)S(1)}, u32[]{:S(2)}, u32[]{:S(2)}) collective-permute-start(bf16[2,64,3584]{2,1,0:T(8,128)(2,1)} %chip_share.3.refs_6_), channel_id=1, source_target_pairs={{0,8},{4,12},{8,0},{12,4},{1,9},{5,13},{9,1},{13,5},{2,10},{6,14},... | collective-permute-start | bytes 2752520 | tf_op jit(solution)/shard_map/ppermute | solution.py:589
  181.4 5.0 %collective-permute-start.31 = (bf16[128,8192]{1,0:T(8,128)(2,1)}, bf16[128,8192]{1,0:T(8,128)(2,1)S(1)}, u32[]{:S(2)}, u32[]{:S(2)}) collective-permute-start(bf16[128,8192]{1,0:T(8,128)(2,1)} %get-tuple-element.73), channel_id=1, source_target_pairs={{0,4},{4,0},{8,12},{12,8},{1,5},{5,1},{9,13},{13,9},{2,6},{6,2},{1... | collective-permute-start | bytes 6291464 | tf_op jit(solution)/shard_map/ppermute | solution.py:592
  185.7 8.6 %copy-start.43 = (s32[32,28]{1,0:T(8,128)S(1)}, s32[32,28]{1,0:T(8,128)}, u32[]{:S(2)}) copy-start(s32[32,28]{1,0:T(8,128)} %copy-done.42) | copy-start | bytes 10756
  185.7 10.0 %copy-start.47 = (s32[128]{0:T(128)S(1)}, s32[128]{0:T(128)}, u32[]{:S(2)}) copy-start(s32[128]{0:T(128)} %param.14) | copy-start | bytes 1540
  185.7 10.7 %copy-start.9 = (bf16[2,64,3584]{2,1,0:T(8,128)(2,1)S(1)}, bf16[2,64,3584]{2,1,0:T(8,128)(2,1)}, u32[]{:S(2)}) copy-start(bf16[2,64,3584]{2,1,0:T(8,128)(2,1)} %get-tuple-element.72.refs_2_.refs_1_.refs_0_.refs_6_) | copy-start | bytes 2752516
  185.7 35.7 %collective-permute-start.30 = (bf16[2,64,3584]{2,1,0:T(8,128)(2,1)}, bf16[2,64,3584]{2,1,0:T(8,128)(2,1)S(1)}, u32[]{:S(2)}, u32[]{:S(2)}) collective-permute-start(bf16[2,64,3584]{2,1,0:T(8,128)(2,1)} %get-tuple-element.72.refs_2_.refs_1_.refs_0_.refs_6_), channel_id=1, source_target_pairs={{0,8},{4,12},{8,0},{12,4},{1,9},{5,13},{9,1},{13,5},{2,10},{6,14},... | collective-permute-start | bytes 2752520 | tf_op jit(solution)/shard_map/ppermute | solution.py:589
  191.4 30.0 %collective-permute-start.32 = (bf16[128,2048]{1,0:T(8,128)(2,1)}, bf16[128,2048]{1,0:T(8,128)(2,1)S(1)}, u32[]{:S(2)}, u32[]{:S(2)}) collective-permute-start(bf16[128,2048]{1,0:T(8,128)(2,1)} %get-tuple-element.74), channel_id=1, source_target_pairs={{0,3},{1,0},{2,1},{3,2},{4,7},{5,4},{6,5},{7,6},{8,11},{9,8},{10,9... | collective-permute-start | bytes 1572872 | tf_op jit(solution)/shard_map/ppermute | solution.py:602
  194.3 27.2 %collective-permute-start.33 = (bf16[128,2048]{1,0:T(8,128)(2,1)}, bf16[128,2048]{1,0:T(8,128)(2,1)S(1)}, u32[]{:S(2)}, u32[]{:S(2)}) collective-permute-start(bf16[128,2048]{1,0:T(8,128)(2,1)} %get-tuple-element.75), channel_id=1, source_target_pairs={{0,1},{1,2},{2,3},{3,0},{4,5},{5,6},{6,7},{7,4},{8,9},{9,10},{10,1... | collective-permute-start | bytes 1572872 | tf_op jit(solution)/shard_map/ppermute | solution.py:602
  196.4 31.8 %collective-permute-start.34 = (bf16[2,64,3584]{2,1,0:T(8,128)(2,1)S(1)}, bf16[2,64,3584]{2,1,0:T(8,128)(2,1)}, u32[]{:S(2)}, u32[]{:S(2)}) collective-permute-start(bf16[2,64,3584]{2,1,0:T(8,128)(2,1)S(1)} %copy-done.9), channel_id=1, source_target_pairs={{0,4},{4,0},{8,12},{12,8},{1,5},{5,1},{9,13},{13,9},{2,6},{6,2},{1... | collective-permute-start | bytes 2752520 | tf_op jit(solution)/shard_map/ppermute | solution.py:592
  223.3 9.1 %collective-permute-start.35 = (bf16[2,64,3584]{2,1,0:T(8,128)(2,1)}, bf16[2,64,3584]{2,1,0:T(8,128)(2,1)S(1)}, u32[]{:S(2)}, u32[]{:S(2)}) collective-permute-start(bf16[2,64,3584]{2,1,0:T(8,128)(2,1)} %get-tuple-element.77.refs_1_.refs_7_), channel_id=1, source_target_pairs={{0,4},{4,0},{8,12},{12,8},{1,5},{5,1},{9,13},{13,9},{2,6},{6,2},{1... | collective-permute-start | bytes 2752520 | tf_op jit(solution)/shard_map/ppermute | solution.py:592
  223.8 5.9 %collective-permute-start.37 = (f32[8,128]{1,0:T(8,128)}, f32[8,128]{1,0:T(8,128)S(1)}, u32[]{:S(2)}, u32[]{:S(2)}) collective-permute-start(f32[8,128]{1,0:T(8,128)} %example_squares.1.refs_3_), channel_id=1, source_target_pairs={{0,1},{1,2},{2,3},{3,0},{4,5},{5,6},{6,7},{7,4},{8,9},{9,10},{10,1... | collective-permute-start | bytes 12296 | tf_op jit(solution)/shard_map/ppermute | solution.py:602
  223.8 6.2 %collective-permute-start.38 = (f32[8,128]{1,0:T(8,128)}, f32[8,128]{1,0:T(8,128)S(1)}, u32[]{:S(2)}, u32[]{:S(2)}) collective-permute-start(f32[8,128]{1,0:T(8,128)} %example_squares.1.refs_3_), channel_id=1, source_target_pairs={{0,2},{1,3},{2,0},{3,1},{4,6},{5,7},{6,4},{7,5},{8,10},{9,11},{10,... | collective-permute-start | bytes 12296 | tf_op jit(solution)/shard_map/ppermute | solution.py:602
  228.2 4.2 %collective-permute-start.39 = (f32[8,128]{1,0:T(8,128)}, f32[8,128]{1,0:T(8,128)S(1)}, u32[]{:S(2)}, u32[]{:S(2)}) collective-permute-start(f32[8,128]{1,0:T(8,128)} %example_squares.1.refs_3_), channel_id=1, source_target_pairs={{0,3},{1,0},{2,1},{3,2},{4,7},{5,4},{6,5},{7,6},{8,11},{9,8},{10,9... | collective-permute-start | bytes 12296 | tf_op jit(solution)/shard_map/ppermute | solution.py:602
  228.2 25.7 %collective-permute-start.36 = (bf16[128,2048]{1,0:T(8,128)(2,1)}, bf16[128,2048]{1,0:T(8,128)(2,1)S(1)}, u32[]{:S(2)}, u32[]{:S(2)}) collective-permute-start(bf16[128,2048]{1,0:T(8,128)(2,1)} %get-tuple-element.78), channel_id=1, source_target_pairs={{0,2},{1,3},{2,0},{3,1},{4,6},{5,7},{6,4},{7,5},{8,10},{9,11},{10,... | collective-permute-start | bytes 1572872 | tf_op jit(solution)/shard_map/ppermute | solution.py:602
  254.7 8.1 %collective-permute-start.43 = (bf16[128,8192]{1,0:T(8,128)(2,1)}, bf16[128,8192]{1,0:T(8,128)(2,1)S(1)}, u32[]{:S(2)}, u32[]{:S(2)}) collective-permute-start(bf16[128,8192]{1,0:T(8,128)(2,1)} %get-tuple-element.84.refs_4_), channel_id=1, source_target_pairs={{0,4},{4,0},{8,12},{12,8},{1,5},{5,1},{9,13},{13,9},{2,6},{6,2},{1... | collective-permute-start | bytes 6291464 | tf_op jit(solution)/shard_map/ppermute | solution.py:592
  256.2 6.2 %collective-permute-start.42 = (f32[128]{0:T(128)S(1)}, f32[128]{0:T(128)S(1)}, u32[]{:S(2)}, u32[]{:S(2)}) collective-permute-start(f32[128]{0:T(128)S(1)} %select_reduce_fusion), channel_id=1, source_target_pairs={{0,12},{4,8},{8,4},{12,0},{1,13},{5,9},{9,5},{13,1},{2,14},{6,10},... | collective-permute-start | bytes 1544 | tf_op jit(solution)/shard_map/ppermute | solution.py:599
  257.9 4.7 %collective-permute-start.41 = (f32[128]{0:T(128)S(1)}, f32[128]{0:T(128)S(1)}, u32[]{:S(2)}, u32[]{:S(2)}) collective-permute-start(f32[128]{0:T(128)S(1)} %select_reduce_fusion), channel_id=1, source_target_pairs={{0,4},{4,0},{8,12},{12,8},{1,5},{5,1},{9,13},{13,9},{2,6},{6,2},{1... | collective-permute-start | bytes 1544 | tf_op jit(solution)/shard_map/ppermute | solution.py:599
  257.9 4.7 %collective-permute-start.40 = (f32[128]{0:T(128)S(1)}, f32[128]{0:T(128)S(1)}, u32[]{:S(2)}, u32[]{:S(2)}) collective-permute-start(f32[128]{0:T(128)S(1)} %select_reduce_fusion), channel_id=1, source_target_pairs={{0,8},{4,12},{8,0},{12,4},{1,9},{5,13},{9,1},{13,5},{2,10},{6,14},... | collective-permute-start | bytes 1544 | tf_op jit(solution)/shard_map/ppermute | solution.py:599
  261.0 44.3 %collective-permute-start.44 = (bf16[64,2048]{1,0:T(8,128)(2,1)}, bf16[64,2048]{1,0:T(8,128)(2,1)S(1)}, u32[]{:S(2)}, u32[]{:S(2)}) collective-permute-start(bf16[64,2048]{1,0:T(8,128)(2,1)} %get-tuple-element.92), channel_id=1, source_target_pairs={{0,8},{4,12},{8,0},{12,4},{1,9},{5,13},{9,1},{13,5},{2,10},{6,14},... | collective-permute-start | bytes 786440 | tf_op jit(solution)/shard_map/ppermute | solution.py:589
  267.8 29.8 %collective-permute-start.49 = (bf16[32,8192]{1,0:T(8,128)(2,1)}, bf16[32,8192]{1,0:T(8,128)(2,1)S(1)}, u32[]{:S(2)}, u32[]{:S(2)}) collective-permute-start(bf16[32,8192]{1,0:T(8,128)(2,1)} %get-tuple-element.99), channel_id=1, source_target_pairs={{0,8},{4,12},{8,0},{12,4},{1,9},{5,13},{9,1},{13,5},{2,10},{6,14},... | collective-permute-start | bytes 1572872 | tf_op jit(solution)/shard_map/ppermute | solution.py:589
  268.3 24.9 %collective-permute-start.45 = (bf16[64,2048]{1,0:T(8,128)(2,1)}, bf16[64,2048]{1,0:T(8,128)(2,1)S(1)}, u32[]{:S(2)}, u32[]{:S(2)}) collective-permute-start(bf16[64,2048]{1,0:T(8,128)(2,1)} %get-tuple-element.93), channel_id=1, source_target_pairs={{0,3},{1,0},{2,1},{3,2},{4,7},{5,4},{6,5},{7,6},{8,11},{9,8},{10,9... | collective-permute-start | bytes 786440 | tf_op jit(solution)/shard_map/ppermute | solution.py:602
  269.9 23.4 %collective-permute-start.46 = (bf16[64,2048]{1,0:T(8,128)(2,1)}, bf16[64,2048]{1,0:T(8,128)(2,1)S(1)}, u32[]{:S(2)}, u32[]{:S(2)}) collective-permute-start(bf16[64,2048]{1,0:T(8,128)(2,1)} %get-tuple-element.94), channel_id=1, source_target_pairs={{0,2},{1,3},{2,0},{3,1},{4,6},{5,7},{6,4},{7,5},{8,10},{9,11},{10,... | collective-permute-start | bytes 786440 | tf_op jit(solution)/shard_map/ppermute | solution.py:602
  269.9 23.4 %collective-permute-start.47 = (bf16[64,2048]{1,0:T(8,128)(2,1)}, bf16[64,2048]{1,0:T(8,128)(2,1)S(1)}, u32[]{:S(2)}, u32[]{:S(2)}) collective-permute-start(bf16[64,2048]{1,0:T(8,128)(2,1)} %get-tuple-element.95), channel_id=1, source_target_pairs={{0,1},{1,2},{2,3},{3,0},{4,5},{5,6},{6,7},{7,4},{8,9},{9,10},{10,1... | collective-permute-start | bytes 786440 | tf_op jit(solution)/shard_map/ppermute | solution.py:602
  296.1 9.2 %collective-permute-start.48 = (bf16[32,2048]{1,0:T(8,128)(2,1)}, bf16[32,2048]{1,0:T(8,128)(2,1)S(1)}, u32[]{:S(2)}, u32[]{:S(2)}) collective-permute-start(bf16[32,2048]{1,0:T(8,128)(2,1)} %get-tuple-element.97), channel_id=1, source_target_pairs={{0,8},{4,12},{8,0},{12,4},{1,9},{5,13},{9,1},{13,5},{2,10},{6,14},... | collective-permute-start | bytes 393224 | tf_op jit(solution)/shard_map/ppermute | solution.py:589
  300.4 7.5 %collective-permute-start.50 = (bf16[32,2048]{1,0:T(8,128)(2,1)}, bf16[32,2048]{1,0:T(8,128)(2,1)S(1)}, u32[]{:S(2)}, u32[]{:S(2)}) collective-permute-start(bf16[32,2048]{1,0:T(8,128)(2,1)} %get-tuple-element.101), channel_id=1, source_target_pairs={{0,3},{1,0},{2,1},{3,2},{4,7},{5,4},{6,5},{7,6},{8,11},{9,8},{10,9... | collective-permute-start | bytes 393224 | tf_op jit(solution)/shard_map/ppermute | solution.py:602
  303.7 11.7 %collective-permute-start.51 = (bf16[32,2048]{1,0:T(8,128)(2,1)}, bf16[32,2048]{1,0:T(8,128)(2,1)S(1)}, u32[]{:S(2)}, u32[]{:S(2)}) collective-permute-start(bf16[32,2048]{1,0:T(8,128)(2,1)} %get-tuple-element.102), channel_id=1, source_target_pairs={{0,2},{1,3},{2,0},{3,1},{4,6},{5,7},{6,4},{7,5},{8,10},{9,11},{10,... | collective-permute-start | bytes 393224 | tf_op jit(solution)/shard_map/ppermute | solution.py:602
  304.8 10.6 %collective-permute-start.52 = (bf16[32,2048]{1,0:T(8,128)(2,1)}, bf16[32,2048]{1,0:T(8,128)(2,1)S(1)}, u32[]{:S(2)}, u32[]{:S(2)}) collective-permute-start(bf16[32,2048]{1,0:T(8,128)(2,1)} %get-tuple-element.103), channel_id=1, source_target_pairs={{0,1},{1,2},{2,3},{3,0},{4,5},{5,6},{6,7},{7,4},{8,9},{9,10},{10,1... | collective-permute-start | bytes 393224 | tf_op jit(solution)/shard_map/ppermute | solution.py:602
  305.3 10.0 %copy-start.34 = (bf16[64,2048]{1,0:T(8,128)(2,1)}, bf16[64,2048]{1,0:T(8,128)(2,1)S(1)}, u32[]{:S(2)}) copy-start(bf16[64,2048]{1,0:T(8,128)(2,1)S(1)} %collective-permute-done.44.refs_1_) | copy-start | bytes 786436
  305.3 10.0 %copy-start.38 = (bf16[32,2048]{1,0:T(8,128)(2,1)}, bf16[32,2048]{1,0:T(8,128)(2,1)S(1)}, u32[]{:S(2)}) copy-start(bf16[32,2048]{1,0:T(8,128)(2,1)S(1)} %collective-permute-done.48.refs_3_) | copy-start | bytes 393220
  (38 other events, 91.6 us)

commit v3 on v2

--- a/solution.py
+++ b/solution.py
@@ -14,17 +14,17 @@
 LANES = 128
 CORES = 2
 CHUNKS = 2
-VMEM = 56 * 1024 * 1024
+MIB = 1024 * 1024
 BF16 = jnp.bfloat16
 F32 = jnp.float32
 
 
 def column_group(blocks):
-    return max(n for n in (1, 2, 3, 4) if blocks % n == 0)
-
-
-def params():
-    return pltpu.CompilerParams(vmem_limit_bytes=VMEM, dimension_semantics=("arbitrary",))
+    return max(n for n in range(1, 8) if blocks % n == 0)
+
+
+def params(held):
+    return pltpu.CompilerParams(vmem_limit_bytes=held + 6 * MIB)
 
 
 def block_at(index):
@@ -57,6 +57,17 @@
             copy.start()
         for copy in copies:
             copy.wait()
+
+
+MARK = jax.ShapeDtypeStruct((8, LANES), F32)
+
+
+def mark_spec():
+    return pl.BlockSpec((8, LANES), lambda *_: (0, 0))
+
+
+def mark(ref):
+    ref[...] = jnp.zeros(ref.shape, ref.dtype)
 
 
 def waits(deps):
@@ -102,7 +113,7 @@
                 pltpu.SemaphoreType.DMA((copy_count(pieces),)),
             ],
         ),
-        compiler_params=params(),
+        compiler_params=params(50 * MIB),
         cost_estimate=pl.CostEstimate(
             flops=8 * rows * depth * blocks * BLK,
             bytes_accessed=4 * depth * blocks * BLK + 2 * rows * width,
@@ -119,21 +130,21 @@
     )
 
 
-def after(arrays, deps):
+def after(arrays, deps, marked=False):
     arrays = list(arrays)
 
     def kernel(*refs):
-        pass
-
-    return pl.pallas_call(
-        kernel,
-        out_shape=[jax.ShapeDtypeStruct(array.shape, array.dtype) for array in arrays],
+        mark(refs[-1])
+
+    return pl.pallas_call(
+        kernel,
+        out_shape=[jax.ShapeDtypeStruct(array.shape, array.dtype) for array in arrays] + [MARK],
         in_specs=waits(arrays) + waits(deps),
-        out_specs=waits(arrays),
+        out_specs=waits(arrays) + [pl.BlockSpec(memory_space=pltpu.VMEM)],
         input_output_aliases={n: n for n in range(len(arrays))},
         cost_estimate=pl.CostEstimate(flops=0, bytes_accessed=0, transcendentals=0),
         name="after",
-    )(*arrays, *deps)
+    )(*arrays, *deps)[: None if marked else len(arrays)]
 
 
 def rows_of(array, spans, deps):
@@ -148,7 +159,7 @@
         out_shape=[jax.ShapeDtypeStruct((count, width), array.dtype) for _, count in spans],
         in_specs=[pl.BlockSpec(memory_space=pltpu.VMEM)] + waits(deps),
         out_specs=[pl.BlockSpec(memory_space=pltpu.VMEM)] * len(spans),
-        compiler_params=pltpu.CompilerParams(vmem_limit_bytes=VMEM),
+        compiler_params=params(4 * MIB),
         cost_estimate=pl.CostEstimate(
             flops=0, bytes_accessed=4 * array.shape[0] * width, transcendentals=0
         ),
@@ -161,18 +172,19 @@
     group = column_group(width // BLK)
 
     def kernel(source, *refs):
-        out = refs[len(deps)]
+        out, done = refs[len(deps) :]
+        mark(done)
         for j in range(group):
             cols = slice(j * BLK, (j + 1) * BLK)
             out[cols, :] = source[:, cols].T
 
     return pl.pallas_call(
         kernel,
-        out_shape=jax.ShapeDtypeStruct((width, depth), BF16),
+        out_shape=(jax.ShapeDtypeStruct((width, depth), BF16), MARK),
         grid=(width // BLK // group,),
         in_specs=[pl.BlockSpec((depth, group * BLK), lambda i: (0, i))] + waits(deps),
-        out_specs=pl.BlockSpec((group * BLK, depth), lambda i: (i, 0)),
-        compiler_params=params(),
+        out_specs=(pl.BlockSpec((group * BLK, depth), lambda i: (i, 0)), mark_spec()),
+        compiler_params=params(50 * MIB),
         cost_estimate=pl.CostEstimate(
             flops=0, bytes_accessed=4 * depth * width, transcendentals=0
         ),
@@ -186,7 +198,8 @@
 
     def kernel(*refs):
         token_refs = refs[:count]
-        out, held, sems = refs[count + len(deps) :]
+        out, done, held, sems = refs[count + len(deps) :]
+        mark(done)
         load_pieces(pieces, token_refs, held, sems)
         step = pl.program_id(0)
         for j in range(step_cols // BLK):
@@ -194,15 +207,15 @@
 
     return pl.pallas_call(
         kernel,
-        out_shape=jax.ShapeDtypeStruct((width, rows), BF16),
+        out_shape=(jax.ShapeDtypeStruct((width, rows), BF16), MARK),
         grid=(width // step_cols,),
         in_specs=[pl.BlockSpec(memory_space=pl.ANY)] * count + waits(deps),
-        out_specs=pl.BlockSpec((step_cols, rows), lambda i: (i, 0)),
+        out_specs=(pl.BlockSpec((step_cols, rows), lambda i: (i, 0)), mark_spec()),
         scratch_shapes=[
             pltpu.VMEM((rows, width), BF16),
             pltpu.SemaphoreType.DMA((copy_count(pieces),)),
         ],
-        compiler_params=params(),
+        compiler_params=params(50 * MIB),
         cost_estimate=pl.CostEstimate(
             flops=0, bytes_accessed=4 * rows * width, transcendentals=0
         ),
@@ -223,7 +236,7 @@
         grid=(2,),
         in_specs=[spec, spec] + waits(deps),
         out_specs=pl.BlockSpec((1, chunk_rows, width), lambda i: (i, 0, 0)),
-        compiler_params=params(),
+        compiler_params=params(12 * chunk_rows * width),
         cost_estimate=pl.CostEstimate(
             flops=2 * chunk_rows * width, bytes_accessed=12 * chunk_rows * width, transcendentals=0
         ),
@@ -233,13 +246,14 @@
 
 def cotangents(keep, received, arrived, incoming, chunk, chunk_rows, before, deps):
     width = keep.shape[2]
-    cols = max(n for n in range(1, 8) if width // BLK % n == 0) * BLK
+    cols = column_group(width // BLK) * BLK
     unread = list(before) + list(deps)
 
     def kernel(a, b, *refs):
         others = refs[: len(arrived)]
         cot_in = refs[len(arrived)]
-        hidden, cots = refs[len(arrived) + 1 + len(unread) :]
+        hidden, cots, done = refs[len(arrived) + 1 + len(unread) :]
+        mark(done)
         sums = []
         for proj in range(2):
             total = a[proj].astype(F32) + b[proj].astype(F32)
@@ -261,14 +275,15 @@
         out_shape=(
             jax.ShapeDtypeStruct(incoming.shape, BF16),
             jax.ShapeDtypeStruct((2, chunk_rows, width), BF16),
+            MARK,
         ),
         grid=(width // cols,),
         in_specs=[both] * (2 + len(arrived))
         + [pl.BlockSpec((chunk_rows, cols), lambda i: (chunk, i))]
         + waits(unread),
-        out_specs=(pl.BlockSpec((chunk_rows, cols), lambda i: (chunk, i)), both),
+        out_specs=(pl.BlockSpec((chunk_rows, cols), lambda i: (chunk, i)), both, mark_spec()),
         input_output_aliases={3 + len(arrived) + n: n for n in range(len(before))},
-        compiler_params=params(),
+        compiler_params=params(24 * (3 + len(arrived)) * chunk_rows * cols),
         cost_estimate=pl.CostEstimate(
             flops=20 * chunk_rows * width,
             bytes_accessed=20 * chunk_rows * width,
@@ -280,13 +295,15 @@
 
 def reached_pairs(pieces, rows, width, gate_kept, up_kept, same_example, deps):
     keep, blocks = gate_kept.shape
+    group = column_group(blocks)
     row_blocks = width // BLK
     count = len(pieces)
 
     def kernel(gk, uk, *refs):
         token_refs = refs[:count]
         same = refs[count]
-        out, held, pairs, sems = refs[count + 1 + len(deps) :]
+        out, done, held, pairs, sems = refs[count + 1 + len(deps) :]
+        mark(done)
         load_pieces(pieces, token_refs, held, sems)
         step = pl.program_id(0)
 
@@ -302,29 +319,34 @@
 
             lax.fori_loop(0, row_blocks // 8, some, 0)
 
-        for proj, kept in enumerate((gk, uk)):
-            total = pairs[kept[step]]
-            for k in range(1, keep):
-                total = total + pairs[kept[k * blocks + step]]
-            out[proj, 0] = total * same[...]
-
-    return pl.pallas_call(
-        kernel,
-        out_shape=jax.ShapeDtypeStruct((2, blocks, rows, rows), F32),
+        for j in range(group):
+            for proj, kept in enumerate((gk, uk)):
+                column = step * group + j
+                total = pairs[kept[column]]
+                for k in range(1, keep):
+                    total = total + pairs[kept[k * blocks + column]]
+                out[proj, j] = total * same[...]
+
+    return pl.pallas_call(
+        kernel,
+        out_shape=(jax.ShapeDtypeStruct((2, blocks, rows, rows), F32), MARK),
         grid_spec=pltpu.PrefetchScalarGridSpec(
             num_scalar_prefetch=2,
-            grid=(blocks,),
+            grid=(blocks // group,),
             in_specs=[pl.BlockSpec(memory_space=pl.ANY)] * count
             + [pl.BlockSpec((rows, rows), lambda i, *_: (0, 0))]
             + waits(deps),
-            out_specs=pl.BlockSpec((2, 1, rows, rows), lambda i, *_: (0, i, 0, 0)),
+            out_specs=(
+                pl.BlockSpec((2, group, rows, rows), lambda i, *_: (0, i, 0, 0)),
+                mark_spec(),
+            ),
             scratch_shapes=[
                 pltpu.VMEM((rows, width), BF16),
                 pltpu.VMEM((row_blocks, rows, rows), F32),
                 pltpu.SemaphoreType.DMA((copy_count(pieces),)),
             ],
         ),
-        compiler_params=params(),
+        compiler_params=params(50 * MIB),
         cost_estimate=pl.CostEstimate(
             flops=2 * keep * blocks * rows * rows,
             bytes_accessed=40 * blocks * rows * rows,
@@ -385,7 +407,7 @@
         + waits(deps),
         out_specs=pl.BlockSpec((8, LANES), lambda i: (0, 0)),
         scratch_shapes=[pltpu.VMEM((rows, rows), F32)],
-        compiler_params=params(),
+        compiler_params=params((16 * group + 8) * rows * rows + 8 * rows * group * BLK),
         cost_estimate=pl.CostEstimate(
             flops=8 * blocks * rows * rows * BLK,
             bytes_accessed=8 * blocks * rows * rows,
@@ -407,7 +429,8 @@
     def kernel(gk, uk, *refs):
         cot_refs = refs[:count]
         wg, wu = refs[count : count + 2]
-        keep, send, total = refs[count + 2 + len(deps) :]
+        keep, send, done, total = refs[count + 2 + len(deps) :]
+        mark(done)
         step = pl.program_id(0)
 
         @pl.when(step == 0)
@@ -435,7 +458,7 @@
     out_spec = pl.BlockSpec((half, width), lambda i, *_: (0, 0))
     return pl.pallas_call(
         kernel,
-        out_shape=(out, out),
+        out_shape=(out, out, MARK),
         grid_spec=pltpu.PrefetchScalarGridSpec(
             num_scalar_prefetch=2,
             grid=(blocks // group,),
@@ -445,10 +468,10 @@
             * count
             + [weight_spec] * 2
             + waits(deps),
-            out_specs=(out_spec, out_spec),
+            out_specs=(out_spec, out_spec, mark_spec()),
             scratch_shapes=[pltpu.VMEM((width // BLK, rows, BLK), F32)],
         ),
-        compiler_params=params(),
+        compiler_params=params(50 * MIB),
         cost_estimate=pl.CostEstimate(
             flops=8 * rows * depth * blocks * BLK,
             bytes_accessed=4 * depth * blocks * BLK + 2 * rows * width,
@@ -462,7 +485,9 @@
     count = len(arrays)
 
     def kernel(*refs):
-        for cuts, out in zip(outputs, refs[count + len(deps) :], strict=True):
+        *outs, done = refs[count + len(deps) :]
+        mark(done)
+        for cuts, out in zip(outputs, outs, strict=True):
             target = 0
             for which, row, rows, col, cols in cuts:
                 at = (slice(row, row + rows), slice(col, col + cols))
@@ -478,10 +503,11 @@
         out_shape=[
             jax.ShapeDtypeStruct((sum(cut[2] for cut in cuts), cuts[0][4]), BF16)
             for cuts in outputs
-        ],
+        ]
+        + [MARK],
         in_specs=[pl.BlockSpec(memory_space=pltpu.VMEM)] * count + waits(deps),
-        out_specs=[pl.BlockSpec(memory_space=pltpu.VMEM)] * len(outputs),
-        compiler_params=pltpu.CompilerParams(vmem_limit_bytes=VMEM),
+        out_specs=[pl.BlockSpec(memory_space=pltpu.VMEM)] * (len(outputs) + 1),
+        compiler_params=params(4 * MIB),
         cost_estimate=pl.CostEstimate(flops=size, bytes_accessed=4 * size, transcendentals=0),
         name="added_cuts",
     )(*arrays, *deps)
@@ -502,7 +528,8 @@
         token_refs = refs[:chunks]
         cot_refs = refs[chunks : chunks + len(cots)]
         factor = refs[chunks + len(cots)]
-        gate_out, up_out = refs[chunks + len(cots) + 1 + len(deps) :]
+        gate_out, up_out, done = refs[chunks + len(cots) + 1 + len(deps) :]
+        mark(done)
         step = pl.program_id(0)
         for j in range(group):
             cols = slice(j * BLK, (j + 1) * BLK)
@@ -534,7 +561,7 @@
     operands = [gate_own.reshape(-1), up_own.reshape(-1), *turned, *cots, factors]
     return pl.pallas_call(
         kernel,
-        out_shape=(out, out),
+        out_shape=(out, out, MARK),
         grid_spec=pltpu.PrefetchScalarGridSpec(
             num_scalar_prefetch=2,
             grid=(steps,),
@@ -546,9 +573,9 @@
             * len(cots)
             + [pl.BlockSpec((rows * chunks, LANES), lambda i, *_: (0, 0))]
             + waits(deps),
-            out_specs=(out_spec, out_spec),
-        ),
-        compiler_params=params(),
+            out_specs=(out_spec, out_spec, mark_spec()),
+        ),
+        compiler_params=params(55 * MIB),
         cost_estimate=pl.CostEstimate(
             flops=8 * rows * chunks * depth * steps * group * BLK,
             bytes_accessed=4 * depth * steps * group * BLK + 2 * rows * chunks * width,
@@ -620,49 +647,66 @@
     part_0, part_1 = rows_of(tokens, [(0, chunk_rows), (chunk_rows, chunk_rows)], ())
     along = [part_0] + [from_tensor(part_0, p) for p in range(1, tensor)]
     stack = jnp.concatenate([part_1] + [from_chip(part_1, s) for s in range(1, chips)], axis=0)
-    (stack,) = after([stack], along[1:])
+    moved = {0: [from_chip(part_0, s) for s in range(1, chips)]}
+    last = 0
+    for p in sorted(range(1, tensor), key=lambda p: min(p, tensor - p)):
+        along[p], stack, *moved[last] = after([along[p], stack] + moved[last], ())
+        moved[p] = [from_chip(along[p], s) for s in range(1, chips)]
+        last = p
     pieces_0, mine = [], []
     for p in range(tensor):
         mine.append((along[p], [(0, chunk_rows, 0)], p * own_features))
-        for s in range(chips):
-            array = along[p] if s == 0 else from_chip(along[p], s)
+        for s, array in enumerate([along[p]] + moved[p]):
             pieces_0 += [piece(array, 0, s, p), piece(from_core(array), 1, s, p)]
     middle = tensor // 2
-    others = [p for p in range(1, tensor) if p != middle]
-    first, second = others[: len(others) // 2], others[len(others) // 2 :]
-    direct = {0: stack} | {p: from_tensor(stack, p) for p in range(1, tensor)}
+    ring = [stack]
+
+    def step_on():
+        return [from_tensor(ring[-1], 1)] if len(ring) < tensor else []
+
+    def arrive(moving, arrays, deps):
+        if moving + arrays:
+            moving = after(moving + arrays, deps)
+            ring.extend(moving[: len(moving) - len(arrays)])
+        return moving[len(moving) - len(arrays) :]
+
+    moving = step_on()
     keep_0, send_0 = forward(
         pieces_0, rows, width, gate_own, up_own, gate_weight, up_weight, [stack]
     )
-    send_0, *done = after([send_0] + [direct[p] for p in first], ())
-    direct.update(zip(first, done, strict=True))
+    (send_0,) = arrive(moving, [send_0], ())
+    moving = step_on()
     received_0 = from_core(send_0)
-    gate_turned = turned_weight(gate_weight, [send_0])
-    received_0, *done = after([received_0] + [direct[p] for p in second], [gate_turned])
-    direct.update(zip(second, done, strict=True))
-    leaving_0 = [chip_share(keep_0, received_0, s, chunk_rows, ()) for s in range(1, chips)]
-    up_turned = turned_weight(up_weight, leaving_0)
-    tokens_0 = transposed(pieces_0, rows, width, [up_turned])
-    (direct[middle],) = after([direct[middle]], [tokens_0])
-    direct = [direct[p] for p in range(tensor)]
+    gate_turned, gate_done = turned_weight(gate_weight, [send_0])
+    arrive(moving, [], [gate_done])
+    moving = step_on()
+    leaving_0 = [
+        chip_share(keep_0, received_0, s, chunk_rows, [gate_done]) for s in range(1, chips)
+    ]
+    up_turned, up_done = turned_weight(up_weight, leaving_0)
+    arrive(moving, [], [up_done])
+    while len(ring) < tensor:
+        ring += step_on()
+    tokens_0, tokens_0_done = transposed(pieces_0, rows, width, [up_done, ring[-1]])
     arrived_0 = [from_chip(part, -s - 1) for s, part in enumerate(leaving_0)]
     pieces_1 = []
-    for p, array in enumerate(direct):
+    for p, array in enumerate(ring):
         mine.append((array, [(0, chunk_rows, chunk_rows)], p * own_features))
         pieces_1 += [piece(array, 0, 0, p), piece(from_core(array), 1, 0, p)]
 
-    hidden_0, cots_0 = cotangents(
-        keep_0, received_0, arrived_0, hidden_cotangent, 0, chunk_rows, (), [direct[middle]]
+    hidden_0, cots_0, cots_0_done = cotangents(
+        keep_0, received_0, arrived_0, hidden_cotangent, 0, chunk_rows, (), [tokens_0_done]
     )
     far_0 = [from_chip(cots_0, s) for s in range(1, chips)]
     keep_1, send_1 = forward(
-        pieces_1, rows, width, gate_own, up_own, gate_weight, up_weight, [cots_0]
+        pieces_1, rows, width, gate_own, up_own, gate_weight, up_weight, [cots_0_done]
     )
     *far_0, send_1 = after(far_0 + [send_1], [keep_1])
     received_1 = from_core(send_1)
-    tokens_1 = transposed(pieces_1, rows, width, [send_1])
-    (received_1,) = after([received_1], [tokens_1])
-    leaving_1 = [chip_share(keep_1, received_1, s, chunk_rows, ()) for s in range(1, chips)]
+    tokens_1, tokens_1_done = transposed(pieces_1, rows, width, [send_1])
+    leaving_1 = [
+        chip_share(keep_1, received_1, s, chunk_rows, [tokens_1_done]) for s in range(1, chips)
+    ]
     arrived_1 = [from_chip(part, -s - 1) for s, part in enumerate(leaving_1)]
     every_0 = [cots_0] + far_0 + [from_core(part) for part in [cots_0] + far_0]
     back_0 = token_backward(
@@ -670,8 +714,8 @@
     )
     *arrived_1, sent = after(arrived_1 + [back_0[1]], ())
     received = from_core(sent)
-    hidden, cots_1 = cotangents(
-        keep_1, received_1, arrived_1, hidden_cotangent, 1, chunk_rows, [hidden_0], back_0[:1]
+    hidden, cots_1, cots_1_done = cotangents(
+        keep_1, received_1, arrived_1, hidden_cotangent, 1, chunk_rows, [hidden_0], [back_0[2]]
     )
     far_1 = [from_chip(cots_1, s) for s in range(1, chips)]
 
@@ -687,7 +731,7 @@
         if rest:
             outputs += [[((0, 1), s * chunk_rows + count, rest, 0, width)] for s in range(chips)]
         outs = added_cuts([keep, received], outputs, deps)
-        return outs[:tensor], outs[tensor:]
+        return outs[:tensor], outs[tensor:-1], outs[-1]
 
     def over_tensor_first(stacks):
         return [stacks[0]] + [from_tensor(stacks[p], -p) for p in range(1, tensor)]
@@ -696,23 +740,25 @@
         every = tuple(range(len(stacks)))
         outputs = [[(every, s * count, count, 0, own_features)] for s in range(chips)]
         outs = added_cuts(stacks, outputs, deps)
-        return [outs[0]] + [from_chip(outs[s], -s) for s in range(1, chips)]
-
-    parts_0, _ = leave(back_0[0], received, chunk_rows, [cots_1])
+        return [outs[0]] + [from_chip(outs[s], -s) for s in range(1, chips)], outs[-1]
+
+    parts_0, _, parts_0_done = leave(back_0[0], received, chunk_rows, [cots_1_done])
     crossing_0 = over_tensor_first(parts_0)
-    reached = reached_pairs(
-        mine, own_rows, width, gate_all, up_all, same_example, parts_0[:1]
-    )
-    partial = example_squares(reached, [cots_0, cots_1], member, ())
+    reached, reached_done = reached_pairs(
+        mine, own_rows, width, gate_all, up_all, same_example, [parts_0_done]
+    )
     early = [p for p in range(1, tensor) if p != middle]
-    ordered = after(far_1 + [crossing_0[p] for p in early], [partial])
+    *ordered, ordered_done = after(
+        far_1 + [crossing_0[p] for p in early], [reached_done], marked=True
+    )
     far_1 = list(ordered[: len(far_1)])
     for p, array in zip(early, ordered[len(far_1) :], strict=True):
         crossing_0[p] = array
     every_1 = [cots_1] + far_1 + [from_core(part) for part in [cots_1] + far_1]
+    partial = example_squares(reached, [cots_0, cots_1], member, [ordered_done])
     apart = [from_tensor(partial, p) for p in range(1, tensor)]
     back_1 = token_backward(
-        every_1, width, gate_own, up_own, gate_turned, up_turned, apart
+        every_1, width, gate_own, up_own, gate_turned, up_turned, [partial]
     )
     crossing_0[middle], sent, *apart = after([crossing_0[middle], back_1[1]] + apart, ())
     squares = partial[0]
@@ -725,7 +771,7 @@
         from_rank(own_factor, core, s) for core in range(CORES) for s in range(chips) if core or s
     ]
     received = from_core(sent)
-    final_0 = then_chips(crossing_0, chunk_rows, [sent])
+    final_0, final_0_done = then_chips(crossing_0, chunk_rows, [back_1[2]])
     factors = jnp.concatenate(
         [
             part[chunk * chunk_rows : (chunk + 1) * chunk_rows]
@@ -735,28 +781,28 @@
     )
     factors = jnp.broadcast_to(factors[:, None], (rows * CHUNKS, LANES))
 
-    parts_1, rest_1 = leave(back_1[0], received, first_rows, [final_0[0], factors])
+    parts_1, rest_1, parts_1_done = leave(back_1[0], received, first_rows, [final_0_done])
     crossing_1 = over_tensor_first(parts_1)
     over_chips = [rest_1[0]] + [from_chip(rest_1[s], -s) for s in range(1, chips)]
     rest = chunk_rows - first_rows
 
-    gate_grad, up_grad = weight_gradients(
-        [tokens_0, tokens_1], every_0 + every_1, factors, gate_own, up_own, [parts_1[0]]
+    gate_grad, up_grad, grads_done = weight_gradients(
+        [tokens_0, tokens_1], every_0 + every_1, factors, gate_own, up_own, [parts_1_done]
     )
     every = tuple(range(chips))
     shares = added_cuts(
         over_chips,
         [[(every, 0, rest, p * own_features, own_features)] for p in range(tensor)],
-        [gate_grad],
+        [grads_done],
     )
     late = [shares[0]] + [from_tensor(shares[p], -p) for p in range(1, tensor)]
-    final_1 = then_chips(crossing_1, first_rows, [gate_grad])
+    final_1, _ = then_chips(crossing_1, first_rows, [grads_done])
     parts, cuts = [], []
     for arrays, count in ((final_0, chunk_rows), (final_1, first_rows), (late, rest)):
         places = tuple(range(len(parts), len(parts) + len(arrays)))
         parts += arrays
         cuts.append((places, 0, count, 0, own_features))
-    (token_grad,) = added_cuts(parts, [cuts], [gate_grad])
+    token_grad, _ = added_cuts(parts, [cuts], [grads_done])
     return (hidden, gate_grad, up_grad, token_grad)
 
 

time: 320 us -> 289 us (0.903)
  Pallas kernels: 178 us -> 154 us
  waiting for transfers between devices: 60.8 us -> 55 us
  local copies, waits for them, and re-layouts: 23.5 us -> 27.3 us
    pallas_call x8, Pallas kernels: 108 us -> 97.7 us  [the longest x2 33.9 us: token_backward(): pl.pallas_call(kernel, out_shape=(out, out, MARK), grid_spec=pltpu.Prefet...]
    pallas_call x6, Pallas kernels: 16 us -> 6.35 us  [added_cuts(): pl.pallas_call(kernel, out_shape=[jax.ShapeDtypeStruct((sum((cut[2] for c...]
    pallas_call x9 -> x10, Pallas kernels: 0.01 us -> 5.92 us  [after(): pl.pallas_call(kernel, out_shape=[jax.ShapeDtypeStruct(array.shape, array...]
    ppermute x18, waiting for transfers between devices: 37.8 us -> 32.4 us  [from_tensor(): lax.ppermute(value, 'tensor', [(i, (i + back) % tensor) for i in range(te...]
    unnamed x98 -> x122, local copies, waits for them, and re-layouts: 19.5 us -> 23.4 us
    ppermute x18, starting transfers between devices: 31.6 us -> 28 us  [from_tensor(): lax.ppermute(value, 'tensor', [(i, (i + back) % tensor) for i in range(te...]
    pallas_call x2, Pallas kernels: 4.71 us -> 1.26 us  [chip_share(): pl.pallas_call(kernel, out_shape=jax.ShapeDtypeStruct((2, chunk_rows, wid...]
  transfers between devices with their start and end apart: 53 -> 53, of which waited for: 12 -> 15; matrix products, arithmetic and copies ran while one was open for 3% -> 2% of each run, Pallas kernels for 54% -> 52%
where the time goes in v3:
time: 289 us; the launch traced here: 288 us
  Pallas kernels  154 us (53%)
  waiting for transfers between devices  55 us (19%)
  starting transfers between devices  47.6 us (16%)
  local copies, waits for them, and re-layouts  27.3 us (9%)
    pallas_call x2, Pallas kernels, token_backward(): pl.pallas_call(kernel, out_shape=(out, out, MARK), grid_spec=pltpu.Prefet...  33.9 us
    ppermute x18, waiting for transfers between devices, from_tensor(): lax.ppermute(value, 'tensor', [(i, (i + back) % tensor) for i in range(te...  32.4 us
    pallas_call x2, Pallas kernels, forward(): pl.pallas_call(kernel, out_shape=(out, out), grid_spec=pltpu.PrefetchScal...  30.8 us
    ppermute x18, starting transfers between devices, from_tensor(): lax.ppermute(value, 'tensor', [(i, (i + back) % tensor) for i in range(te...  28 us
    unnamed x122, local copies, waits for them, and re-layouts  23.4 us
    pallas_call x1, Pallas kernels, weight_gradients(): pl.pallas_call(kernel, out_shape=(out, out, MARK), grid_spec=pltpu.Prefet...  23 us
    ppermute x12, waiting for transfers between devices, from_chip(): return lax.ppermute(value, 'fsdp', pairs)  22.5 us
    ppermute x12, starting transfers between devices, from_chip(): return lax.ppermute(value, 'fsdp', pairs)  14.6 us
  transfers between devices with their start and end apart: 53, of which 15 were waited for; matrix products, arithmetic and copies ran while one was open for 2% of the time, Pallas kernels for 52%

profile of v3, /device:TPU:0, one launch (start us, length us, event | category | flops | bytes accessed | tf_op | source)
XLA Modules:
  0.0 288.3 jit_solution(16615226573763113530)
XLA Ops:
  0.6 1.0 copy-done.18
  1.7 3.0 %collective-permute-start.3 = (bf16[64,2048]{1,0:T(8,128)(2,1)S(1)}, bf16[64,2048]{1,0:T(8,128)(2,1)S(1)}, u32[]{:S(2)}, u32[]{:S(2)}) collective-permute-start(bf16[64,2048]{1,0:T(8,128)(2,1)S(1)} %get-tuple-element.84), channel_id=1, source_target_pairs={{0,8},{4,12},{8,0},{12,4},{1,9},{5,13},{9,1},{13,5},{2,10},{6,14},... | collective-permute-start | bytes 786440 | tf_op jit(solution)/shard_map/ppermute | solution.py:616
  4.7 1.6 collective-permute-start.2
  6.8 2.0 collective-permute-start.1
  8.9 3.0 %collective-permute-done.3 = bf16[64,2048]{1,0:T(8,128)(2,1)S(1)} collective-permute-done((bf16[64,2048]{1,0:T(8,128)(2,1)S(1)}, bf16[64,2048]{1,0:T(8,128)(2,1)S(1)}, u32[]{:S(2)}, u32[]{:S(2)}) %collective-permute-start.3) | collective-permute-done | bytes 262176 | tf_op jit(solution)/shard_map/ppermute | solution.py:616
  12.7 3.1 %collective-permute-done.2.refs_0_ = bf16[64,2048]{1,0:T(8,128)(2,1)S(1)} collective-permute-done((bf16[64,2048]{1,0:T(8,128)(2,1)S(1)}, bf16[64,2048]{1,0:T(8,128)(2,1)S(1)}, u32[]{:S(2)}, u32[]{:S(2)}) %collective-permute-start.2) | collective-permute-done | bytes 262176 | tf_op jit(solution)/shard_map/ppermute | solution.py:629
  15.8 0.8 collective-permute-done.4.refs_2_
  17.9 1.7 collective-permute-start.5
  19.7 3.6 %collective-permute-start = (bf16[64,2048]{1,0:T(8,128)(2,1)S(1)}, bf16[64,2048]{1,0:T(8,128)(2,1)S(1)}, u32[]{:S(2)}, u32[]{:S(2)}) collective-permute-start(bf16[64,2048]{1,0:T(8,128)(2,1)S(1)} %get-tuple-element.83.refs_0_), channel_id=1, source_target_pairs={{0,2},{1,3},{2,0},{3,1},{4,6},{5,7},{6,4},{7,5},{8,10},{9,11},{10,... | collective-permute-start | bytes 786440 | tf_op jit(solution)/shard_map/ppermute | solution.py:629
  23.3 2.4 collective-permute-done.5.refs_2_
  26.9 1.4 collective-permute-start.6
  28.9 4.2 %collective-permute-done.refs_0_ = bf16[64,2048]{1,0:T(8,128)(2,1)S(1)} collective-permute-done((bf16[64,2048]{1,0:T(8,128)(2,1)S(1)}, bf16[64,2048]{1,0:T(8,128)(2,1)S(1)}, u32[]{:S(2)}, u32[]{:S(2)}) %collective-permute-start) | collective-permute-done | bytes 262176 | tf_op jit(solution)/shard_map/ppermute | solution.py:629
  35.1 1.2 collective-permute-start.14
  37.3 4.5 %collective-permute-done.14.refs_10_ = bf16[64,2048]{1,0:T(8,128)(2,1)S(1)} collective-permute-done((bf16[64,2048]{1,0:T(8,128)(2,1)}, bf16[64,2048]{1,0:T(8,128)(2,1)S(1)}, u32[]{:S(2)}, u32[]{:S(2)}) %collective-permute-start.14) | collective-permute-done | bytes 262176 | tf_op jit(solution)/shard_map/ppermute | solution.py:616
  43.3 1.3 collective-permute-start.8
  46.2 15.4 %forward.2 = (bf16[2,128,3584]{2,1,0:T(8,128)(2,1)}, bf16[2,128,3584]{2,1,0:T(8,128)(2,1)}) custom-call(s32[224]{0:T(256)} %reshape.33.gk, s32[224]{0:T(256)} %reshape.34.uk, bf16[64,2048]{1,0:T(8,128)(2,1)} %copy-done.16, bf16[64,2048]{1,0:T(8,128)(2,1)} %copy-done.41, bf16[64,2048]{1,0:T(8,128)(2,1)} %get-tuple-element.90.refs_2_, ...), custom_call_target="tpu_custom_call" | custom-call | flops 7516192768 | bytes 18874368 | tf_op jit(solution)/shard_map/forward/pallas_call | solution.py:103
  62.5 3.2 %collective-permute-start.19 = (bf16[128,2048]{1,0:T(8,128)(2,1)}, bf16[128,2048]{1,0:T(8,128)(2,1)}, u32[]{:S(2)}, u32[]{:S(2)}) collective-permute-start(bf16[128,2048]{1,0:T(8,128)(2,1)} %get-tuple-element.95.refs_2_.refs_5_), channel_id=1, source_target_pairs={{0,1},{1,2},{2,3},{3,0},{4,5},{5,6},{6,7},{7,4},{8,9},{9,10},{10,1... | collective-permute-start | bytes 1572872 | tf_op jit(solution)/shard_map/ppermute | solution.py:629
  65.7 7.2 %turned_weight.2 = (bf16[3584,1024]{1,0:T(8,128)(2,1)}, f32[8,128]{1,0:T(8,128)}) custom-call(bf16[1024,3584]{1,0:T(8,128)(2,1)} %refs_8_.1, bf16[2,128,3584]{2,1,0:T(8,128)(2,1)} %get-tuple-element.96.refs_0_), custom_call_target="tpu_custom_call" | custom-call | bytes 14680064 | tf_op jit(solution)/shard_map/turned_weight/pallas_call | solution.py:181
  73.6 1.0 chip_share.2.refs_0_
  74.6 4.1 %collective-permute-done.19.refs_0_ = bf16[128,2048]{1,0:T(8,128)(2,1)} collective-permute-done((bf16[128,2048]{1,0:T(8,128)(2,1)}, bf16[128,2048]{1,0:T(8,128)(2,1)}, u32[]{:S(2)}, u32[]{:S(2)}) %collective-permute-start.19) | collective-permute-done | bytes 524320 | tf_op jit(solution)/shard_map/ppermute | solution.py:629
  79.3 1.4 collective-permute-start.21
  81.3 7.2 %turned_weight.3 = (bf16[3584,1024]{1,0:T(8,128)(2,1)}, f32[8,128]{1,0:T(8,128)}) custom-call(bf16[1024,3584]{1,0:T(8,128)(2,1)} %refs_9_.1, bf16[2,64,3584]{2,1,0:T(8,128)(2,1)} %chip_share.2.refs_0_), custom_call_target="tpu_custom_call" | custom-call | bytes 14680064 | tf_op jit(solution)/shard_map/turned_weight/pallas_call | solution.py:181
  88.5 6.3 %collective-permute-done.21.refs_0_ = bf16[128,2048]{1,0:T(8,128)(2,1)} collective-permute-done((bf16[128,2048]{1,0:T(8,128)(2,1)}, bf16[128,2048]{1,0:T(8,128)(2,1)}, u32[]{:S(2)}, u32[]{:S(2)}) %collective-permute-start.21) | collective-permute-done | bytes 524320 | tf_op jit(solution)/shard_map/ppermute | solution.py:629
  95.3 6.6 %transposed.2 = (bf16[8192,256]{1,0:T(8,128)(2,1)}, f32[8,128]{1,0:T(8,128)}) custom-call(bf16[64,2048]{1,0:T(8,128)(2,1)} %copy-done.16, bf16[64,2048]{1,0:T(8,128)(2,1)} %copy-done.41, bf16[64,2048]{1,0:T(8,128)(2,1)} %get-tuple-element.90.refs_2_, bf16[64,2048]{1,0:T(8,128)(2,1)} %copy-done.43, bf16[64,2048]{1,0:T(8,128)(2,1)} %get-tuple-element.86.refs_4_.refs_1_, ...), custom_call_target="tpu_custom_call" | custom-call | bytes 8388608 | tf_op jit(solution)/shard_map/transposed/pallas_call | solution.py:208
  102.7 3.8 %cotangents.2 = (bf16[128,3584]{1,0:T(8,128)(2,1)}, bf16[2,64,3584]{2,1,0:T(8,128)(2,1)}, f32[8,128]{1,0:T(8,128)S(1)}) custom-call(bf16[2,128,3584]{2,1,0:T(8,128)(2,1)S(1)} %copy-done.1, bf16[2,128,3584]{2,1,0:T(8,128)(2,1)S(1)} %copy-done.3, bf16[2,64,3584]{2,1,0:T(8,128)(2,1)} %collective-permute-done.24.refs_0_, bf16[128,3584]{1,0:T(8,128)(2,1)S(1)} %copy-done.7, ...), custom_call_target="tpu_custom_call" | custom-call | flops 4587520 | bytes 4587520 | tf_op jit(solution)/shard_map/cotangents/pallas_call | solution.py:273
  107.1 1.3 collective-permute-start.25
  109.2 15.4 %forward.3 = (bf16[2,128,3584]{2,1,0:T(8,128)(2,1)}, bf16[2,128,3584]{2,1,0:T(8,128)(2,1)}) custom-call(s32[224]{0:T(256)} %reshape.33.gk, s32[224]{0:T(256)} %reshape.34.uk, bf16[128,2048]{1,0:T(8,128)(2,1)} %get-tuple-element.89.refs_18_.refs_0_.refs_4_, bf16[128,2048]{1,0:T(8,128)(2,1)} %collective-permute-done.7.refs_1_, ...), custom_call_target="tpu_custom_call" | custom-call | flops 7516192768 | bytes 18874368 | tf_op jit(solution)/shard_map/forward/pallas_call | solution.py:103
  124.6 5.3 %collective-permute-done.25.refs_0_ = bf16[2,64,3584]{2,1,0:T(8,128)(2,1)S(1)} collective-permute-done((bf16[2,64,3584]{2,1,0:T(8,128)(2,1)}, bf16[2,64,3584]{2,1,0:T(8,128)(2,1)S(1)}, u32[]{:S(2)}, u32[]{:S(2)}) %collective-permute-start.25) | collective-permute-done | bytes 917536 | tf_op jit(solution)/shard_map/ppermute | solution.py:616
  129.9 1.0 copy-done.39
  132.0 6.5 %transposed.3 = (bf16[8192,256]{1,0:T(8,128)(2,1)}, f32[8,128]{1,0:T(8,128)}) custom-call(bf16[128,2048]{1,0:T(8,128)(2,1)} %get-tuple-element.89.refs_18_.refs_0_.refs_4_, bf16[128,2048]{1,0:T(8,128)(2,1)} %collective-permute-done.7.refs_1_, bf16[128,2048]{1,0:T(8,128)(2,1)} %get-tuple-element.95.refs_2_.refs_5_, ...), custom_call_target="tpu_custom_call" | custom-call | bytes 8388608 | tf_op jit(solution)/shard_map/transposed/pallas_call | solution.py:208
  139.8 1.3 collective-permute-start.27
  141.2 0.9 copy-done.58
  142.4 17.0 %token_backward.2 = (bf16[128,8192]{1,0:T(8,128)(2,1)}, bf16[128,8192]{1,0:T(8,128)(2,1)}, f32[8,128]{1,0:T(8,128)}) custom-call(s32[224]{0:T(256)} %reshape.33.gk, s32[224]{0:T(256)} %reshape.34.uk, bf16[2,64,3584]{2,1,0:T(8,128)(2,1)} %get-tuple-element.105.refs_0_.refs_2_, bf16[2,64,3584]{2,1,0:T(8,128)(2,1)} %get-tuple-element.109.refs_1_.refs_3_, ...), custom_call_target="tpu_custom_call" | custom-call | flops 7516192768 | bytes 18874368 | tf_op jit(solution)/shard_map/token_backward/pallas_call | solution.py:459
  159.3 3.3 %collective-permute-done.27.refs_0_ = bf16[2,64,3584]{2,1,0:T(8,128)(2,1)} collective-permute-done((bf16[2,64,3584]{2,1,0:T(8,128)(2,1)S(1)}, bf16[2,64,3584]{2,1,0:T(8,128)(2,1)}, u32[]{:S(2)}, u32[]{:S(2)}) %collective-permute-start.27) | collective-permute-done | bytes 917536 | tf_op jit(solution)/shard_map/ppermute | solution.py:616
  163.2 1.5 copy-done.5
  164.7 3.9 %cotangents.3 = (bf16[128,3584]{1,0:T(8,128)(2,1)}, bf16[2,64,3584]{2,1,0:T(8,128)(2,1)}, f32[8,128]{1,0:T(8,128)S(1)}) custom-call(bf16[2,128,3584]{2,1,0:T(8,128)(2,1)S(1)} %copy-done, bf16[2,128,3584]{2,1,0:T(8,128)(2,1)S(1)} %copy-done.5, bf16[2,64,3584]{2,1,0:T(8,128)(2,1)} %get-tuple-element.113.refs_0_, ...), custom_call_target="tpu_custom_call", output_to_operand_aliasing={{0}: (4, {})} | custom-call | flops 4587520 | bytes 4587520 | tf_op jit(solution)/shard_map/cotangents/pallas_call | solution.py:273
  168.6 1.3 collective-permute-start.30
  171.8 2.0 collective-permute-start.33
  175.9 13.3 %reached_pairs.1 = (f32[2,28,128,128]{3,2,1,0:T(8,128)}, f32[8,128]{1,0:T(8,128)}) custom-call(s32[896]{0:T(1024)} %reshape.35.gk, s32[896]{0:T(1024)} %reshape.36.uk, bf16[64,2048]{1,0:T(8,128)(2,1)} %copy-done.16, bf16[64,2048]{1,0:T(8,128)(2,1)} %get-tuple-element.86.refs_4_.refs_1_, bf16[64,2048]{1,0:T(8,128)(2,1)} %get-tuple-element.92.refs_8_.refs_2_, ...), custom_call_target="tpu_custom_call" | custom-call | flops 29360128 | bytes 18350080 | tf_op jit(solution)/shard_map/reached_pairs/pallas_call | solution.py:330
  189.2 2.5 collective-permute-done.30.refs_0_
  191.7 5.4 %collective-permute-done.32.refs_1_ = bf16[128,2048]{1,0:T(8,128)(2,1)S(1)} collective-permute-done((bf16[128,2048]{1,0:T(8,128)(2,1)S(1)}, bf16[128,2048]{1,0:T(8,128)(2,1)S(1)}, u32[]{:S(2)}, u32[]{:S(2)}) %collective-permute-start.32) | collective-permute-done | bytes 524320 | tf_op jit(solution)/shard_map/ppermute | solution.py:629
  198.7 1.1 collective-permute-start.36
  199.7 2.0 copy-done.6
  202.4 4.3 %example_squares.1.refs_6_ = f32[8,128]{1,0:T(8,128)} custom-call(bf16[2,64,3584]{2,1,0:T(8,128)(2,1)} %get-tuple-element.105.refs_0_.refs_2_, bf16[2,64,3584]{2,1,0:T(8,128)(2,1)} %get-tuple-element.119.refs_1_.refs_0_.refs_6_, f32[2,28,128,128]{3,2,1,0:T(8,128)S(1)} %copy-done.6, f32[128,128]{1,0:T(8,128)S(1)} %get-tuple-element.170.refs_3_, ...), custom_call_target="tpu_custom_call" | custom-call | flops 469762048 | bytes 3670016 | tf_op jit(solution)/shard_map/example_squares/pallas_call | solution.py:398
  206.7 2.0 collective-permute-start.38
  208.7 2.8 collective-permute-start.39
  211.5 0.9 copy-done.60
  212.4 16.9 %token_backward.3 = (bf16[128,8192]{1,0:T(8,128)(2,1)}, bf16[128,8192]{1,0:T(8,128)(2,1)}, f32[8,128]{1,0:T(8,128)}) custom-call(s32[224]{0:T(256)} %reshape.33.gk, s32[224]{0:T(256)} %reshape.34.uk, bf16[2,64,3584]{2,1,0:T(8,128)(2,1)} %get-tuple-element.119.refs_1_.refs_0_.refs_6_, bf16[2,64,3584]{2,1,0:T(8,128)(2,1)} %get-tuple-element.127.refs_1_.refs_7_, ...), custom_call_target="tpu_custom_call" | custom-call | flops 7516192768 | bytes 18874368 | tf_op jit(solution)/shard_map/token_backward/pallas_call | solution.py:459
  232.4 0.9 collective-permute-start.42
  233.3 1.3 collective-permute-start.40
  234.7 1.0 copy-done.11
  235.7 1.0 copy-done.15
  236.8 1.0 copy-done.20
  237.8 0.9 added_cuts.7
  239.7 2.8 added_cuts.8
  242.5 1.3 collective-permute-start.49
  243.8 1.1 collective-permute-start.46
  244.9 2.0 collective-permute-start.47
  247.7 23.0 %weight_gradients.1 = (bf16[1024,3584]{1,0:T(8,128)(2,1)}, bf16[1024,3584]{1,0:T(8,128)(2,1)}, f32[8,128]{1,0:T(8,128)}) custom-call(s32[224]{0:T(256)} %reshape.33.gk, s32[224]{0:T(256)} %reshape.34.uk, bf16[8192,256]{1,0:T(8,128)(2,1)} %get-tuple-element.117.refs_0_, bf16[8192,256]{1,0:T(8,128)(2,1)} %get-tuple-element.118.refs_1_, ...), custom_call_target="tpu_custom_call" | custom-call | flops 15032385536 | bytes 23068672 | tf_op jit(solution)/shard_map/weight_gradients/pallas_call | solution.py:562
  274.1 1.8 collective-permute-start.50
  276.0 2.0 collective-permute-start.52
  278.0 1.8 collective-permute-done.50.refs_5_
  279.8 7.5 %collective-permute-done.51.refs_6_ = bf16[32,2048]{1,0:T(8,128)(2,1)S(1)} collective-permute-done((bf16[32,2048]{1,0:T(8,128)(2,1)S(1)}, bf16[32,2048]{1,0:T(8,128)(2,1)S(1)}, u32[]{:S(2)}, u32[]{:S(2)}) %collective-permute-start.51) | collective-permute-done | bytes 131104 | tf_op jit(solution)/shard_map/ppermute | solution.py:629
  287.3 1.0 added_cuts.11
  (213 shorter events, 32.8 us)
Async XLA Ops:
  1.7 33.4 %copy-start.16 = (bf16[64,2048]{1,0:T(8,128)(2,1)}, bf16[64,2048]{1,0:T(8,128)(2,1)S(1)}, u32[]{:S(2)}) copy-start(bf16[64,2048]{1,0:T(8,128)(2,1)S(1)} %get-tuple-element.83.refs_0_) | copy-start | bytes 786436
  1.7 10.1 %collective-permute-start.3 = (bf16[64,2048]{1,0:T(8,128)(2,1)S(1)}, bf16[64,2048]{1,0:T(8,128)(2,1)S(1)}, u32[]{:S(2)}, u32[]{:S(2)}) collective-permute-start(bf16[64,2048]{1,0:T(8,128)(2,1)S(1)} %get-tuple-element.84), channel_id=1, source_target_pairs={{0,8},{4,12},{8,0},{12,4},{1,9},{5,13},{9,1},{13,5},{2,10},{6,14},... | collective-permute-start | bytes 786440 | tf_op jit(solution)/shard_map/ppermute | solution.py:616
  4.7 37.2 %copy-start.52 = (s32[32,28]{1,0:T(8,128)S(1)}, s32[32,28]{1,0:T(8,128)}, u32[]{:S(2)}) copy-start(s32[32,28]{1,0:T(8,128)} %param.12) | copy-start | bytes 10756
  4.7 37.2 %copy-start.53 = (s32[32,28]{1,0:T(8,128)S(1)}, s32[32,28]{1,0:T(8,128)}, u32[]{:S(2)}) copy-start(s32[32,28]{1,0:T(8,128)} %param.13) | copy-start | bytes 10756
  4.7 11.1 %collective-permute-start.2 = (bf16[64,2048]{1,0:T(8,128)(2,1)S(1)}, bf16[64,2048]{1,0:T(8,128)(2,1)S(1)}, u32[]{:S(2)}, u32[]{:S(2)}) collective-permute-start(bf16[64,2048]{1,0:T(8,128)(2,1)S(1)} %get-tuple-element.83.refs_0_), channel_id=1, source_target_pairs={{0,1},{1,2},{2,3},{3,0},{4,5},{5,6},{6,7},{7,4},{8,9},{9,10},{10,1... | collective-permute-start | bytes 786440 | tf_op jit(solution)/shard_map/ppermute | solution.py:629
  6.3 10.3 %collective-permute-start.4 = (bf16[64,2048]{1,0:T(8,128)(2,1)S(1)}, bf16[64,2048]{1,0:T(8,128)(2,1)S(1)}, u32[]{:S(2)}, u32[]{:S(2)}) collective-permute-start(bf16[64,2048]{1,0:T(8,128)(2,1)S(1)} %get-tuple-element.83.refs_0_), channel_id=1, source_target_pairs={{0,8},{4,12},{8,0},{12,4},{1,9},{5,13},{9,1},{13,5},{2,10},{6,14},... | collective-permute-start | bytes 786440 | tf_op jit(solution)/shard_map/ppermute | solution.py:616
  6.8 16.4 %collective-permute-start.1 = (bf16[64,2048]{1,0:T(8,128)(2,1)S(1)}, bf16[64,2048]{1,0:T(8,128)(2,1)S(1)}, u32[]{:S(2)}, u32[]{:S(2)}) collective-permute-start(bf16[64,2048]{1,0:T(8,128)(2,1)S(1)} %get-tuple-element.83.refs_0_), channel_id=1, source_target_pairs={{0,3},{1,0},{2,1},{3,2},{4,7},{5,4},{6,5},{7,6},{8,11},{9,8},{10,9... | collective-permute-start | bytes 786440 | tf_op jit(solution)/shard_map/ppermute | solution.py:629
  17.9 7.7 %collective-permute-start.5 = (bf16[64,2048]{1,0:T(8,128)(2,1)}, bf16[64,2048]{1,0:T(8,128)(2,1)S(1)}, u32[]{:S(2)}, u32[]{:S(2)}) collective-permute-start(bf16[64,2048]{1,0:T(8,128)(2,1)} %get-tuple-element.86.refs_4_.refs_1_), channel_id=1, source_target_pairs={{0,8},{4,12},{8,0},{12,4},{1,9},{5,13},{9,1},{13,5},{2,10},{6,14},... | collective-permute-start | bytes 786440 | tf_op jit(solution)/shard_map/ppermute | solution.py:616
  19.7 13.4 %collective-permute-start = (bf16[64,2048]{1,0:T(8,128)(2,1)S(1)}, bf16[64,2048]{1,0:T(8,128)(2,1)S(1)}, u32[]{:S(2)}, u32[]{:S(2)}) collective-permute-start(bf16[64,2048]{1,0:T(8,128)(2,1)S(1)} %get-tuple-element.83.refs_0_), channel_id=1, source_target_pairs={{0,2},{1,3},{2,0},{3,1},{4,6},{5,7},{6,4},{7,5},{8,10},{9,11},{10,... | collective-permute-start | bytes 786440 | tf_op jit(solution)/shard_map/ppermute | solution.py:629
  26.9 6.8 %collective-permute-start.6 = (bf16[64,2048]{1,0:T(8,128)(2,1)}, bf16[64,2048]{1,0:T(8,128)(2,1)S(1)}, u32[]{:S(2)}, u32[]{:S(2)}) collective-permute-start(bf16[64,2048]{1,0:T(8,128)(2,1)} %get-tuple-element.88.refs_12_.refs_3_), channel_id=1, source_target_pairs={{0,8},{4,12},{8,0},{12,4},{1,9},{5,13},{9,1},{13,5},{2,10},{6,14},... | collective-permute-start | bytes 786440 | tf_op jit(solution)/shard_map/ppermute | solution.py:616
  28.4 7.9 %collective-permute-start.9 = (bf16[64,2048]{1,0:T(8,128)(2,1)S(1)}, bf16[64,2048]{1,0:T(8,128)(2,1)S(1)}, u32[]{:S(2)}, u32[]{:S(2)}) collective-permute-start(bf16[64,2048]{1,0:T(8,128)(2,1)S(1)} %get-tuple-element.83.refs_0_), channel_id=1, source_target_pairs={{0,4},{4,0},{8,12},{12,8},{1,5},{5,1},{9,13},{13,9},{2,6},{6,2},{1... | collective-permute-start | bytes 786440 | tf_op jit(solution)/shard_map/ppermute | solution.py:619
  28.4 8.4 %collective-permute-start.11 = (bf16[64,2048]{1,0:T(8,128)(2,1)}, bf16[64,2048]{1,0:T(8,128)(2,1)S(1)}, u32[]{:S(2)}, u32[]{:S(2)}) collective-permute-start(bf16[64,2048]{1,0:T(8,128)(2,1)} %get-tuple-element.86.refs_4_.refs_1_), channel_id=1, source_target_pairs={{0,4},{4,0},{8,12},{12,8},{1,5},{5,1},{9,13},{13,9},{2,6},{6,2},{1... | collective-permute-start | bytes 786440 | tf_op jit(solution)/shard_map/ppermute | solution.py:619
  28.9 8.0 %collective-permute-start.10 = (bf16[64,2048]{1,0:T(8,128)(2,1)}, bf16[64,2048]{1,0:T(8,128)(2,1)S(1)}, u32[]{:S(2)}, u32[]{:S(2)}) collective-permute-start(bf16[64,2048]{1,0:T(8,128)(2,1)} %get-tuple-element.90.refs_2_), channel_id=1, source_target_pairs={{0,4},{4,0},{8,12},{12,8},{1,5},{5,1},{9,13},{13,9},{2,6},{6,2},{1... | collective-permute-start | bytes 786440 | tf_op jit(solution)/shard_map/ppermute | solution.py:619
  35.1 6.8 %collective-permute-start.14 = (bf16[64,2048]{1,0:T(8,128)(2,1)}, bf16[64,2048]{1,0:T(8,128)(2,1)S(1)}, u32[]{:S(2)}, u32[]{:S(2)}) collective-permute-start(bf16[64,2048]{1,0:T(8,128)(2,1)} %get-tuple-element.92.refs_8_.refs_2_), channel_id=1, source_target_pairs={{0,8},{4,12},{8,0},{12,4},{1,9},{5,13},{9,1},{13,5},{2,10},{6,14},... | collective-permute-start | bytes 786440 | tf_op jit(solution)/shard_map/ppermute | solution.py:616
  36.3 7.0 %collective-permute-start.16 = (bf16[64,2048]{1,0:T(8,128)(2,1)}, bf16[64,2048]{1,0:T(8,128)(2,1)S(1)}, u32[]{:S(2)}, u32[]{:S(2)}) collective-permute-start(bf16[64,2048]{1,0:T(8,128)(2,1)} %get-tuple-element.88.refs_12_.refs_3_), channel_id=1, source_target_pairs={{0,4},{4,0},{8,12},{12,8},{1,5},{5,1},{9,13},{13,9},{2,6},{6,2},{1... | collective-permute-start | bytes 786440 | tf_op jit(solution)/shard_map/ppermute | solution.py:619
  36.3 8.4 %copy-start.41 = (bf16[64,2048]{1,0:T(8,128)(2,1)}, bf16[64,2048]{1,0:T(8,128)(2,1)S(1)}, u32[]{:S(2)}) copy-start(bf16[64,2048]{1,0:T(8,128)(2,1)S(1)} %collective-permute-done.9.refs_1_) | copy-start | bytes 786436
  36.3 8.3 %collective-permute-start.12 = (bf16[64,2048]{1,0:T(8,128)(2,1)}, bf16[64,2048]{1,0:T(8,128)(2,1)S(1)}, u32[]{:S(2)}, u32[]{:S(2)}) collective-permute-start(bf16[64,2048]{1,0:T(8,128)(2,1)} %get-tuple-element.91.refs_6_), channel_id=1, source_target_pairs={{0,4},{4,0},{8,12},{12,8},{1,5},{5,1},{9,13},{13,9},{2,6},{6,2},{1... | collective-permute-start | bytes 786440 | tf_op jit(solution)/shard_map/ppermute | solution.py:619
  36.8 7.9 %copy-start.42 = (bf16[64,2048]{1,0:T(8,128)(2,1)}, bf16[64,2048]{1,0:T(8,128)(2,1)S(1)}, u32[]{:S(2)}) copy-start(bf16[64,2048]{1,0:T(8,128)(2,1)S(1)} %collective-permute-done.11.refs_5_) | copy-start | bytes 786436
  36.8 7.8 %collective-permute-start.13 = (bf16[64,2048]{1,0:T(8,128)(2,1)}, bf16[64,2048]{1,0:T(8,128)(2,1)S(1)}, u32[]{:S(2)}, u32[]{:S(2)}) collective-permute-start(bf16[64,2048]{1,0:T(8,128)(2,1)} %get-tuple-element.92.refs_8_.refs_2_), channel_id=1, source_target_pairs={{0,4},{4,0},{8,12},{12,8},{1,5},{5,1},{9,13},{13,9},{2,6},{6,2},{1... | collective-permute-start | bytes 786440 | tf_op jit(solution)/shard_map/ppermute | solution.py:619
  36.9 7.8 %copy-start.43 = (bf16[64,2048]{1,0:T(8,128)(2,1)}, bf16[64,2048]{1,0:T(8,128)(2,1)S(1)}, u32[]{:S(2)}) copy-start(bf16[64,2048]{1,0:T(8,128)(2,1)S(1)} %collective-permute-done.10.refs_3_) | copy-start | bytes 786436
  36.9 7.7 %collective-permute-start.17 = (bf16[64,2048]{1,0:T(8,128)(2,1)}, bf16[64,2048]{1,0:T(8,128)(2,1)S(1)}, u32[]{:S(2)}, u32[]{:S(2)}) collective-permute-start(bf16[64,2048]{1,0:T(8,128)(2,1)} %get-tuple-element.93.refs_14_), channel_id=1, source_target_pairs={{0,4},{4,0},{8,12},{12,8},{1,5},{5,1},{9,13},{13,9},{2,6},{6,2},{1... | collective-permute-start | bytes 786440 | tf_op jit(solution)/shard_map/ppermute | solution.py:619
  41.9 2.8 collective-permute-start.15
  42.0 19.7 %copy-start.50 = (s32[32,28]{1,0:T(8,128)}, s32[32,28]{1,0:T(8,128)S(1)}, u32[]{:S(2)}) copy-start(s32[32,28]{1,0:T(8,128)S(1)} %get-tuple-element.172) | copy-start | bytes 10756
  43.3 18.4 %collective-permute-start.8 = (bf16[128,2048]{1,0:T(8,128)(2,1)}, bf16[128,2048]{1,0:T(8,128)(2,1)}, u32[]{:S(2)}, u32[]{:S(2)}) collective-permute-start(bf16[128,2048]{1,0:T(8,128)(2,1)} %get-tuple-element.89.refs_18_.refs_0_.refs_4_), channel_id=1, source_target_pairs={{0,1},{1,2},{2,3},{3,0},{4,5},{5,6},{6,7},{7,4},{8,9},{9,10},{10,1... | collective-permute-start | bytes 1572872 | tf_op jit(solution)/shard_map/ppermute | solution.py:629
  62.3 10.6 %collective-permute-start.22 = (bf16[2,128,3584]{2,1,0:T(8,128)(2,1)}, bf16[2,128,3584]{2,1,0:T(8,128)(2,1)S(1)}, u32[]{:S(2)}, u32[]{:S(2)}) collective-permute-start(bf16[2,128,3584]{2,1,0:T(8,128)(2,1)} %get-tuple-element.96.refs_0_), channel_id=1, source_target_pairs={{0,4},{4,0},{8,12},{12,8},{1,5},{5,1},{9,13},{13,9},{2,6},{6,2},{1... | collective-permute-start | bytes 5505032 | tf_op jit(solution)/shard_map/ppermute | solution.py:619
  62.5 10.4 %copy-start.1 = (bf16[2,128,3584]{2,1,0:T(8,128)(2,1)S(1)}, bf16[2,128,3584]{2,1,0:T(8,128)(2,1)}, u32[]{:S(2)}) copy-start(bf16[2,128,3584]{2,1,0:T(8,128)(2,1)} %get-tuple-element.99.a) | copy-start | bytes 5505028
  62.5 16.2 %collective-permute-start.19 = (bf16[128,2048]{1,0:T(8,128)(2,1)}, bf16[128,2048]{1,0:T(8,128)(2,1)}, u32[]{:S(2)}, u32[]{:S(2)}) collective-permute-start(bf16[128,2048]{1,0:T(8,128)(2,1)} %get-tuple-element.95.refs_2_.refs_5_), channel_id=1, source_target_pairs={{0,1},{1,2},{2,3},{3,0},{4,5},{5,6},{6,7},{7,4},{8,9},{9,10},{10,1... | collective-permute-start | bytes 1572872 | tf_op jit(solution)/shard_map/ppermute | solution.py:629
  73.6 7.1 %copy-start.32 = (bf16[128,2048]{1,0:T(8,128)(2,1)S(1)}, bf16[128,2048]{1,0:T(8,128)(2,1)}, u32[]{:S(2)}) copy-start(bf16[128,2048]{1,0:T(8,128)(2,1)} %get-tuple-element.89.refs_18_.refs_0_.refs_4_) | copy-start | bytes 1572868
  74.6 27.4 %collective-permute-start.24 = (bf16[2,64,3584]{2,1,0:T(8,128)(2,1)}, bf16[2,64,3584]{2,1,0:T(8,128)(2,1)}, u32[]{:S(2)}, u32[]{:S(2)}) collective-permute-start(bf16[2,64,3584]{2,1,0:T(8,128)(2,1)} %chip_share.2.refs_0_), channel_id=1, source_target_pairs={{0,8},{4,12},{8,0},{12,4},{1,9},{5,13},{9,1},{13,5},{2,10},{6,14},... | collective-permute-start | bytes 2752520 | tf_op jit(solution)/shard_map/ppermute | solution.py:616
  79.3 15.4 %collective-permute-start.21 = (bf16[128,2048]{1,0:T(8,128)(2,1)}, bf16[128,2048]{1,0:T(8,128)(2,1)}, u32[]{:S(2)}, u32[]{:S(2)}) collective-permute-start(bf16[128,2048]{1,0:T(8,128)(2,1)} %get-tuple-element.98.refs_4_.refs_6_), channel_id=1, source_target_pairs={{0,1},{1,2},{2,3},{3,0},{4,5},{5,6},{6,7},{7,4},{8,9},{9,10},{10,1... | collective-permute-start | bytes 1572872 | tf_op jit(solution)/shard_map/ppermute | solution.py:629
  80.7 27.7 %collective-permute-start.7 = (bf16[128,2048]{1,0:T(8,128)(2,1)S(1)}, bf16[128,2048]{1,0:T(8,128)(2,1)}, u32[]{:S(2)}, u32[]{:S(2)}) collective-permute-start(bf16[128,2048]{1,0:T(8,128)(2,1)S(1)} %copy-done.32), channel_id=1, source_target_pairs={{0,4},{4,0},{8,12},{12,8},{1,5},{5,1},{9,13},{13,9},{2,6},{6,2},{1... | collective-permute-start | bytes 1572872 | tf_op jit(solution)/shard_map/ppermute | solution.py:619
  80.7 27.7 %collective-permute-start.18 = (bf16[128,2048]{1,0:T(8,128)(2,1)}, bf16[128,2048]{1,0:T(8,128)(2,1)}, u32[]{:S(2)}, u32[]{:S(2)}) collective-permute-start(bf16[128,2048]{1,0:T(8,128)(2,1)} %get-tuple-element.95.refs_2_.refs_5_), channel_id=1, source_target_pairs={{0,4},{4,0},{8,12},{12,8},{1,5},{5,1},{9,13},{13,9},{2,6},{6,2},{1... | collective-permute-start | bytes 1572872 | tf_op jit(solution)/shard_map/ppermute | solution.py:619
  81.3 27.2 %collective-permute-start.20 = (bf16[128,2048]{1,0:T(8,128)(2,1)}, bf16[128,2048]{1,0:T(8,128)(2,1)}, u32[]{:S(2)}, u32[]{:S(2)}) collective-permute-start(bf16[128,2048]{1,0:T(8,128)(2,1)} %get-tuple-element.98.refs_4_.refs_6_), channel_id=1, source_target_pairs={{0,4},{4,0},{8,12},{12,8},{1,5},{5,1},{9,13},{13,9},{2,6},{6,2},{1... | collective-permute-start | bytes 1572872 | tf_op jit(solution)/shard_map/ppermute | solution.py:619
  95.3 6.7 %copy-start.7 = (bf16[128,3584]{1,0:T(8,128)(2,1)S(1)}, bf16[128,3584]{1,0:T(8,128)(2,1)}, u32[]{:S(2)}) copy-start(bf16[128,3584]{1,0:T(8,128)(2,1)} %refs_1_.3) | copy-start | bytes 2752516
  95.3 13.1 %collective-permute-start.23 = (bf16[128,2048]{1,0:T(8,128)(2,1)}, bf16[128,2048]{1,0:T(8,128)(2,1)S(1)}, u32[]{:S(2)}, u32[]{:S(2)}) collective-permute-start(bf16[128,2048]{1,0:T(8,128)(2,1)} %get-tuple-element.101.refs_17_.refs_6_.refs_7_), channel_id=1, source_target_pairs={{0,4},{4,0},{8,12},{12,8},{1,5},{5,1},{9,13},{13,9},{2,6},{6,2},{1... | collective-permute-start | bytes 1572872 | tf_op jit(solution)/shard_map/ppermute | solution.py:619
  107.1 22.8 %collective-permute-start.25 = (bf16[2,64,3584]{2,1,0:T(8,128)(2,1)}, bf16[2,64,3584]{2,1,0:T(8,128)(2,1)S(1)}, u32[]{:S(2)}, u32[]{:S(2)}) collective-permute-start(bf16[2,64,3584]{2,1,0:T(8,128)(2,1)} %get-tuple-element.105.refs_0_.refs_2_), channel_id=1, source_target_pairs={{0,8},{4,12},{8,0},{12,4},{1,9},{5,13},{9,1},{13,5},{2,10},{6,14},... | collective-permute-start | bytes 2752520 | tf_op jit(solution)/shard_map/ppermute | solution.py:616
  131.5 7.0 %collective-permute-start.26 = (bf16[2,128,3584]{2,1,0:T(8,128)(2,1)}, bf16[2,128,3584]{2,1,0:T(8,128)(2,1)S(1)}, u32[]{:S(2)}, u32[]{:S(2)}) collective-permute-start(bf16[2,128,3584]{2,1,0:T(8,128)(2,1)} %get-tuple-element.107.refs_8_), channel_id=1, source_target_pairs={{0,4},{4,0},{8,12},{12,8},{1,5},{5,1},{9,13},{13,9},{2,6},{6,2},{1... | collective-permute-start | bytes 5505032 | tf_op jit(solution)/shard_map/ppermute | solution.py:619
  131.5 9.6 %collective-permute-start.28 = (bf16[2,64,3584]{2,1,0:T(8,128)(2,1)}, bf16[2,64,3584]{2,1,0:T(8,128)(2,1)S(1)}, u32[]{:S(2)}, u32[]{:S(2)}) collective-permute-start(bf16[2,64,3584]{2,1,0:T(8,128)(2,1)} %get-tuple-element.105.refs_0_.refs_2_), channel_id=1, source_target_pairs={{0,4},{4,0},{8,12},{12,8},{1,5},{5,1},{9,13},{13,9},{2,6},{6,2},{1... | collective-permute-start | bytes 2752520 | tf_op jit(solution)/shard_map/ppermute | solution.py:619
  132.0 9.1 %collective-permute-start.29 = (bf16[2,64,3584]{2,1,0:T(8,128)(2,1)}, bf16[2,64,3584]{2,1,0:T(8,128)(2,1)S(1)}, u32[]{:S(2)}, u32[]{:S(2)}) collective-permute-start(bf16[2,64,3584]{2,1,0:T(8,128)(2,1)} %get-tuple-element.109.refs_1_.refs_3_), channel_id=1, source_target_pairs={{0,4},{4,0},{8,12},{12,8},{1,5},{5,1},{9,13},{13,9},{2,6},{6,2},{1... | collective-permute-start | bytes 2752520 | tf_op jit(solution)/shard_map/ppermute | solution.py:619
  139.8 22.8 %collective-permute-start.27 = (bf16[2,64,3584]{2,1,0:T(8,128)(2,1)S(1)}, bf16[2,64,3584]{2,1,0:T(8,128)(2,1)}, u32[]{:S(2)}, u32[]{:S(2)}) collective-permute-start(bf16[2,64,3584]{2,1,0:T(8,128)(2,1)S(1)} %chip_share.3.refs_6_), channel_id=1, source_target_pairs={{0,8},{4,12},{8,0},{12,4},{1,9},{5,13},{9,1},{13,5},{2,10},{6,14},... | collective-permute-start | bytes 2752520 | tf_op jit(solution)/shard_map/ppermute | solution.py:616
  163.2 6.7 %collective-permute-start.31 = (bf16[128,8192]{1,0:T(8,128)(2,1)}, bf16[128,8192]{1,0:T(8,128)(2,1)S(1)}, u32[]{:S(2)}, u32[]{:S(2)}) collective-permute-start(bf16[128,8192]{1,0:T(8,128)(2,1)} %get-tuple-element.121), channel_id=1, source_target_pairs={{0,4},{4,0},{8,12},{12,8},{1,5},{5,1},{9,13},{13,9},{2,6},{6,2},{1... | collective-permute-start | bytes 6291464 | tf_op jit(solution)/shard_map/ppermute | solution.py:619
  168.6 23.1 %collective-permute-start.30 = (bf16[2,64,3584]{2,1,0:T(8,128)(2,1)}, bf16[2,64,3584]{2,1,0:T(8,128)(2,1)}, u32[]{:S(2)}, u32[]{:S(2)}) collective-permute-start(bf16[2,64,3584]{2,1,0:T(8,128)(2,1)} %get-tuple-element.119.refs_1_.refs_0_.refs_6_), channel_id=1, source_target_pairs={{0,8},{4,12},{8,0},{12,4},{1,9},{5,13},{9,1},{13,5},{2,10},{6,14},... | collective-permute-start | bytes 2752520 | tf_op jit(solution)/shard_map/ppermute | solution.py:616
  171.8 25.3 %collective-permute-start.32 = (bf16[128,2048]{1,0:T(8,128)(2,1)S(1)}, bf16[128,2048]{1,0:T(8,128)(2,1)S(1)}, u32[]{:S(2)}, u32[]{:S(2)}) collective-permute-start(bf16[128,2048]{1,0:T(8,128)(2,1)S(1)} %get-tuple-element.123), channel_id=1, source_target_pairs={{0,3},{1,0},{2,1},{3,2},{4,7},{5,4},{6,5},{7,6},{8,11},{9,8},{10,9... | collective-permute-start | bytes 1572872 | tf_op jit(solution)/shard_map/ppermute | solution.py:629
  171.8 25.3 %collective-permute-start.33 = (bf16[128,2048]{1,0:T(8,128)(2,1)S(1)}, bf16[128,2048]{1,0:T(8,128)(2,1)S(1)}, u32[]{:S(2)}, u32[]{:S(2)}) collective-permute-start(bf16[128,2048]{1,0:T(8,128)(2,1)S(1)} %get-tuple-element.124), channel_id=1, source_target_pairs={{0,1},{1,2},{2,3},{3,0},{4,5},{5,6},{6,7},{7,4},{8,9},{9,10},{10,1... | collective-permute-start | bytes 1572872 | tf_op jit(solution)/shard_map/ppermute | solution.py:629
  175.9 32.8 %collective-permute-start.34 = (bf16[2,64,3584]{2,1,0:T(8,128)(2,1)}, bf16[2,64,3584]{2,1,0:T(8,128)(2,1)}, u32[]{:S(2)}, u32[]{:S(2)}) collective-permute-start(bf16[2,64,3584]{2,1,0:T(8,128)(2,1)} %get-tuple-element.119.refs_1_.refs_0_.refs_6_), channel_id=1, source_target_pairs={{0,4},{4,0},{8,12},{12,8},{1,5},{5,1},{9,13},{13,9},{2,6},{6,2},{1... | collective-permute-start | bytes 2752520 | tf_op jit(solution)/shard_map/ppermute | solution.py:619
  198.7 12.8 %collective-permute-start.35 = (bf16[2,64,3584]{2,1,0:T(8,128)(2,1)}, bf16[2,64,3584]{2,1,0:T(8,128)(2,1)S(1)}, u32[]{:S(2)}, u32[]{:S(2)}) collective-permute-start(bf16[2,64,3584]{2,1,0:T(8,128)(2,1)} %get-tuple-element.127.refs_1_.refs_7_), channel_id=1, source_target_pairs={{0,4},{4,0},{8,12},{12,8},{1,5},{5,1},{9,13},{13,9},{2,6},{6,2},{1... | collective-permute-start | bytes 2752520 | tf_op jit(solution)/shard_map/ppermute | solution.py:619
  198.7 30.7 %collective-permute-start.36 = (bf16[128,2048]{1,0:T(8,128)(2,1)S(1)}, bf16[128,2048]{1,0:T(8,128)(2,1)S(1)}, u32[]{:S(2)}, u32[]{:S(2)}) collective-permute-start(bf16[128,2048]{1,0:T(8,128)(2,1)S(1)} %get-tuple-element.130), channel_id=1, source_target_pairs={{0,2},{1,3},{2,0},{3,1},{4,6},{5,7},{6,4},{7,5},{8,10},{9,11},{10,... | collective-permute-start | bytes 1572872 | tf_op jit(solution)/shard_map/ppermute | solution.py:629
  206.7 22.7 %collective-permute-start.37 = (f32[8,128]{1,0:T(8,128)}, f32[8,128]{1,0:T(8,128)S(1)}, u32[]{:S(2)}, u32[]{:S(2)}) collective-permute-start(f32[8,128]{1,0:T(8,128)} %example_squares.1.refs_6_), channel_id=1, source_target_pairs={{0,1},{1,2},{2,3},{3,0},{4,5},{5,6},{6,7},{7,4},{8,9},{9,10},{10,1... | collective-permute-start | bytes 12296 | tf_op jit(solution)/shard_map/ppermute | solution.py:629
  206.7 22.7 %collective-permute-start.38 = (f32[8,128]{1,0:T(8,128)}, f32[8,128]{1,0:T(8,128)S(1)}, u32[]{:S(2)}, u32[]{:S(2)}) collective-permute-start(f32[8,128]{1,0:T(8,128)} %example_squares.1.refs_6_), channel_id=1, source_target_pairs={{0,2},{1,3},{2,0},{3,1},{4,6},{5,7},{6,4},{7,5},{8,10},{9,11},{10,... | collective-permute-start | bytes 12296 | tf_op jit(solution)/shard_map/ppermute | solution.py:629
  208.7 20.7 %collective-permute-start.39 = (f32[8,128]{1,0:T(8,128)}, f32[8,128]{1,0:T(8,128)S(1)}, u32[]{:S(2)}, u32[]{:S(2)}) collective-permute-start(f32[8,128]{1,0:T(8,128)} %example_squares.1.refs_6_), channel_id=1, source_target_pairs={{0,3},{1,0},{2,1},{3,2},{4,7},{5,4},{6,5},{7,6},{8,11},{9,8},{10,9... | collective-permute-start | bytes 12296 | tf_op jit(solution)/shard_map/ppermute | solution.py:629
  230.2 9.5 %copy-start.8 = (bf16[128,8192]{1,0:T(8,128)(2,1)S(1)}, bf16[128,8192]{1,0:T(8,128)(2,1)}, u32[]{:S(2)}) copy-start(bf16[128,8192]{1,0:T(8,128)(2,1)} %get-tuple-element.135.refs_0_) | copy-start | bytes 6291460
  230.8 8.9 %collective-permute-start.43 = (bf16[128,8192]{1,0:T(8,128)(2,1)}, bf16[128,8192]{1,0:T(8,128)(2,1)}, u32[]{:S(2)}, u32[]{:S(2)}) collective-permute-start(bf16[128,8192]{1,0:T(8,128)(2,1)} %get-tuple-element.136), channel_id=1, source_target_pairs={{0,4},{4,0},{8,12},{12,8},{1,5},{5,1},{9,13},{13,9},{2,6},{6,2},{1... | collective-permute-start | bytes 6291464 | tf_op jit(solution)/shard_map/ppermute | solution.py:619
  232.4 7.0 %collective-permute-start.42 = (f32[128]{0:T(128)S(1)}, f32[128]{0:T(128)S(1)}, u32[]{:S(2)}, u32[]{:S(2)}) collective-permute-start(f32[128]{0:T(128)S(1)} %select_reduce_fusion), channel_id=1, source_target_pairs={{0,12},{4,8},{8,4},{12,0},{1,13},{5,9},{9,5},{13,1},{2,14},{6,10},... | collective-permute-start | bytes 1544 | tf_op jit(solution)/shard_map/ppermute | solution.py:626
  233.3 6.2 %collective-permute-start.41 = (f32[128]{0:T(128)S(1)}, f32[128]{0:T(128)S(1)}, u32[]{:S(2)}, u32[]{:S(2)}) collective-permute-start(f32[128]{0:T(128)S(1)} %select_reduce_fusion), channel_id=1, source_target_pairs={{0,4},{4,0},{8,12},{12,8},{1,5},{5,1},{9,13},{13,9},{2,6},{6,2},{1... | collective-permute-start | bytes 1544 | tf_op jit(solution)/shard_map/ppermute | solution.py:626
  233.3 6.3 %collective-permute-start.40 = (f32[128]{0:T(128)S(1)}, f32[128]{0:T(128)S(1)}, u32[]{:S(2)}, u32[]{:S(2)}) collective-permute-start(f32[128]{0:T(128)S(1)} %select_reduce_fusion), channel_id=1, source_target_pairs={{0,8},{4,12},{8,0},{12,4},{1,9},{5,13},{9,1},{13,5},{2,10},{6,14},... | collective-permute-start | bytes 1544 | tf_op jit(solution)/shard_map/ppermute | solution.py:626
  238.7 39.3 %collective-permute-start.44 = (bf16[64,2048]{1,0:T(8,128)(2,1)}, bf16[64,2048]{1,0:T(8,128)(2,1)S(1)}, u32[]{:S(2)}, u32[]{:S(2)}) collective-permute-start(bf16[64,2048]{1,0:T(8,128)(2,1)} %get-tuple-element.147), channel_id=1, source_target_pairs={{0,8},{4,12},{8,0},{12,4},{1,9},{5,13},{9,1},{13,5},{2,10},{6,14},... | collective-permute-start | bytes 786440 | tf_op jit(solution)/shard_map/ppermute | solution.py:616
  242.5 30.3 %collective-permute-start.49 = (bf16[32,8192]{1,0:T(8,128)(2,1)}, bf16[32,8192]{1,0:T(8,128)(2,1)S(1)}, u32[]{:S(2)}, u32[]{:S(2)}) collective-permute-start(bf16[32,8192]{1,0:T(8,128)(2,1)} %get-tuple-element.156), channel_id=1, source_target_pairs={{0,8},{4,12},{8,0},{12,4},{1,9},{5,13},{9,1},{13,5},{2,10},{6,14},... | collective-permute-start | bytes 1572872 | tf_op jit(solution)/shard_map/ppermute | solution.py:616
  243.8 26.9 %collective-permute-start.45 = (bf16[64,2048]{1,0:T(8,128)(2,1)}, bf16[64,2048]{1,0:T(8,128)(2,1)S(1)}, u32[]{:S(2)}, u32[]{:S(2)}) collective-permute-start(bf16[64,2048]{1,0:T(8,128)(2,1)} %get-tuple-element.149), channel_id=1, source_target_pairs={{0,3},{1,0},{2,1},{3,2},{4,7},{5,4},{6,5},{7,6},{8,11},{9,8},{10,9... | collective-permute-start | bytes 786440 | tf_op jit(solution)/shard_map/ppermute | solution.py:629
  243.8 26.9 %collective-permute-start.46 = (bf16[64,2048]{1,0:T(8,128)(2,1)}, bf16[64,2048]{1,0:T(8,128)(2,1)S(1)}, u32[]{:S(2)}, u32[]{:S(2)}) collective-permute-start(bf16[64,2048]{1,0:T(8,128)(2,1)} %get-tuple-element.150), channel_id=1, source_target_pairs={{0,2},{1,3},{2,0},{3,1},{4,6},{5,7},{6,4},{7,5},{8,10},{9,11},{10,... | collective-permute-start | bytes 786440 | tf_op jit(solution)/shard_map/ppermute | solution.py:629
  244.9 25.9 %collective-permute-start.47 = (bf16[64,2048]{1,0:T(8,128)(2,1)}, bf16[64,2048]{1,0:T(8,128)(2,1)S(1)}, u32[]{:S(2)}, u32[]{:S(2)}) collective-permute-start(bf16[64,2048]{1,0:T(8,128)(2,1)} %get-tuple-element.151), channel_id=1, source_target_pairs={{0,1},{1,2},{2,3},{3,0},{4,5},{5,6},{6,7},{7,4},{8,9},{9,10},{10,1... | collective-permute-start | bytes 786440 | tf_op jit(solution)/shard_map/ppermute | solution.py:629
  272.0 5.9 %collective-permute-start.48 = (bf16[32,2048]{1,0:T(8,128)(2,1)S(1)}, bf16[32,2048]{1,0:T(8,128)(2,1)S(1)}, u32[]{:S(2)}, u32[]{:S(2)}) collective-permute-start(bf16[32,2048]{1,0:T(8,128)(2,1)S(1)} %get-tuple-element.154), channel_id=1, source_target_pairs={{0,8},{4,12},{8,0},{12,4},{1,9},{5,13},{9,1},{13,5},{2,10},{6,14},... | collective-permute-start | bytes 393224 | tf_op jit(solution)/shard_map/ppermute | solution.py:616
  274.1 5.8 %collective-permute-start.50 = (bf16[32,2048]{1,0:T(8,128)(2,1)S(1)}, bf16[32,2048]{1,0:T(8,128)(2,1)S(1)}, u32[]{:S(2)}, u32[]{:S(2)}) collective-permute-start(bf16[32,2048]{1,0:T(8,128)(2,1)S(1)} %get-tuple-element.158), channel_id=1, source_target_pairs={{0,3},{1,0},{2,1},{3,2},{4,7},{5,4},{6,5},{7,6},{8,11},{9,8},{10,9... | collective-permute-start | bytes 393224 | tf_op jit(solution)/shard_map/ppermute | solution.py:629
  275.9 11.5 %collective-permute-start.51 = (bf16[32,2048]{1,0:T(8,128)(2,1)S(1)}, bf16[32,2048]{1,0:T(8,128)(2,1)S(1)}, u32[]{:S(2)}, u32[]{:S(2)}) collective-permute-start(bf16[32,2048]{1,0:T(8,128)(2,1)S(1)} %get-tuple-element.159), channel_id=1, source_target_pairs={{0,2},{1,3},{2,0},{3,1},{4,6},{5,7},{6,4},{7,5},{8,10},{9,11},{10,... | collective-permute-start | bytes 393224 | tf_op jit(solution)/shard_map/ppermute | solution.py:629
  276.0 11.4 %collective-permute-start.52 = (bf16[32,2048]{1,0:T(8,128)(2,1)S(1)}, bf16[32,2048]{1,0:T(8,128)(2,1)S(1)}, u32[]{:S(2)}, u32[]{:S(2)}) collective-permute-start(bf16[32,2048]{1,0:T(8,128)(2,1)S(1)} %get-tuple-element.160), channel_id=1, source_target_pairs={{0,1},{1,2},{2,3},{3,0},{4,5},{5,6},{6,7},{7,4},{8,9},{9,10},{10,1... | collective-permute-start | bytes 393224 | tf_op jit(solution)/shard_map/ppermute | solution.py:629
  (50 other events, 88.6 us)

commit v4 on v3

--- a/solution.py
+++ b/solution.py
@@ -20,7 +20,7 @@
 
 
 def column_group(blocks):
-    return max(n for n in range(1, 8) if blocks % n == 0)
+    return max(n for n in range(1, 8) if blocks % n == 0 and (n == 1 or n < blocks))
 
 
 def params(held):
@@ -130,7 +130,7 @@
     )
 
 
-def after(arrays, deps, marked=False):
+def after(arrays, deps):
     arrays = list(arrays)
 
     def kernel(*refs):
@@ -144,7 +144,7 @@
         input_output_aliases={n: n for n in range(len(arrays))},
         cost_estimate=pl.CostEstimate(flops=0, bytes_accessed=0, transcendentals=0),
         name="after",
-    )(*arrays, *deps)[: None if marked else len(arrays)]
+    )(*arrays, *deps)[: len(arrays)]
 
 
 def rows_of(array, spans, deps):
@@ -703,10 +703,7 @@
     )
     *far_0, send_1 = after(far_0 + [send_1], [keep_1])
     received_1 = from_core(send_1)
-    tokens_1, tokens_1_done = transposed(pieces_1, rows, width, [send_1])
-    leaving_1 = [
-        chip_share(keep_1, received_1, s, chunk_rows, [tokens_1_done]) for s in range(1, chips)
-    ]
+    leaving_1 = [chip_share(keep_1, received_1, s, chunk_rows, ()) for s in range(1, chips)]
     arrived_1 = [from_chip(part, -s - 1) for s, part in enumerate(leaving_1)]
     every_0 = [cots_0] + far_0 + [from_core(part) for part in [cots_0] + far_0]
     back_0 = token_backward(
@@ -744,21 +741,21 @@
 
     parts_0, _, parts_0_done = leave(back_0[0], received, chunk_rows, [cots_1_done])
     crossing_0 = over_tensor_first(parts_0)
-    reached, reached_done = reached_pairs(
+    reached, _ = reached_pairs(
         mine, own_rows, width, gate_all, up_all, same_example, [parts_0_done]
     )
     early = [p for p in range(1, tensor) if p != middle]
-    *ordered, ordered_done = after(
-        far_1 + [crossing_0[p] for p in early], [reached_done], marked=True
-    )
+    partial = example_squares(reached, [cots_0, cots_1], member, ())
+    apart = [from_tensor(partial, p) for p in range(1, tensor)]
+    ordered = after(far_1 + [crossing_0[p] for p in early] + apart, [partial])
     far_1 = list(ordered[: len(far_1)])
-    for p, array in zip(early, ordered[len(far_1) :], strict=True):
+    apart = list(ordered[len(far_1) + len(early) :])
+    for p, array in zip(early, ordered[len(far_1) : len(far_1) + len(early)], strict=True):
         crossing_0[p] = array
     every_1 = [cots_1] + far_1 + [from_core(part) for part in [cots_1] + far_1]
-    partial = example_squares(reached, [cots_0, cots_1], member, [ordered_done])
-    apart = [from_tensor(partial, p) for p in range(1, tensor)]
+    tokens_1, tokens_1_done = transposed(pieces_1, rows, width, ordered[:1])
     back_1 = token_backward(
-        every_1, width, gate_own, up_own, gate_turned, up_turned, [partial]
+        every_1, width, gate_own, up_own, gate_turned, up_turned, [tokens_1_done]
     )
     crossing_0[middle], sent, *apart = after([crossing_0[middle], back_1[1]] + apart, ())
     squares = partial[0]

time: 289 us -> 288 us (level)
    ppermute x20, waiting for transfers between devices: 0.05 us -> 3.74 us  [from_core(): return lax.ppermute(value, 'fsdp', [(i, i ^ 1) for i in range(fsdp)])]
    unnamed x122 -> x124, local copies, waits for them, and re-layouts: 23.4 us -> 22.8 us
  transfers between devices with their start and end apart: 53 -> 53, of which waited for: 15 -> 18; matrix products, arithmetic and copies ran while one was open for 2% -> 2% of each run, Pallas kernels for 52% -> 52%
where the time goes in v4:
time: 288 us; the launch traced here: 287 us
  Pallas kernels  153 us (53%)
  waiting for transfers between devices  54.8 us (19%)
  starting transfers between devices  47.3 us (16%)
  local copies, waits for them, and re-layouts  26.7 us (9%)
    pallas_call x2, Pallas kernels, token_backward(): pl.pallas_call(kernel, out_shape=(out, out, MARK), grid_spec=pltpu.Prefet...  33.9 us
    pallas_call x2, Pallas kernels, forward(): pl.pallas_call(kernel, out_shape=(out, out), grid_spec=pltpu.PrefetchScal...  30.9 us
    ppermute x18, waiting for transfers between devices, from_tensor(): lax.ppermute(value, 'tensor', [(i, (i + back) % tensor) for i in range(te...  30.5 us
    ppermute x18, starting transfers between devices, from_tensor(): lax.ppermute(value, 'tensor', [(i, (i + back) % tensor) for i in range(te...  28 us
    pallas_call x1, Pallas kernels, weight_gradients(): pl.pallas_call(kernel, out_shape=(out, out, MARK), grid_spec=pltpu.Prefet...  23 us
    unnamed x124, local copies, waits for them, and re-layouts  22.8 us
    ppermute x12, waiting for transfers between devices, from_chip(): return lax.ppermute(value, 'fsdp', pairs)  20.5 us
    pallas_call x2, Pallas kernels, turned_weight(): pl.pallas_call(kernel, out_shape=(jax.ShapeDtypeStruct((width, depth), BF...  14.5 us
  transfers between devices with their start and end apart: 53, of which 18 were waited for; matrix products, arithmetic and copies ran while one was open for 2% of the time, Pallas kernels for 52%

profile of v4, /device:TPU:0, one launch (start us, length us, event | category | flops | bytes accessed | tf_op | source)
XLA Modules:
  0.0 286.6 jit_solution(11024681219148868271)
XLA Ops:
  0.6 1.0 copy-done.20
  1.7 3.0 %collective-permute-start.3 = (bf16[64,2048]{1,0:T(8,128)(2,1)S(1)}, bf16[64,2048]{1,0:T(8,128)(2,1)S(1)}, u32[]{:S(2)}, u32[]{:S(2)}) collective-permute-start(bf16[64,2048]{1,0:T(8,128)(2,1)S(1)} %get-tuple-element.85), channel_id=1, source_target_pairs={{0,8},{4,12},{8,0},{12,4},{1,9},{5,13},{9,1},{13,5},{2,10},{6,14},... | collective-permute-start | bytes 786440 | tf_op jit(solution)/shard_map/ppermute | solution.py:616
  4.7 1.6 collective-permute-start.2
  6.8 2.0 collective-permute-start.1
  8.9 3.0 %collective-permute-done.3 = bf16[64,2048]{1,0:T(8,128)(2,1)S(1)} collective-permute-done((bf16[64,2048]{1,0:T(8,128)(2,1)S(1)}, bf16[64,2048]{1,0:T(8,128)(2,1)S(1)}, u32[]{:S(2)}, u32[]{:S(2)}) %collective-permute-start.3) | collective-permute-done | bytes 262176 | tf_op jit(solution)/shard_map/ppermute | solution.py:616
  12.7 3.1 %collective-permute-done.2.refs_0_ = bf16[64,2048]{1,0:T(8,128)(2,1)S(1)} collective-permute-done((bf16[64,2048]{1,0:T(8,128)(2,1)S(1)}, bf16[64,2048]{1,0:T(8,128)(2,1)S(1)}, u32[]{:S(2)}, u32[]{:S(2)}) %collective-permute-start.2) | collective-permute-done | bytes 262176 | tf_op jit(solution)/shard_map/ppermute | solution.py:629
  18.0 1.7 collective-permute-start.5
  19.7 3.5 %collective-permute-start = (bf16[64,2048]{1,0:T(8,128)(2,1)S(1)}, bf16[64,2048]{1,0:T(8,128)(2,1)S(1)}, u32[]{:S(2)}, u32[]{:S(2)}) collective-permute-start(bf16[64,2048]{1,0:T(8,128)(2,1)S(1)} %get-tuple-element.84.refs_0_), channel_id=1, source_target_pairs={{0,2},{1,3},{2,0},{3,1},{4,6},{5,7},{6,4},{7,5},{8,10},{9,11},{10,... | collective-permute-start | bytes 786440 | tf_op jit(solution)/shard_map/ppermute | solution.py:629
  23.3 2.4 collective-permute-done.5.refs_2_
  27.0 1.4 collective-permute-start.6
  28.9 4.2 %collective-permute-done.refs_0_ = bf16[64,2048]{1,0:T(8,128)(2,1)S(1)} collective-permute-done((bf16[64,2048]{1,0:T(8,128)(2,1)S(1)}, bf16[64,2048]{1,0:T(8,128)(2,1)S(1)}, u32[]{:S(2)}, u32[]{:S(2)}) %collective-permute-start) | collective-permute-done | bytes 262176 | tf_op jit(solution)/shard_map/ppermute | solution.py:629
  35.1 1.2 collective-permute-start.14
  37.3 4.6 %collective-permute-done.14.refs_10_ = bf16[64,2048]{1,0:T(8,128)(2,1)S(1)} collective-permute-done((bf16[64,2048]{1,0:T(8,128)(2,1)}, bf16[64,2048]{1,0:T(8,128)(2,1)S(1)}, u32[]{:S(2)}, u32[]{:S(2)}) %collective-permute-start.14) | collective-permute-done | bytes 262176 | tf_op jit(solution)/shard_map/ppermute | solution.py:616
  43.3 1.3 collective-permute-start.8
  46.3 15.4 %forward.2 = (bf16[2,128,3584]{2,1,0:T(8,128)(2,1)}, bf16[2,128,3584]{2,1,0:T(8,128)(2,1)}) custom-call(s32[224]{0:T(256)} %reshape.33.gk, s32[224]{0:T(256)} %reshape.34.uk, bf16[64,2048]{1,0:T(8,128)(2,1)} %copy-done.16, bf16[64,2048]{1,0:T(8,128)(2,1)} %copy-done.41, bf16[64,2048]{1,0:T(8,128)(2,1)} %get-tuple-element.91.refs_2_, ...), custom_call_target="tpu_custom_call" | custom-call | flops 7516192768 | bytes 18874368 | tf_op jit(solution)/shard_map/forward/pallas_call | solution.py:103
  62.6 3.1 %collective-permute-start.19 = (bf16[128,2048]{1,0:T(8,128)(2,1)}, bf16[128,2048]{1,0:T(8,128)(2,1)}, u32[]{:S(2)}, u32[]{:S(2)}) collective-permute-start(bf16[128,2048]{1,0:T(8,128)(2,1)} %get-tuple-element.96.refs_2_.refs_5_), channel_id=1, source_target_pairs={{0,1},{1,2},{2,3},{3,0},{4,5},{5,6},{6,7},{7,4},{8,9},{9,10},{10,1... | collective-permute-start | bytes 1572872 | tf_op jit(solution)/shard_map/ppermute | solution.py:629
  65.7 7.2 %turned_weight.2 = (bf16[3584,1024]{1,0:T(8,128)(2,1)}, f32[8,128]{1,0:T(8,128)}) custom-call(bf16[1024,3584]{1,0:T(8,128)(2,1)} %refs_8_.1, bf16[2,128,3584]{2,1,0:T(8,128)(2,1)} %get-tuple-element.97.refs_0_), custom_call_target="tpu_custom_call" | custom-call | bytes 14680064 | tf_op jit(solution)/shard_map/turned_weight/pallas_call | solution.py:181
  73.6 1.0 chip_share.2.refs_0_
  74.7 4.1 %collective-permute-done.19.refs_0_ = bf16[128,2048]{1,0:T(8,128)(2,1)} collective-permute-done((bf16[128,2048]{1,0:T(8,128)(2,1)}, bf16[128,2048]{1,0:T(8,128)(2,1)}, u32[]{:S(2)}, u32[]{:S(2)}) %collective-permute-start.19) | collective-permute-done | bytes 524320 | tf_op jit(solution)/shard_map/ppermute | solution.py:629
  79.4 1.3 collective-permute-start.21
  81.3 7.2 %turned_weight.3 = (bf16[3584,1024]{1,0:T(8,128)(2,1)}, f32[8,128]{1,0:T(8,128)}) custom-call(bf16[1024,3584]{1,0:T(8,128)(2,1)} %refs_9_.1, bf16[2,64,3584]{2,1,0:T(8,128)(2,1)} %chip_share.2.refs_0_), custom_call_target="tpu_custom_call" | custom-call | bytes 14680064 | tf_op jit(solution)/shard_map/turned_weight/pallas_call | solution.py:181
  88.5 6.3 %collective-permute-done.21.refs_0_ = bf16[128,2048]{1,0:T(8,128)(2,1)} collective-permute-done((bf16[128,2048]{1,0:T(8,128)(2,1)}, bf16[128,2048]{1,0:T(8,128)(2,1)}, u32[]{:S(2)}, u32[]{:S(2)}) %collective-permute-start.21) | collective-permute-done | bytes 524320 | tf_op jit(solution)/shard_map/ppermute | solution.py:629
  95.4 6.6 %transposed.2 = (bf16[8192,256]{1,0:T(8,128)(2,1)}, f32[8,128]{1,0:T(8,128)}) custom-call(bf16[64,2048]{1,0:T(8,128)(2,1)} %copy-done.16, bf16[64,2048]{1,0:T(8,128)(2,1)} %copy-done.41, bf16[64,2048]{1,0:T(8,128)(2,1)} %get-tuple-element.91.refs_2_, bf16[64,2048]{1,0:T(8,128)(2,1)} %copy-done.43, bf16[64,2048]{1,0:T(8,128)(2,1)} %get-tuple-element.87.refs_4_.refs_1_, ...), custom_call_target="tpu_custom_call" | custom-call | bytes 8388608 | tf_op jit(solution)/shard_map/transposed/pallas_call | solution.py:208
  102.7 3.5 %cotangents.2 = (bf16[128,3584]{1,0:T(8,128)(2,1)}, bf16[2,64,3584]{2,1,0:T(8,128)(2,1)S(1)}, f32[8,128]{1,0:T(8,128)S(1)}) custom-call(bf16[2,128,3584]{2,1,0:T(8,128)(2,1)S(1)} %copy-done.3, bf16[2,128,3584]{2,1,0:T(8,128)(2,1)S(1)} %copy-done.5, bf16[2,64,3584]{2,1,0:T(8,128)(2,1)} %collective-permute-done.24.refs_0_, bf16[128,3584]{1,0:T(8,128)(2,1)S(1)} %copy-done.7, ...), custom_call_target="tpu_custom_call" | custom-call | flops 4587520 | bytes 4587520 | tf_op jit(solution)/shard_map/cotangents/pallas_call | solution.py:273
  106.9 1.2 collective-permute-start.25
  108.0 15.4 %forward.3 = (bf16[2,128,3584]{2,1,0:T(8,128)(2,1)}, bf16[2,128,3584]{2,1,0:T(8,128)(2,1)}) custom-call(s32[224]{0:T(256)} %reshape.33.gk, s32[224]{0:T(256)} %reshape.34.uk, bf16[128,2048]{1,0:T(8,128)(2,1)} %get-tuple-element.90.refs_18_.refs_0_.refs_4_, bf16[128,2048]{1,0:T(8,128)(2,1)} %collective-permute-done.7.refs_1_, ...), custom_call_target="tpu_custom_call" | custom-call | flops 7516192768 | bytes 18874368 | tf_op jit(solution)/shard_map/forward/pallas_call | solution.py:103
  123.5 6.0 %collective-permute-done.25.refs_0_ = bf16[2,64,3584]{2,1,0:T(8,128)(2,1)S(1)} collective-permute-done((bf16[2,64,3584]{2,1,0:T(8,128)(2,1)S(1)}, bf16[2,64,3584]{2,1,0:T(8,128)(2,1)S(1)}, u32[]{:S(2)}, u32[]{:S(2)}) %collective-permute-start.25) | collective-permute-done | bytes 917536 | tf_op jit(solution)/shard_map/ppermute | solution.py:616
  129.5 0.9 copy-done.40
  131.5 3.5 %collective-permute-done.26.b = bf16[2,128,3584]{2,1,0:T(8,128)(2,1)S(1)} collective-permute-done((bf16[2,128,3584]{2,1,0:T(8,128)(2,1)}, bf16[2,128,3584]{2,1,0:T(8,128)(2,1)S(1)}, u32[]{:S(2)}, u32[]{:S(2)}) %collective-permute-start.26) | collective-permute-done | bytes 1835040 | tf_op jit(solution)/shard_map/ppermute | solution.py:619
  135.2 1.0 copy-done.1
  136.2 1.2 collective-permute-start.27
  138.7 17.0 %token_backward.2 = (bf16[128,8192]{1,0:T(8,128)(2,1)}, bf16[128,8192]{1,0:T(8,128)(2,1)}, f32[8,128]{1,0:T(8,128)}) custom-call(s32[224]{0:T(256)} %reshape.33.gk, s32[224]{0:T(256)} %reshape.34.uk, bf16[2,64,3584]{2,1,0:T(8,128)(2,1)} %copy-done.17, bf16[2,64,3584]{2,1,0:T(8,128)(2,1)} %get-tuple-element.109.refs_1_.refs_3_, ...), custom_call_target="tpu_custom_call" | custom-call | flops 7516192768 | bytes 18874368 | tf_op jit(solution)/shard_map/token_backward/pallas_call | solution.py:459
  155.6 3.1 %collective-permute-done.27.refs_0_ = bf16[2,64,3584]{2,1,0:T(8,128)(2,1)} collective-permute-done((bf16[2,64,3584]{2,1,0:T(8,128)(2,1)S(1)}, bf16[2,64,3584]{2,1,0:T(8,128)(2,1)}, u32[]{:S(2)}, u32[]{:S(2)}) %collective-permute-start.27) | collective-permute-done | bytes 917536 | tf_op jit(solution)/shard_map/ppermute | solution.py:616
  159.3 1.5 copy-done.2
  160.8 3.9 %cotangents.3 = (bf16[128,3584]{1,0:T(8,128)(2,1)}, bf16[2,64,3584]{2,1,0:T(8,128)(2,1)}, f32[8,128]{1,0:T(8,128)S(1)}) custom-call(bf16[2,128,3584]{2,1,0:T(8,128)(2,1)S(1)} %copy-done, bf16[2,128,3584]{2,1,0:T(8,128)(2,1)S(1)} %copy-done.2, bf16[2,64,3584]{2,1,0:T(8,128)(2,1)} %get-tuple-element.113.refs_0_, ...), custom_call_target="tpu_custom_call", output_to_operand_aliasing={{0}: (4, {})} | custom-call | flops 4587520 | bytes 4587520 | tf_op jit(solution)/shard_map/cotangents/pallas_call | solution.py:273
  164.7 1.2 collective-permute-start.30
  165.9 1.0 added_cuts.6
  168.3 2.0 collective-permute-start.33
  172.4 13.3 %reached_pairs.1 = (f32[2,28,128,128]{3,2,1,0:T(8,128)}, f32[8,128]{1,0:T(8,128)}) custom-call(s32[896]{0:T(1024)} %reshape.35.gk, s32[896]{0:T(1024)} %reshape.36.uk, bf16[64,2048]{1,0:T(8,128)(2,1)} %copy-done.16, bf16[64,2048]{1,0:T(8,128)(2,1)} %get-tuple-element.87.refs_4_.refs_1_, bf16[64,2048]{1,0:T(8,128)(2,1)} %get-tuple-element.93.refs_8_.refs_2_, ...), custom_call_target="tpu_custom_call" | custom-call | flops 29360128 | bytes 18350080 | tf_op jit(solution)/shard_map/reached_pairs/pallas_call | solution.py:330
  185.7 2.0 copy-done.6
  187.7 3.5 %example_squares.1.refs_6_ = f32[8,128]{1,0:T(8,128)S(1)} custom-call(bf16[2,64,3584]{2,1,0:T(8,128)(2,1)S(1)} %copy-done.18, bf16[2,64,3584]{2,1,0:T(8,128)(2,1)} %get-tuple-element.118.refs_1_.refs_0_.refs_6_, f32[2,28,128,128]{3,2,1,0:T(8,128)S(1)} %copy-done.6, f32[128,128]{1,0:T(8,128)S(1)} %get-tuple-element.172.refs_3_), custom_call_target="tpu_custom_call" | custom-call | flops 469762048 | bytes 3670016 | tf_op jit(solution)/shard_map/example_squares/pallas_call | solution.py:398
  191.3 2.3 collective-permute-start.35
  193.6 1.5 collective-permute-start.36
  195.1 1.6 collective-permute-done.34.refs_3_
  199.5 1.2 collective-permute-start.39
  200.8 6.5 %transposed.3 = (bf16[8192,256]{1,0:T(8,128)(2,1)}, f32[8,128]{1,0:T(8,128)}) custom-call(bf16[128,2048]{1,0:T(8,128)(2,1)} %get-tuple-element.90.refs_18_.refs_0_.refs_4_, bf16[128,2048]{1,0:T(8,128)(2,1)} %collective-permute-done.7.refs_1_, bf16[128,2048]{1,0:T(8,128)(2,1)} %get-tuple-element.96.refs_2_.refs_5_, ...), custom_call_target="tpu_custom_call" | custom-call | bytes 8388608 | tf_op jit(solution)/shard_map/transposed/pallas_call | solution.py:208
  207.3 0.9 copy-done.60
  208.5 16.9 %token_backward.3 = (bf16[128,8192]{1,0:T(8,128)(2,1)}, bf16[128,8192]{1,0:T(8,128)(2,1)}, f32[8,128]{1,0:T(8,128)}) custom-call(s32[224]{0:T(256)} %reshape.33.gk, s32[224]{0:T(256)} %reshape.34.uk, bf16[2,64,3584]{2,1,0:T(8,128)(2,1)} %get-tuple-element.118.refs_1_.refs_0_.refs_6_, bf16[2,64,3584]{2,1,0:T(8,128)(2,1)} %get-tuple-element.126.refs_8_.refs_1_.refs_7_, ...), custom_call_target="tpu_custom_call" | custom-call | flops 7516192768 | bytes 18874368 | tf_op jit(solution)/shard_map/token_backward/pallas_call | solution.py:459
  229.2 1.0 collective-permute-start.42
  230.2 1.2 collective-permute-start.40
  231.5 1.0 copy-done.11
  232.5 1.0 copy-done.15
  233.6 1.0 copy-done.22
  234.6 0.9 added_cuts.7
  235.5 0.9 collective-permute-start.44
  236.7 2.8 added_cuts.8
  239.4 1.2 collective-permute-start.49
  240.6 2.6 collective-permute-start.45
  243.2 0.9 collective-permute-start.46
  244.9 23.0 %weight_gradients.1 = (bf16[1024,3584]{1,0:T(8,128)(2,1)}, bf16[1024,3584]{1,0:T(8,128)(2,1)}, f32[8,128]{1,0:T(8,128)}) custom-call(s32[224]{0:T(256)} %reshape.33.gk, s32[224]{0:T(256)} %reshape.34.uk, bf16[8192,256]{1,0:T(8,128)(2,1)} %get-tuple-element.117.refs_0_, bf16[8192,256]{1,0:T(8,128)(2,1)} %get-tuple-element.127.refs_1_, ...), custom_call_target="tpu_custom_call" | custom-call | flops 15032385536 | bytes 23068672 | tf_op jit(solution)/shard_map/weight_gradients/pallas_call | solution.py:562
  271.4 3.8 %collective-permute-start.50 = (bf16[32,2048]{1,0:T(8,128)(2,1)S(1)}, bf16[32,2048]{1,0:T(8,128)(2,1)S(1)}, u32[]{:S(2)}, u32[]{:S(2)}) collective-permute-start(bf16[32,2048]{1,0:T(8,128)(2,1)S(1)} %get-tuple-element.160), channel_id=1, source_target_pairs={{0,3},{1,0},{2,1},{3,2},{4,7},{5,4},{6,5},{7,6},{8,11},{9,8},{10,9... | collective-permute-start | bytes 393224 | tf_op jit(solution)/shard_map/ppermute | solution.py:629
  275.8 3.4 %collective-permute-done.50.refs_5_ = bf16[32,2048]{1,0:T(8,128)(2,1)S(1)} collective-permute-done((bf16[32,2048]{1,0:T(8,128)(2,1)S(1)}, bf16[32,2048]{1,0:T(8,128)(2,1)S(1)}, u32[]{:S(2)}, u32[]{:S(2)}) %collective-permute-start.50) | collective-permute-done | bytes 131104 | tf_op jit(solution)/shard_map/ppermute | solution.py:629
  279.2 6.5 %collective-permute-done.51.refs_6_ = bf16[32,2048]{1,0:T(8,128)(2,1)S(1)} collective-permute-done((bf16[32,2048]{1,0:T(8,128)(2,1)S(1)}, bf16[32,2048]{1,0:T(8,128)(2,1)S(1)}, u32[]{:S(2)}, u32[]{:S(2)}) %collective-permute-start.51) | collective-permute-done | bytes 131104 | tf_op jit(solution)/shard_map/ppermute | solution.py:629
  285.7 1.0 added_cuts.11
  (215 shorter events, 34.1 us)
Async XLA Ops:
  1.7 33.3 %copy-start.16 = (bf16[64,2048]{1,0:T(8,128)(2,1)}, bf16[64,2048]{1,0:T(8,128)(2,1)S(1)}, u32[]{:S(2)}) copy-start(bf16[64,2048]{1,0:T(8,128)(2,1)S(1)} %get-tuple-element.84.refs_0_) | copy-start | bytes 786436
  1.7 10.1 %collective-permute-start.3 = (bf16[64,2048]{1,0:T(8,128)(2,1)S(1)}, bf16[64,2048]{1,0:T(8,128)(2,1)S(1)}, u32[]{:S(2)}, u32[]{:S(2)}) collective-permute-start(bf16[64,2048]{1,0:T(8,128)(2,1)S(1)} %get-tuple-element.85), channel_id=1, source_target_pairs={{0,8},{4,12},{8,0},{12,4},{1,9},{5,13},{9,1},{13,5},{2,10},{6,14},... | collective-permute-start | bytes 786440 | tf_op jit(solution)/shard_map/ppermute | solution.py:616
  4.7 37.2 %copy-start.55 = (s32[32,28]{1,0:T(8,128)S(1)}, s32[32,28]{1,0:T(8,128)}, u32[]{:S(2)}) copy-start(s32[32,28]{1,0:T(8,128)} %param.12) | copy-start | bytes 10756
  4.7 37.2 %copy-start.56 = (s32[32,28]{1,0:T(8,128)S(1)}, s32[32,28]{1,0:T(8,128)}, u32[]{:S(2)}) copy-start(s32[32,28]{1,0:T(8,128)} %param.13) | copy-start | bytes 10756
  4.7 11.1 %collective-permute-start.2 = (bf16[64,2048]{1,0:T(8,128)(2,1)S(1)}, bf16[64,2048]{1,0:T(8,128)(2,1)S(1)}, u32[]{:S(2)}, u32[]{:S(2)}) collective-permute-start(bf16[64,2048]{1,0:T(8,128)(2,1)S(1)} %get-tuple-element.84.refs_0_), channel_id=1, source_target_pairs={{0,1},{1,2},{2,3},{3,0},{4,5},{5,6},{6,7},{7,4},{8,9},{9,10},{10,1... | collective-permute-start | bytes 786440 | tf_op jit(solution)/shard_map/ppermute | solution.py:629
  6.3 10.3 %collective-permute-start.4 = (bf16[64,2048]{1,0:T(8,128)(2,1)S(1)}, bf16[64,2048]{1,0:T(8,128)(2,1)S(1)}, u32[]{:S(2)}, u32[]{:S(2)}) collective-permute-start(bf16[64,2048]{1,0:T(8,128)(2,1)S(1)} %get-tuple-element.84.refs_0_), channel_id=1, source_target_pairs={{0,8},{4,12},{8,0},{12,4},{1,9},{5,13},{9,1},{13,5},{2,10},{6,14},... | collective-permute-start | bytes 786440 | tf_op jit(solution)/shard_map/ppermute | solution.py:616
  6.8 16.4 %collective-permute-start.1 = (bf16[64,2048]{1,0:T(8,128)(2,1)S(1)}, bf16[64,2048]{1,0:T(8,128)(2,1)S(1)}, u32[]{:S(2)}, u32[]{:S(2)}) collective-permute-start(bf16[64,2048]{1,0:T(8,128)(2,1)S(1)} %get-tuple-element.84.refs_0_), channel_id=1, source_target_pairs={{0,3},{1,0},{2,1},{3,2},{4,7},{5,4},{6,5},{7,6},{8,11},{9,8},{10,9... | collective-permute-start | bytes 786440 | tf_op jit(solution)/shard_map/ppermute | solution.py:629
  18.0 7.7 %collective-permute-start.5 = (bf16[64,2048]{1,0:T(8,128)(2,1)}, bf16[64,2048]{1,0:T(8,128)(2,1)S(1)}, u32[]{:S(2)}, u32[]{:S(2)}) collective-permute-start(bf16[64,2048]{1,0:T(8,128)(2,1)} %get-tuple-element.87.refs_4_.refs_1_), channel_id=1, source_target_pairs={{0,8},{4,12},{8,0},{12,4},{1,9},{5,13},{9,1},{13,5},{2,10},{6,14},... | collective-permute-start | bytes 786440 | tf_op jit(solution)/shard_map/ppermute | solution.py:616
  19.7 13.4 %collective-permute-start = (bf16[64,2048]{1,0:T(8,128)(2,1)S(1)}, bf16[64,2048]{1,0:T(8,128)(2,1)S(1)}, u32[]{:S(2)}, u32[]{:S(2)}) collective-permute-start(bf16[64,2048]{1,0:T(8,128)(2,1)S(1)} %get-tuple-element.84.refs_0_), channel_id=1, source_target_pairs={{0,2},{1,3},{2,0},{3,1},{4,6},{5,7},{6,4},{7,5},{8,10},{9,11},{10,... | collective-permute-start | bytes 786440 | tf_op jit(solution)/shard_map/ppermute | solution.py:629
  27.0 6.8 %collective-permute-start.6 = (bf16[64,2048]{1,0:T(8,128)(2,1)}, bf16[64,2048]{1,0:T(8,128)(2,1)S(1)}, u32[]{:S(2)}, u32[]{:S(2)}) collective-permute-start(bf16[64,2048]{1,0:T(8,128)(2,1)} %get-tuple-element.89.refs_12_.refs_3_), channel_id=1, source_target_pairs={{0,8},{4,12},{8,0},{12,4},{1,9},{5,13},{9,1},{13,5},{2,10},{6,14},... | collective-permute-start | bytes 786440 | tf_op jit(solution)/shard_map/ppermute | solution.py:616
  28.4 7.9 %collective-permute-start.9 = (bf16[64,2048]{1,0:T(8,128)(2,1)S(1)}, bf16[64,2048]{1,0:T(8,128)(2,1)S(1)}, u32[]{:S(2)}, u32[]{:S(2)}) collective-permute-start(bf16[64,2048]{1,0:T(8,128)(2,1)S(1)} %get-tuple-element.84.refs_0_), channel_id=1, source_target_pairs={{0,4},{4,0},{8,12},{12,8},{1,5},{5,1},{9,13},{13,9},{2,6},{6,2},{1... | collective-permute-start | bytes 786440 | tf_op jit(solution)/shard_map/ppermute | solution.py:619
  28.4 8.4 %collective-permute-start.11 = (bf16[64,2048]{1,0:T(8,128)(2,1)}, bf16[64,2048]{1,0:T(8,128)(2,1)S(1)}, u32[]{:S(2)}, u32[]{:S(2)}) collective-permute-start(bf16[64,2048]{1,0:T(8,128)(2,1)} %get-tuple-element.87.refs_4_.refs_1_), channel_id=1, source_target_pairs={{0,4},{4,0},{8,12},{12,8},{1,5},{5,1},{9,13},{13,9},{2,6},{6,2},{1... | collective-permute-start | bytes 786440 | tf_op jit(solution)/shard_map/ppermute | solution.py:619
  28.9 8.0 %collective-permute-start.10 = (bf16[64,2048]{1,0:T(8,128)(2,1)}, bf16[64,2048]{1,0:T(8,128)(2,1)S(1)}, u32[]{:S(2)}, u32[]{:S(2)}) collective-permute-start(bf16[64,2048]{1,0:T(8,128)(2,1)} %get-tuple-element.91.refs_2_), channel_id=1, source_target_pairs={{0,4},{4,0},{8,12},{12,8},{1,5},{5,1},{9,13},{13,9},{2,6},{6,2},{1... | collective-permute-start | bytes 786440 | tf_op jit(solution)/shard_map/ppermute | solution.py:619
  35.1 6.8 %collective-permute-start.14 = (bf16[64,2048]{1,0:T(8,128)(2,1)}, bf16[64,2048]{1,0:T(8,128)(2,1)S(1)}, u32[]{:S(2)}, u32[]{:S(2)}) collective-permute-start(bf16[64,2048]{1,0:T(8,128)(2,1)} %get-tuple-element.93.refs_8_.refs_2_), channel_id=1, source_target_pairs={{0,8},{4,12},{8,0},{12,4},{1,9},{5,13},{9,1},{13,5},{2,10},{6,14},... | collective-permute-start | bytes 786440 | tf_op jit(solution)/shard_map/ppermute | solution.py:616
  36.3 7.1 %collective-permute-start.16 = (bf16[64,2048]{1,0:T(8,128)(2,1)}, bf16[64,2048]{1,0:T(8,128)(2,1)S(1)}, u32[]{:S(2)}, u32[]{:S(2)}) collective-permute-start(bf16[64,2048]{1,0:T(8,128)(2,1)} %get-tuple-element.89.refs_12_.refs_3_), channel_id=1, source_target_pairs={{0,4},{4,0},{8,12},{12,8},{1,5},{5,1},{9,13},{13,9},{2,6},{6,2},{1... | collective-permute-start | bytes 786440 | tf_op jit(solution)/shard_map/ppermute | solution.py:619
  36.3 8.5 %copy-start.41 = (bf16[64,2048]{1,0:T(8,128)(2,1)}, bf16[64,2048]{1,0:T(8,128)(2,1)S(1)}, u32[]{:S(2)}) copy-start(bf16[64,2048]{1,0:T(8,128)(2,1)S(1)} %collective-permute-done.9.refs_1_) | copy-start | bytes 786436
  36.3 8.4 %collective-permute-start.12 = (bf16[64,2048]{1,0:T(8,128)(2,1)}, bf16[64,2048]{1,0:T(8,128)(2,1)S(1)}, u32[]{:S(2)}, u32[]{:S(2)}) collective-permute-start(bf16[64,2048]{1,0:T(8,128)(2,1)} %get-tuple-element.92.refs_6_), channel_id=1, source_target_pairs={{0,4},{4,0},{8,12},{12,8},{1,5},{5,1},{9,13},{13,9},{2,6},{6,2},{1... | collective-permute-start | bytes 786440 | tf_op jit(solution)/shard_map/ppermute | solution.py:619
  36.8 8.0 %copy-start.42 = (bf16[64,2048]{1,0:T(8,128)(2,1)}, bf16[64,2048]{1,0:T(8,128)(2,1)S(1)}, u32[]{:S(2)}) copy-start(bf16[64,2048]{1,0:T(8,128)(2,1)S(1)} %collective-permute-done.11.refs_5_) | copy-start | bytes 786436
  36.8 7.9 %collective-permute-start.13 = (bf16[64,2048]{1,0:T(8,128)(2,1)}, bf16[64,2048]{1,0:T(8,128)(2,1)S(1)}, u32[]{:S(2)}, u32[]{:S(2)}) collective-permute-start(bf16[64,2048]{1,0:T(8,128)(2,1)} %get-tuple-element.93.refs_8_.refs_2_), channel_id=1, source_target_pairs={{0,4},{4,0},{8,12},{12,8},{1,5},{5,1},{9,13},{13,9},{2,6},{6,2},{1... | collective-permute-start | bytes 786440 | tf_op jit(solution)/shard_map/ppermute | solution.py:619
  36.9 7.9 %copy-start.43 = (bf16[64,2048]{1,0:T(8,128)(2,1)}, bf16[64,2048]{1,0:T(8,128)(2,1)S(1)}, u32[]{:S(2)}) copy-start(bf16[64,2048]{1,0:T(8,128)(2,1)S(1)} %collective-permute-done.10.refs_3_) | copy-start | bytes 786436
  36.9 7.8 %collective-permute-start.17 = (bf16[64,2048]{1,0:T(8,128)(2,1)}, bf16[64,2048]{1,0:T(8,128)(2,1)S(1)}, u32[]{:S(2)}, u32[]{:S(2)}) collective-permute-start(bf16[64,2048]{1,0:T(8,128)(2,1)} %get-tuple-element.94.refs_14_), channel_id=1, source_target_pairs={{0,4},{4,0},{8,12},{12,8},{1,5},{5,1},{9,13},{13,9},{2,6},{6,2},{1... | collective-permute-start | bytes 786440 | tf_op jit(solution)/shard_map/ppermute | solution.py:619
  41.9 2.8 collective-permute-start.15
  42.0 19.8 %copy-start.50 = (s32[32,28]{1,0:T(8,128)}, s32[32,28]{1,0:T(8,128)S(1)}, u32[]{:S(2)}) copy-start(s32[32,28]{1,0:T(8,128)S(1)} %get-tuple-element.174) | copy-start | bytes 10756
  43.3 18.4 %collective-permute-start.8 = (bf16[128,2048]{1,0:T(8,128)(2,1)}, bf16[128,2048]{1,0:T(8,128)(2,1)}, u32[]{:S(2)}, u32[]{:S(2)}) collective-permute-start(bf16[128,2048]{1,0:T(8,128)(2,1)} %get-tuple-element.90.refs_18_.refs_0_.refs_4_), channel_id=1, source_target_pairs={{0,1},{1,2},{2,3},{3,0},{4,5},{5,6},{6,7},{7,4},{8,9},{9,10},{10,1... | collective-permute-start | bytes 1572872 | tf_op jit(solution)/shard_map/ppermute | solution.py:629
  62.3 10.6 %collective-permute-start.22 = (bf16[2,128,3584]{2,1,0:T(8,128)(2,1)}, bf16[2,128,3584]{2,1,0:T(8,128)(2,1)S(1)}, u32[]{:S(2)}, u32[]{:S(2)}) collective-permute-start(bf16[2,128,3584]{2,1,0:T(8,128)(2,1)} %get-tuple-element.97.refs_0_), channel_id=1, source_target_pairs={{0,4},{4,0},{8,12},{12,8},{1,5},{5,1},{9,13},{13,9},{2,6},{6,2},{1... | collective-permute-start | bytes 5505032 | tf_op jit(solution)/shard_map/ppermute | solution.py:619
  62.6 10.4 %copy-start.3 = (bf16[2,128,3584]{2,1,0:T(8,128)(2,1)S(1)}, bf16[2,128,3584]{2,1,0:T(8,128)(2,1)}, u32[]{:S(2)}) copy-start(bf16[2,128,3584]{2,1,0:T(8,128)(2,1)} %get-tuple-element.100.a) | copy-start | bytes 5505028
  62.6 16.2 %collective-permute-start.19 = (bf16[128,2048]{1,0:T(8,128)(2,1)}, bf16[128,2048]{1,0:T(8,128)(2,1)}, u32[]{:S(2)}, u32[]{:S(2)}) collective-permute-start(bf16[128,2048]{1,0:T(8,128)(2,1)} %get-tuple-element.96.refs_2_.refs_5_), channel_id=1, source_target_pairs={{0,1},{1,2},{2,3},{3,0},{4,5},{5,6},{6,7},{7,4},{8,9},{9,10},{10,1... | collective-permute-start | bytes 1572872 | tf_op jit(solution)/shard_map/ppermute | solution.py:629
  74.7 27.4 %collective-permute-start.24 = (bf16[2,64,3584]{2,1,0:T(8,128)(2,1)}, bf16[2,64,3584]{2,1,0:T(8,128)(2,1)}, u32[]{:S(2)}, u32[]{:S(2)}) collective-permute-start(bf16[2,64,3584]{2,1,0:T(8,128)(2,1)} %chip_share.2.refs_0_), channel_id=1, source_target_pairs={{0,8},{4,12},{8,0},{12,4},{1,9},{5,13},{9,1},{13,5},{2,10},{6,14},... | collective-permute-start | bytes 2752520 | tf_op jit(solution)/shard_map/ppermute | solution.py:616
  79.4 15.4 %collective-permute-start.21 = (bf16[128,2048]{1,0:T(8,128)(2,1)}, bf16[128,2048]{1,0:T(8,128)(2,1)}, u32[]{:S(2)}, u32[]{:S(2)}) collective-permute-start(bf16[128,2048]{1,0:T(8,128)(2,1)} %get-tuple-element.99.refs_4_.refs_6_), channel_id=1, source_target_pairs={{0,1},{1,2},{2,3},{3,0},{4,5},{5,6},{6,7},{7,4},{8,9},{9,10},{10,1... | collective-permute-start | bytes 1572872 | tf_op jit(solution)/shard_map/ppermute | solution.py:629
  80.7 27.3 %collective-permute-start.7 = (bf16[128,2048]{1,0:T(8,128)(2,1)S(1)}, bf16[128,2048]{1,0:T(8,128)(2,1)}, u32[]{:S(2)}, u32[]{:S(2)}) collective-permute-start(bf16[128,2048]{1,0:T(8,128)(2,1)S(1)} %copy-done.33), channel_id=1, source_target_pairs={{0,4},{4,0},{8,12},{12,8},{1,5},{5,1},{9,13},{13,9},{2,6},{6,2},{1... | collective-permute-start | bytes 1572872 | tf_op jit(solution)/shard_map/ppermute | solution.py:619
  80.7 27.3 %collective-permute-start.18 = (bf16[128,2048]{1,0:T(8,128)(2,1)}, bf16[128,2048]{1,0:T(8,128)(2,1)}, u32[]{:S(2)}, u32[]{:S(2)}) collective-permute-start(bf16[128,2048]{1,0:T(8,128)(2,1)} %get-tuple-element.96.refs_2_.refs_5_), channel_id=1, source_target_pairs={{0,4},{4,0},{8,12},{12,8},{1,5},{5,1},{9,13},{13,9},{2,6},{6,2},{1... | collective-permute-start | bytes 1572872 | tf_op jit(solution)/shard_map/ppermute | solution.py:619
  81.3 26.8 %collective-permute-start.20 = (bf16[128,2048]{1,0:T(8,128)(2,1)}, bf16[128,2048]{1,0:T(8,128)(2,1)}, u32[]{:S(2)}, u32[]{:S(2)}) collective-permute-start(bf16[128,2048]{1,0:T(8,128)(2,1)} %get-tuple-element.99.refs_4_.refs_6_), channel_id=1, source_target_pairs={{0,4},{4,0},{8,12},{12,8},{1,5},{5,1},{9,13},{13,9},{2,6},{6,2},{1... | collective-permute-start | bytes 1572872 | tf_op jit(solution)/shard_map/ppermute | solution.py:619
  95.4 12.6 %collective-permute-start.23 = (bf16[128,2048]{1,0:T(8,128)(2,1)}, bf16[128,2048]{1,0:T(8,128)(2,1)}, u32[]{:S(2)}, u32[]{:S(2)}) collective-permute-start(bf16[128,2048]{1,0:T(8,128)(2,1)} %get-tuple-element.102.refs_17_.refs_6_.refs_7_), channel_id=1, source_target_pairs={{0,4},{4,0},{8,12},{12,8},{1,5},{5,1},{9,13},{13,9},{2,6},{6,2},{1... | collective-permute-start | bytes 1572872 | tf_op jit(solution)/shard_map/ppermute | solution.py:619
  106.9 16.6 %copy-start.17 = (bf16[2,64,3584]{2,1,0:T(8,128)(2,1)}, bf16[2,64,3584]{2,1,0:T(8,128)(2,1)S(1)}, u32[]{:S(2)}) copy-start(bf16[2,64,3584]{2,1,0:T(8,128)(2,1)S(1)} %get-tuple-element.106.refs_0_.refs_2_) | copy-start | bytes 2752516
  106.9 22.6 %collective-permute-start.25 = (bf16[2,64,3584]{2,1,0:T(8,128)(2,1)S(1)}, bf16[2,64,3584]{2,1,0:T(8,128)(2,1)S(1)}, u32[]{:S(2)}, u32[]{:S(2)}) collective-permute-start(bf16[2,64,3584]{2,1,0:T(8,128)(2,1)S(1)} %get-tuple-element.106.refs_0_.refs_2_), channel_id=1, source_target_pairs={{0,8},{4,12},{8,0},{12,4},{1,9},{5,13},{9,1},{13,5},{2,10},{6,14},... | collective-permute-start | bytes 2752520 | tf_op jit(solution)/shard_map/ppermute | solution.py:616
  131.0 4.0 %collective-permute-start.26 = (bf16[2,128,3584]{2,1,0:T(8,128)(2,1)}, bf16[2,128,3584]{2,1,0:T(8,128)(2,1)S(1)}, u32[]{:S(2)}, u32[]{:S(2)}) collective-permute-start(bf16[2,128,3584]{2,1,0:T(8,128)(2,1)} %get-tuple-element.108), channel_id=1, source_target_pairs={{0,4},{4,0},{8,12},{12,8},{1,5},{5,1},{9,13},{13,9},{2,6},{6,2},{1... | collective-permute-start | bytes 5505032 | tf_op jit(solution)/shard_map/ppermute | solution.py:619
  131.0 6.4 %collective-permute-start.28 = (bf16[2,64,3584]{2,1,0:T(8,128)(2,1)}, bf16[2,64,3584]{2,1,0:T(8,128)(2,1)S(1)}, u32[]{:S(2)}, u32[]{:S(2)}) collective-permute-start(bf16[2,64,3584]{2,1,0:T(8,128)(2,1)} %copy-done.17), channel_id=1, source_target_pairs={{0,4},{4,0},{8,12},{12,8},{1,5},{5,1},{9,13},{13,9},{2,6},{6,2},{1... | collective-permute-start | bytes 2752520 | tf_op jit(solution)/shard_map/ppermute | solution.py:619
  131.5 6.1 %collective-permute-start.29 = (bf16[2,64,3584]{2,1,0:T(8,128)(2,1)}, bf16[2,64,3584]{2,1,0:T(8,128)(2,1)S(1)}, u32[]{:S(2)}, u32[]{:S(2)}) collective-permute-start(bf16[2,64,3584]{2,1,0:T(8,128)(2,1)} %get-tuple-element.109.refs_1_.refs_3_), channel_id=1, source_target_pairs={{0,4},{4,0},{8,12},{12,8},{1,5},{5,1},{9,13},{13,9},{2,6},{6,2},{1... | collective-permute-start | bytes 2752520 | tf_op jit(solution)/shard_map/ppermute | solution.py:619
  136.2 22.5 %collective-permute-start.27 = (bf16[2,64,3584]{2,1,0:T(8,128)(2,1)S(1)}, bf16[2,64,3584]{2,1,0:T(8,128)(2,1)}, u32[]{:S(2)}, u32[]{:S(2)}) collective-permute-start(bf16[2,64,3584]{2,1,0:T(8,128)(2,1)S(1)} %chip_share.3.refs_6_), channel_id=1, source_target_pairs={{0,8},{4,12},{8,0},{12,4},{1,9},{5,13},{9,1},{13,5},{2,10},{6,14},... | collective-permute-start | bytes 2752520 | tf_op jit(solution)/shard_map/ppermute | solution.py:616
  159.3 6.6 %collective-permute-start.31 = (bf16[128,8192]{1,0:T(8,128)(2,1)}, bf16[128,8192]{1,0:T(8,128)(2,1)S(1)}, u32[]{:S(2)}, u32[]{:S(2)}) collective-permute-start(bf16[128,8192]{1,0:T(8,128)(2,1)} %get-tuple-element.120), channel_id=1, source_target_pairs={{0,4},{4,0},{8,12},{12,8},{1,5},{5,1},{9,13},{13,9},{2,6},{6,2},{1... | collective-permute-start | bytes 6291464 | tf_op jit(solution)/shard_map/ppermute | solution.py:619
  164.7 28.9 %collective-permute-start.30 = (bf16[2,64,3584]{2,1,0:T(8,128)(2,1)}, bf16[2,64,3584]{2,1,0:T(8,128)(2,1)}, u32[]{:S(2)}, u32[]{:S(2)}) collective-permute-start(bf16[2,64,3584]{2,1,0:T(8,128)(2,1)} %get-tuple-element.118.refs_1_.refs_0_.refs_6_), channel_id=1, source_target_pairs={{0,8},{4,12},{8,0},{12,4},{1,9},{5,13},{9,1},{13,5},{2,10},{6,14},... | collective-permute-start | bytes 2752520 | tf_op jit(solution)/shard_map/ppermute | solution.py:616
  168.3 17.4 %copy-start.18 = (bf16[2,64,3584]{2,1,0:T(8,128)(2,1)S(1)}, bf16[2,64,3584]{2,1,0:T(8,128)(2,1)}, u32[]{:S(2)}) copy-start(bf16[2,64,3584]{2,1,0:T(8,128)(2,1)} %copy-done.17) | copy-start | bytes 2752516
  168.3 29.0 %collective-permute-start.32 = (bf16[128,2048]{1,0:T(8,128)(2,1)S(1)}, bf16[128,2048]{1,0:T(8,128)(2,1)S(1)}, u32[]{:S(2)}, u32[]{:S(2)}) collective-permute-start(bf16[128,2048]{1,0:T(8,128)(2,1)S(1)} %get-tuple-element.122), channel_id=1, source_target_pairs={{0,3},{1,0},{2,1},{3,2},{4,7},{5,4},{6,5},{7,6},{8,11},{9,8},{10,9... | collective-permute-start | bytes 1572872 | tf_op jit(solution)/shard_map/ppermute | solution.py:629
  168.3 29.0 %collective-permute-start.33 = (bf16[128,2048]{1,0:T(8,128)(2,1)S(1)}, bf16[128,2048]{1,0:T(8,128)(2,1)S(1)}, u32[]{:S(2)}, u32[]{:S(2)}) collective-permute-start(bf16[128,2048]{1,0:T(8,128)(2,1)S(1)} %get-tuple-element.123), channel_id=1, source_target_pairs={{0,1},{1,2},{2,3},{3,0},{4,5},{5,6},{6,7},{7,4},{8,9},{9,10},{10,1... | collective-permute-start | bytes 1572872 | tf_op jit(solution)/shard_map/ppermute | solution.py:629
  191.2 5.5 %collective-permute-start.34 = (f32[8,128]{1,0:T(8,128)S(1)}, f32[8,128]{1,0:T(8,128)S(1)}, u32[]{:S(2)}, u32[]{:S(2)}) collective-permute-start(f32[8,128]{1,0:T(8,128)S(1)} %example_squares.1.refs_6_), channel_id=1, source_target_pairs={{0,1},{1,2},{2,3},{3,0},{4,5},{5,6},{6,7},{7,4},{8,9},{9,10},{10,1... | collective-permute-start | bytes 12296 | tf_op jit(solution)/shard_map/ppermute | solution.py:629
  191.3 5.4 %collective-permute-start.35 = (f32[8,128]{1,0:T(8,128)S(1)}, f32[8,128]{1,0:T(8,128)S(1)}, u32[]{:S(2)}, u32[]{:S(2)}) collective-permute-start(f32[8,128]{1,0:T(8,128)S(1)} %example_squares.1.refs_6_), channel_id=1, source_target_pairs={{0,2},{1,3},{2,0},{3,1},{4,6},{5,7},{6,4},{7,5},{8,10},{9,11},{10,... | collective-permute-start | bytes 12296 | tf_op jit(solution)/shard_map/ppermute | solution.py:629
  193.6 3.7 %collective-permute-start.36 = (f32[8,128]{1,0:T(8,128)S(1)}, f32[8,128]{1,0:T(8,128)S(1)}, u32[]{:S(2)}, u32[]{:S(2)}) collective-permute-start(f32[8,128]{1,0:T(8,128)S(1)} %example_squares.1.refs_6_), channel_id=1, source_target_pairs={{0,3},{1,0},{2,1},{3,2},{4,7},{5,4},{6,5},{7,6},{8,11},{9,8},{10,9... | collective-permute-start | bytes 12296 | tf_op jit(solution)/shard_map/ppermute | solution.py:629
  196.7 10.5 %collective-permute-start.37 = (bf16[2,64,3584]{2,1,0:T(8,128)(2,1)}, bf16[2,64,3584]{2,1,0:T(8,128)(2,1)S(1)}, u32[]{:S(2)}, u32[]{:S(2)}) collective-permute-start(bf16[2,64,3584]{2,1,0:T(8,128)(2,1)} %get-tuple-element.118.refs_1_.refs_0_.refs_6_), channel_id=1, source_target_pairs={{0,4},{4,0},{8,12},{12,8},{1,5},{5,1},{9,13},{13,9},{2,6},{6,2},{1... | collective-permute-start | bytes 2752520 | tf_op jit(solution)/shard_map/ppermute | solution.py:619
  199.5 7.7 %collective-permute-start.38 = (bf16[2,64,3584]{2,1,0:T(8,128)(2,1)}, bf16[2,64,3584]{2,1,0:T(8,128)(2,1)S(1)}, u32[]{:S(2)}, u32[]{:S(2)}) collective-permute-start(bf16[2,64,3584]{2,1,0:T(8,128)(2,1)} %get-tuple-element.126.refs_8_.refs_1_.refs_7_), channel_id=1, source_target_pairs={{0,4},{4,0},{8,12},{12,8},{1,5},{5,1},{9,13},{13,9},{2,6},{6,2},{1... | collective-permute-start | bytes 2752520 | tf_op jit(solution)/shard_map/ppermute | solution.py:619
  199.5 26.7 %collective-permute-start.39 = (bf16[128,2048]{1,0:T(8,128)(2,1)}, bf16[128,2048]{1,0:T(8,128)(2,1)S(1)}, u32[]{:S(2)}, u32[]{:S(2)}) collective-permute-start(bf16[128,2048]{1,0:T(8,128)(2,1)} %get-tuple-element.128), channel_id=1, source_target_pairs={{0,2},{1,3},{2,0},{3,1},{4,6},{5,7},{6,4},{7,5},{8,10},{9,11},{10,... | collective-permute-start | bytes 1572872 | tf_op jit(solution)/shard_map/ppermute | solution.py:629
  227.0 9.6 %copy-start.8 = (bf16[128,8192]{1,0:T(8,128)(2,1)S(1)}, bf16[128,8192]{1,0:T(8,128)(2,1)}, u32[]{:S(2)}) copy-start(bf16[128,8192]{1,0:T(8,128)(2,1)} %get-tuple-element.137.refs_0_) | copy-start | bytes 6291460
  227.6 9.0 %collective-permute-start.43 = (bf16[128,8192]{1,0:T(8,128)(2,1)}, bf16[128,8192]{1,0:T(8,128)(2,1)}, u32[]{:S(2)}, u32[]{:S(2)}) collective-permute-start(bf16[128,8192]{1,0:T(8,128)(2,1)} %get-tuple-element.138), channel_id=1, source_target_pairs={{0,4},{4,0},{8,12},{12,8},{1,5},{5,1},{9,13},{13,9},{2,6},{6,2},{1... | collective-permute-start | bytes 6291464 | tf_op jit(solution)/shard_map/ppermute | solution.py:619
  229.2 7.1 %collective-permute-start.42 = (f32[128]{0:T(128)S(1)}, f32[128]{0:T(128)S(1)}, u32[]{:S(2)}, u32[]{:S(2)}) collective-permute-start(f32[128]{0:T(128)S(1)} %select_reduce_fusion), channel_id=1, source_target_pairs={{0,12},{4,8},{8,4},{12,0},{1,13},{5,9},{9,5},{13,1},{2,14},{6,10},... | collective-permute-start | bytes 1544 | tf_op jit(solution)/shard_map/ppermute | solution.py:626
  230.2 6.2 %collective-permute-start.41 = (f32[128]{0:T(128)S(1)}, f32[128]{0:T(128)S(1)}, u32[]{:S(2)}, u32[]{:S(2)}) collective-permute-start(f32[128]{0:T(128)S(1)} %select_reduce_fusion), channel_id=1, source_target_pairs={{0,4},{4,0},{8,12},{12,8},{1,5},{5,1},{9,13},{13,9},{2,6},{6,2},{1... | collective-permute-start | bytes 1544 | tf_op jit(solution)/shard_map/ppermute | solution.py:626
  230.2 6.3 %collective-permute-start.40 = (f32[128]{0:T(128)S(1)}, f32[128]{0:T(128)S(1)}, u32[]{:S(2)}, u32[]{:S(2)}) collective-permute-start(f32[128]{0:T(128)S(1)} %select_reduce_fusion), channel_id=1, source_target_pairs={{0,8},{4,12},{8,0},{12,4},{1,9},{5,13},{9,1},{13,5},{2,10},{6,14},... | collective-permute-start | bytes 1544 | tf_op jit(solution)/shard_map/ppermute | solution.py:626
  235.5 40.3 %collective-permute-start.44 = (bf16[64,2048]{1,0:T(8,128)(2,1)}, bf16[64,2048]{1,0:T(8,128)(2,1)S(1)}, u32[]{:S(2)}, u32[]{:S(2)}) collective-permute-start(bf16[64,2048]{1,0:T(8,128)(2,1)} %get-tuple-element.149), channel_id=1, source_target_pairs={{0,8},{4,12},{8,0},{12,4},{1,9},{5,13},{9,1},{13,5},{2,10},{6,14},... | collective-permute-start | bytes 786440 | tf_op jit(solution)/shard_map/ppermute | solution.py:616
  239.4 30.7 %collective-permute-start.49 = (bf16[32,8192]{1,0:T(8,128)(2,1)}, bf16[32,8192]{1,0:T(8,128)(2,1)S(1)}, u32[]{:S(2)}, u32[]{:S(2)}) collective-permute-start(bf16[32,8192]{1,0:T(8,128)(2,1)} %get-tuple-element.158), channel_id=1, source_target_pairs={{0,8},{4,12},{8,0},{12,4},{1,9},{5,13},{9,1},{13,5},{2,10},{6,14},... | collective-permute-start | bytes 1572872 | tf_op jit(solution)/shard_map/ppermute | solution.py:616
  240.6 27.3 %collective-permute-start.45 = (bf16[64,2048]{1,0:T(8,128)(2,1)}, bf16[64,2048]{1,0:T(8,128)(2,1)S(1)}, u32[]{:S(2)}, u32[]{:S(2)}) collective-permute-start(bf16[64,2048]{1,0:T(8,128)(2,1)} %get-tuple-element.151), channel_id=1, source_target_pairs={{0,3},{1,0},{2,1},{3,2},{4,7},{5,4},{6,5},{7,6},{8,11},{9,8},{10,9... | collective-permute-start | bytes 786440 | tf_op jit(solution)/shard_map/ppermute | solution.py:629
  243.2 24.7 %collective-permute-start.46 = (bf16[64,2048]{1,0:T(8,128)(2,1)}, bf16[64,2048]{1,0:T(8,128)(2,1)S(1)}, u32[]{:S(2)}, u32[]{:S(2)}) collective-permute-start(bf16[64,2048]{1,0:T(8,128)(2,1)} %get-tuple-element.152), channel_id=1, source_target_pairs={{0,2},{1,3},{2,0},{3,1},{4,6},{5,7},{6,4},{7,5},{8,10},{9,11},{10,... | collective-permute-start | bytes 786440 | tf_op jit(solution)/shard_map/ppermute | solution.py:629
  244.1 23.8 %collective-permute-start.47 = (bf16[64,2048]{1,0:T(8,128)(2,1)}, bf16[64,2048]{1,0:T(8,128)(2,1)S(1)}, u32[]{:S(2)}, u32[]{:S(2)}) collective-permute-start(bf16[64,2048]{1,0:T(8,128)(2,1)} %get-tuple-element.153), channel_id=1, source_target_pairs={{0,1},{1,2},{2,3},{3,0},{4,5},{5,6},{6,7},{7,4},{8,9},{9,10},{10,1... | collective-permute-start | bytes 786440 | tf_op jit(solution)/shard_map/ppermute | solution.py:629
  269.2 6.6 %collective-permute-start.48 = (bf16[32,2048]{1,0:T(8,128)(2,1)S(1)}, bf16[32,2048]{1,0:T(8,128)(2,1)S(1)}, u32[]{:S(2)}, u32[]{:S(2)}) collective-permute-start(bf16[32,2048]{1,0:T(8,128)(2,1)S(1)} %get-tuple-element.156), channel_id=1, source_target_pairs={{0,8},{4,12},{8,0},{12,4},{1,9},{5,13},{9,1},{13,5},{2,10},{6,14},... | collective-permute-start | bytes 393224 | tf_op jit(solution)/shard_map/ppermute | solution.py:616
  271.4 7.8 %collective-permute-start.50 = (bf16[32,2048]{1,0:T(8,128)(2,1)S(1)}, bf16[32,2048]{1,0:T(8,128)(2,1)S(1)}, u32[]{:S(2)}, u32[]{:S(2)}) collective-permute-start(bf16[32,2048]{1,0:T(8,128)(2,1)S(1)} %get-tuple-element.160), channel_id=1, source_target_pairs={{0,3},{1,0},{2,1},{3,2},{4,7},{5,4},{6,5},{7,6},{8,11},{9,8},{10,9... | collective-permute-start | bytes 393224 | tf_op jit(solution)/shard_map/ppermute | solution.py:629
  275.2 10.4 %collective-permute-start.51 = (bf16[32,2048]{1,0:T(8,128)(2,1)S(1)}, bf16[32,2048]{1,0:T(8,128)(2,1)S(1)}, u32[]{:S(2)}, u32[]{:S(2)}) collective-permute-start(bf16[32,2048]{1,0:T(8,128)(2,1)S(1)} %get-tuple-element.161), channel_id=1, source_target_pairs={{0,2},{1,3},{2,0},{3,1},{4,6},{5,7},{6,4},{7,5},{8,10},{9,11},{10,... | collective-permute-start | bytes 393224 | tf_op jit(solution)/shard_map/ppermute | solution.py:629
  275.5 10.2 %collective-permute-start.52 = (bf16[32,2048]{1,0:T(8,128)(2,1)S(1)}, bf16[32,2048]{1,0:T(8,128)(2,1)S(1)}, u32[]{:S(2)}, u32[]{:S(2)}) collective-permute-start(bf16[32,2048]{1,0:T(8,128)(2,1)S(1)} %get-tuple-element.162), channel_id=1, source_target_pairs={{0,1},{1,2},{2,3},{3,0},{4,5},{5,6},{6,7},{7,4},{8,9},{9,10},{10,1... | collective-permute-start | bytes 393224 | tf_op jit(solution)/shard_map/ppermute | solution.py:629
  (51 other events, 106.5 us)
